TPU v7x, 32 devices: a whole 2x2x4 slice. The times are simulated.
32 devices in a mesh: seq: 8 (over y, x, core), head: 4 (over z).
Axes of the slice: x: 2, y: 2, z: 4, core: 2. Of those that a mesh axis runs over, the one named last changes fastest.
Arguments:
- queries: bfloat16 [2048, 8192], P(('seq', 'head')), may hold values from -0.125 to 0.125
- key_rows: bfloat16 [2048, 8192], P(('seq', 'head')), may hold values from -0.125 to 0.125
- value_rows: bfloat16 [2048, 8192], P(('seq', 'head')), may hold values from -0.125 to 0.125
- out_grad: bfloat16 [2048, 8192], P(('seq', 'head')), may hold values from -6 to 6
- log_decay: float32 [64, 2048], P('head', 'seq'), may hold values from -0.9 to 0, as said below
Outputs:
- query_grad: bfloat16 [2048, 8192], P(('seq', 'head'))
- key_grad: bfloat16 [2048, 8192], P(('seq', 'head'))
- value_grad: bfloat16 [2048, 8192], P(('seq', 'head'))
Inputs may be any that keep to these rules, and one draw needn't show every extreme that they name: `log_decay`: never positive.
All inputs are finite; a program needn't handle non-finite values.
Results may differ from a plain program's by a relative error of at most 0.0057.
Values may be sent and summed in bfloat16 or wider, within the bound.
No kernel may reach another device: no remote copies, remote signals or barrier semaphores. Data moves between devices by JAX's collectives and lax.ppermute only.
A program may use at most 128 MiB of HBM per device.

v0:
```python
import jax
import jax.numpy as jnp
from jax import lax
from jax.sharding import PartitionSpec as P

HEAD_DIM = 128
BLOCK = 256


def prefix(shard, axis, combine, identity, reverse):
    peers, place = (lax.axis_size(axis), lax.axis_index(axis))
    everything = jax.tree.map(lambda part: lax.all_gather(part, axis), shard)
    start = jax.tree.map(
        lambda part, zero: jnp.broadcast_to(jnp.asarray(zero, part.dtype), part.shape),
        shard,
        identity,
    )

    def hop(k, before):
        at = peers - 1 - k if reverse else k
        reached = at > place if reverse else at < place
        new = combine(before, jax.tree.map(lambda part: part[at], everything))
        return jax.tree.map(lambda a, b: jnp.where(reached, a, b), new, before)

    return lax.fori_loop(0, peers, hop, start)


def compose(earlier, latter):
    gate_early, state_early = earlier
    gate_late, state_late = latter
    return (gate_early * gate_late, gate_late[..., None, None] * state_early + state_late)


def local_chain(block_gates, block_states, backward):

    def advance(running, element):
        return (compose(running, element), running)

    start_pair = (jnp.ones_like(block_gates[0]), jnp.zeros_like(block_states[0]))
    totals, before = lax.scan(advance, start_pair, (block_gates, block_states), reverse=backward)
    return (totals, before)


def head_major(rows, nblocks, heads_dev):
    return jnp.transpose(rows.reshape(nblocks, BLOCK, heads_dev, HEAD_DIM), (0, 2, 1, 3))


def row_major(blocks, seg_rows, heads_dev):
    return jnp.transpose(blocks, (0, 2, 1, 3)).reshape(seg_rows, heads_dev * HEAD_DIM)


def local(queries, key_rows, value_rows, out_grad, log_decay):
    heads_dev = log_decay.shape[0]
    seg_rows = log_decay.shape[1]
    nblocks = seg_rows // BLOCK
    query_heads, key_heads, value_heads, grad_heads = (
        lax.all_to_all(queries, "head", split_axis=1, concat_axis=0, tiled=True),
        lax.all_to_all(key_rows, "head", split_axis=1, concat_axis=0, tiled=True),
        lax.all_to_all(value_rows, "head", split_axis=1, concat_axis=0, tiled=True),
        lax.all_to_all(out_grad, "head", split_axis=1, concat_axis=0, tiled=True),
    )
    query_heads = head_major(query_heads, nblocks, heads_dev)
    key_heads = head_major(key_heads, nblocks, heads_dev)
    value_heads = head_major(value_heads, nblocks, heads_dev)
    grad_heads = head_major(grad_heads, nblocks, heads_dev)
    decay_blocks = jnp.transpose(log_decay.reshape(heads_dev, nblocks, BLOCK), (1, 0, 2))
    cumulative = jnp.cumsum(decay_blocks, axis=2)
    last_value = cumulative[:, :, -1:]
    query_weight = jnp.exp(cumulative)
    key_weight = jnp.exp(last_value - cumulative)
    block_gates = jnp.exp(last_value[:, :, 0])
    key_scaled = (key_heads.astype(jnp.float32) * key_weight[..., None]).astype(jnp.bfloat16)
    query_scaled = (query_heads.astype(jnp.float32) * query_weight[..., None]).astype(jnp.bfloat16)
    block_state = jnp.einsum(
        "nhbi,nhbj->nhij", key_scaled, value_heads, preferred_element_type=jnp.float32
    )
    block_grad = jnp.einsum(
        "nhbi,nhbj->nhij", query_scaled, grad_heads, preferred_element_type=jnp.float32
    )
    forward_total, forward_before = local_chain(block_gates, block_state, False)
    backward_total, backward_before = local_chain(block_gates, block_grad, True)
    identity_pair = (
        jnp.ones((heads_dev,), jnp.float32),
        jnp.zeros((heads_dev, HEAD_DIM, HEAD_DIM), jnp.float32),
    )
    incoming = prefix(forward_total, "seq", compose, identity_pair, False)[1]
    outgoing = prefix(backward_total, "seq", compose, identity_pair, True)[1]
    state_in = forward_before[0][:, :, None, None] * incoming[None] + forward_before[1]
    state_out = backward_before[0][:, :, None, None] * outgoing[None] + backward_before[1]
    state_in_low = state_in.astype(jnp.bfloat16)
    state_out_low = state_out.astype(jnp.bfloat16)
    token_positions = jnp.arange(BLOCK)
    causal = token_positions[:, None] >= token_positions[None, :]
    spread_log = cumulative[:, :, :, None] - cumulative[:, :, None, :]
    decay_matrix = jnp.where(causal, jnp.exp(jnp.where(causal, spread_log, 0.0)), 0.0)
    grad_scores = (
        jnp.einsum("nhti,nhsi->nhts", grad_heads, value_heads, preferred_element_type=jnp.float32)
        * decay_matrix
    ).astype(jnp.bfloat16)
    scores = (
        jnp.einsum("nhti,nhsi->nhts", query_heads, key_heads, preferred_element_type=jnp.float32)
        * decay_matrix
    ).astype(jnp.bfloat16)
    query_grad = jnp.einsum(
        "nhts,nhsi->nhti", grad_scores, key_heads, preferred_element_type=jnp.float32
    )
    query_grad = query_grad + query_weight[..., None] * jnp.einsum(
        "nhtj,nhij->nhti", grad_heads, state_in_low, preferred_element_type=jnp.float32
    )
    query_grad = row_major(query_grad.astype(jnp.bfloat16), seg_rows, heads_dev)
    key_grad = jnp.einsum(
        "nhts,nhti->nhsi", grad_scores, query_heads, preferred_element_type=jnp.float32
    )
    key_grad = key_grad + key_weight[..., None] * jnp.einsum(
        "nhsj,nhij->nhsi", value_heads, state_out_low, preferred_element_type=jnp.float32
    )
    key_grad = row_major(key_grad.astype(jnp.bfloat16), seg_rows, heads_dev)
    value_grad = jnp.einsum(
        "nhts,nhtj->nhsj", scores, grad_heads, preferred_element_type=jnp.float32
    )
    value_grad = value_grad + key_weight[..., None] * jnp.einsum(
        "nhsi,nhij->nhsj", key_heads, state_out_low, preferred_element_type=jnp.float32
    )
    value_grad = row_major(value_grad.astype(jnp.bfloat16), seg_rows, heads_dev)
    query_back, key_back, value_back = (
        lax.all_to_all(query_grad, "head", split_axis=0, concat_axis=1, tiled=True),
        lax.all_to_all(key_grad, "head", split_axis=0, concat_axis=1, tiled=True),
        lax.all_to_all(value_grad, "head", split_axis=0, concat_axis=1, tiled=True),
    )
    return (query_back, key_back, value_back)


def solution(mesh):
    return jax.shard_map(
        local,
        mesh=mesh,
        in_specs=(
            P(("seq", "head"), None),
            P(("seq", "head"), None),
            P(("seq", "head"), None),
            P(("seq", "head"), None),
            P("head", "seq"),
        ),
        out_specs=(P(("seq", "head"), None), P(("seq", "head"), None), P(("seq", "head"), None)),
        check_vma=False,
    )
```

profile of v0, /device:TPU:0, one launch (start us, length us, event | category | flops | bytes accessed | tf_op | source)
XLA Modules:
  0.0 276.4 jit_solution(65235662730929504)
XLA Ops:
  7.2 2.4 copy.212
  9.6 6.3 %all-to-all-start = ((bf16[64,4,2048]{2,0,1:T(8,128)(2,1)}), bf16[64,4,2048]{2,0,1:T(8,128)(2,1)S(1)}, u32[]{:S(2)}, u32[]{:S(2)}) async-start(bf16[64,4,2048]{2,0,1:T(8,128)(2,1)} %bitcast.163), calls=%async_computation | async-start | bytes 2097152 | tf_op jit(solution)/shard_map/all_to_all | solution.py:60
  16.9 24.7 %all-to-all-done = bf16[64,4,2048]{2,0,1:T(8,128)(2,1)S(1)} async-done(((bf16[64,4,2048]{2,0,1:T(8,128)(2,1)}), bf16[64,4,2048]{2,0,1:T(8,128)(2,1)S(1)}, u32[]{:S(2)}, u32[]{:S(2)}) %all-to-all-start) | async-done | bytes 1048608 | tf_op jit(solution)/shard_map/all_to_all | solution.py:60
  41.6 3.5 %all-to-all-start.4 = ((bf16[64,4,2048]{2,0,1:T(8,128)(2,1)}), bf16[64,4,2048]{2,0,1:T(8,128)(2,1)S(1)}, u32[]{:S(2)}, u32[]{:S(2)}) async-start(bf16[64,4,2048]{2,0,1:T(8,128)(2,1)} %bitcast.160), calls=%async_computation.4 | async-start | bytes 2097152 | tf_op jit(solution)/shard_map/all_to_all | solution.py:57
  46.7 23.7 %all-to-all-done.4 = bf16[64,4,2048]{2,0,1:T(8,128)(2,1)S(1)} async-done(((bf16[64,4,2048]{2,0,1:T(8,128)(2,1)}), bf16[64,4,2048]{2,0,1:T(8,128)(2,1)S(1)}, u32[]{:S(2)}, u32[]{:S(2)}) %all-to-all-start.4) | async-done | bytes 1048608 | tf_op jit(solution)/shard_map/all_to_all | solution.py:57
  71.5 2.9 %convolution_add_fusion = f32[16,128,128]{2,1,0:T(8,128)} fusion(f32[16,256]{1,0:T(8,128)S(1)} %exp.46, bf16[1,256,16,128]{3,2,1,0:T(8,128)(2,1)S(1)} %bitcast.176, bf16[1,256,16,128]{3,2,1,0:T(8,128)(2,1)S(1)} %bitcast.179, f32[16]{0:T(128)S(1)} %exponential_multiply_fusion), kind=kOutput, calls=%fused_computation.21 | convolution fusion | flops 136052736 | bytes 3162176 | tf_op jit(solution)/shard_map/nhbi,nhbj->nhij/dot_general | solution.py:77
  75.5 3.5 %all-to-all-start.2 = ((bf16[64,4,2048]{2,0,1:T(8,128)(2,1)}), bf16[64,4,2048]{2,0,1:T(8,128)(2,1)S(1)}, u32[]{:S(2)}, u32[]{:S(2)}) async-start(bf16[64,4,2048]{2,0,1:T(8,128)(2,1)} %bitcast.161), calls=%async_computation.2 | async-start | bytes 2097152 | tf_op jit(solution)/shard_map/all_to_all | solution.py:58
  80.1 24.1 %all-to-all-done.2 = bf16[64,4,2048]{2,0,1:T(8,128)(2,1)S(1)} async-done(((bf16[64,4,2048]{2,0,1:T(8,128)(2,1)}), bf16[64,4,2048]{2,0,1:T(8,128)(2,1)S(1)}, u32[]{:S(2)}, u32[]{:S(2)}) %all-to-all-start.2) | async-done | bytes 1048608 | tf_op jit(solution)/shard_map/all_to_all | solution.py:58
  104.2 3.5 %all-to-all-start.1 = ((bf16[64,4,2048]{2,0,1:T(8,128)(2,1)}), bf16[64,4,2048]{2,0,1:T(8,128)(2,1)S(1)}, u32[]{:S(2)}, u32[]{:S(2)}) async-start(bf16[64,4,2048]{2,0,1:T(8,128)(2,1)} %bitcast.162), calls=%async_computation.1 | async-start | bytes 2097152 | tf_op jit(solution)/shard_map/all_to_all | solution.py:59
  108.0 24.9 %all-to-all-done.1 = bf16[64,4,2048]{2,0,1:T(8,128)(2,1)S(1)} async-done(((bf16[64,4,2048]{2,0,1:T(8,128)(2,1)}), bf16[64,4,2048]{2,0,1:T(8,128)(2,1)S(1)}, u32[]{:S(2)}, u32[]{:S(2)}) %all-to-all-start.1) | async-done | bytes 1048608 | tf_op jit(solution)/shard_map/all_to_all | solution.py:59
  134.1 2.8 %convolution_add_fusion.1 = f32[16,128,128]{2,1,0:T(8,128)} fusion(f32[16,256]{1,0:T(8,128)S(1)} %get-tuple-element.329, bf16[1,256,16,128]{3,2,1,0:T(8,128)(2,1)S(1)} %bitcast.183, bf16[1,256,16,128]{3,2,1,0:T(8,128)(2,1)S(1)} %bitcast.172, f32[16]{0:T(128)S(1)} %exponential_multiply_fusion), kind=kOutput, calls=%fused_computation.22 | convolution fusion | flops 136052736 | bytes 3162176 | tf_op jit(solution)/shard_map/nhbi,nhbj->nhij/dot_general | solution.py:74
  136.9 8.8 %all-gather = f32[8,16,1]{1,2,0:T(1,128)S(1)} all-gather(f32[1,16,1]{1,2,0:T(1,128)S(1)} %get-tuple-element.331), channel_id=2, replica_groups=mesh['seq'=8,'head'=4] {'seq'}, dimensions={0}, use_global_device_ids=true | all-gather | bytes 576 | tf_op jit(solution)/shard_map/all_gather | solution.py:12
  145.7 3.0 %multiply_convert_fusion.1 = bf16[16,256,256]{2,1,0:T(8,128)(2,1)S(1)} fusion(f32[16,256]{1,0:T(8,128)S(1)} %get-tuple-element.330, pred[256,256]{1,0:T(8,128)(4,1)S(1)} %iota_compare_fusion, bf16[1,256,16,128]{3,2,1,0:T(8,128)(2,1)} %bitcast.184, bf16[1,256,16,128]{3,2,1,0:T(8,128)(2,1)} %bitcast.180), kind=kOutput, calls=%fused_computation.7 | convolution fusion | flops 273678336 | bytes 4276224 | tf_op jit(solution)/shard_map/nhti,nhsi->nhts/dot_general | solution.py:97
  150.1 2.0 fusion.16
  152.1 5.2 %fusion.5 = f32[16,256,128]{2,1,0:T(8,128)} fusion(f32[16,256]{1,0:T(8,128)S(1)} %get-tuple-element.330, pred[256,256]{1,0:T(8,128)(4,1)S(1)} %iota_compare_fusion, bf16[1,256,16,128]{3,2,1,0:T(8,128)(2,1)} %bitcast.177, bf16[1,256,16,128]{3,2,1,0:T(8,128)(2,1)S(1)} %bitcast.174, bf16[1,256,16,128]{3,2,1,0:T(8,128)(2,1)} %bitcast.181), kind=kOutput, calls=%fused_computation.17 | convolution fusion | flops 542113792 | bytes 5324800 | tf_op jit(solution)/shard_map/nhts,nhtj->nhsj/dot_general | solution.py:118
  157.3 12.4 %while.21 = (s32[]{:T(128)}, f32[16,128,128]{2,1,0:T(8,128)S(1)}, s32[]{:T(128)}, f32[8,16]{1,0:T(8,128)S(1)}, f32[8,16,128,128]{3,2,1,0:T(8,128)}, /*index=5*/s32[]{:T(128)}, s32[]{:T(128)}, s32[]{:T(128)}, s32[]{:T(128)}) while((s32[]{:T(128)}, f32[16,128,128]{2,1,0:T(8,128)S(1)}, s32[]{:T(128)}, f32[8,16]{1,0:T(8,128)S(1)}, ...), condition=%wide.region_5.6_spmd.clone, body=%wide.region_4.5_spmd.clone.sunk | while | flops 1048584 | bytes 3146087 | solution.py:25
  163.3 1.8 fusion.60
  169.6 2.2 fusion.8
  173.8 4.4 %all-to-all-start.6 = ((bf16[4,64,2048]{2,1,0:T(8,128)(2,1)}), bf16[4,64,2048]{2,1,0:T(8,128)(2,1)}, u32[]{:S(2)}, u32[]{:S(2)}) async-start(bf16[4,64,2048]{2,1,0:T(8,128)(2,1)} %all_to_all.110), calls=%async_computation.6 | async-start | bytes 2097152 | tf_op jit(solution)/shard_map/all_to_all | solution.py:128
  178.3 12.3 %all-gather.6.cloned.1.call-done = f32[128,128,128]{2,1,0:T(8,128)} async-done(((f32[16,128,128]{2,1,0:T(8,128)}), f32[128,128,128]{2,1,0:T(8,128)}) %all-gather.6.cloned.1.call-update) | async-done | bytes 8388624 | tf_op jit(solution)/shard_map/all_gather | solution.py:12
  190.6 12.0 %while.20 = (s32[]{:T(128)}, f32[16,128,128]{2,1,0:T(8,128)S(1)}, s32[]{:T(128)}, f32[8,16]{1,0:T(8,128)S(1)}, f32[8,16,128,128]{3,2,1,0:T(8,128)}, /*index=5*/s32[]{:T(128)}, s32[]{:T(128)}) while((s32[]{:T(128)}, f32[16,128,128]{2,1,0:T(8,128)S(1)}, s32[]{:T(128)}, f32[8,16]{1,0:T(8,128)S(1)}, f32[8,16,128,128]{3,2,1,0:T(8,128)}, ...), condition=%wide.region_3.4_spmd.clone, body=%wide.region_2.3_spmd.clone.sunk | while | flops 1048580 | bytes 3146025 | solution.py:25
  190.6 1.5 fusion.59
  202.6 2.2 fusion.6
  204.8 1.6 copy.109
  206.5 2.4 all_to_all.99
  208.9 4.6 %all-to-all-start.3 = ((bf16[4,64,2048]{2,1,0:T(8,128)(2,1)}), bf16[4,64,2048]{2,1,0:T(8,128)(2,1)}, u32[]{:S(2)}, u32[]{:S(2)}) async-start(bf16[4,64,2048]{2,1,0:T(8,128)(2,1)} %all_to_all.99), calls=%async_computation.3 | async-start | bytes 2097152 | tf_op jit(solution)/shard_map/all_to_all | solution.py:126
  213.5 2.1 fusion.20
  218.6 21.2 %all-to-all-done.3 = bf16[4,64,2048]{2,1,0:T(8,128)(2,1)} async-done(((bf16[4,64,2048]{2,1,0:T(8,128)(2,1)}), bf16[4,64,2048]{2,1,0:T(8,128)(2,1)}, u32[]{:S(2)}, u32[]{:S(2)}) %all-to-all-start.3) | async-done | bytes 1048608 | tf_op jit(solution)/shard_map/all_to_all | solution.py:126
  239.8 3.5 %all-to-all-start.5 = ((bf16[4,64,2048]{2,1,0:T(8,128)(2,1)}), bf16[4,64,2048]{2,1,0:T(8,128)(2,1)S(1)}, u32[]{:S(2)}, u32[]{:S(2)}) async-start(bf16[4,64,2048]{2,1,0:T(8,128)(2,1)} %all_to_all.106), calls=%async_computation.5 | async-start | bytes 2097152 | tf_op jit(solution)/shard_map/all_to_all | solution.py:127
  243.3 2.3 copy.139
  245.6 2.3 copy.137
  247.9 20.7 %all-to-all-done.5 = bf16[4,64,2048]{2,1,0:T(8,128)(2,1)S(1)} async-done(((bf16[4,64,2048]{2,1,0:T(8,128)(2,1)}), bf16[4,64,2048]{2,1,0:T(8,128)(2,1)S(1)}, u32[]{:S(2)}, u32[]{:S(2)}) %all-to-all-start.5) | async-done | bytes 1048608 | tf_op jit(solution)/shard_map/all_to_all | solution.py:127
  (90 shorter events, 35.1 us)
Async XLA Ops:
  7.2 8.7 %copy-start.7 = (bf16[64,8192]{1,0:T(8,128)(2,1)S(1)}, bf16[64,8192]{1,0:T(8,128)(2,1)}, u32[]{:S(2)}) copy-start(bf16[64,8192]{1,0:T(8,128)(2,1)} %param.9) | copy-start | bytes 3145732
  9.6 32.0 %all-to-all-start = ((bf16[64,4,2048]{2,0,1:T(8,128)(2,1)}), bf16[64,4,2048]{2,0,1:T(8,128)(2,1)S(1)}, u32[]{:S(2)}, u32[]{:S(2)}) async-start(bf16[64,4,2048]{2,0,1:T(8,128)(2,1)} %bitcast.163), calls=%async_computation | async-start | bytes 2097152 | tf_op jit(solution)/shard_map/all_to_all | solution.py:60
  15.9 29.3 %copy-start.10 = (f32[16,256]{1,0:T(8,128)S(1)}, f32[16,256]{1,0:T(8,128)}, u32[]{:S(2)}) copy-start(f32[16,256]{1,0:T(8,128)} %param.13) | copy-start | bytes 49156
  41.6 28.7 %all-to-all-start.4 = ((bf16[64,4,2048]{2,0,1:T(8,128)(2,1)}), bf16[64,4,2048]{2,0,1:T(8,128)(2,1)S(1)}, u32[]{:S(2)}, u32[]{:S(2)}) async-start(bf16[64,4,2048]{2,0,1:T(8,128)(2,1)} %bitcast.160), calls=%async_computation.4 | async-start | bytes 2097152 | tf_op jit(solution)/shard_map/all_to_all | solution.py:57
  45.1 112.1 %all-gather.8.cloned.1.call-start = ((), (), s32[]{:S(2)}) async-start(), calls=%async_computation.8 | async-start | bytes 9437184 | tf_op jit(solution)/shard_map/all_gather | solution.py:12
  46.7 27.7 %copy-start.3 = (bf16[32,8,16,128]{3,2,1,0:T(8,128)(2,1)}, bf16[32,8,16,128]{3,2,1,0:T(8,128)(2,1)S(1)}, u32[]{:S(2)}) copy-start(bf16[32,8,16,128]{3,2,1,0:T(8,128)(2,1)S(1)} %copy.140) | copy-start | bytes 3145732
  70.6 1.0 copy-start.2
  71.5 2.9 %copy-start.8 = (bf16[64,8192]{1,0:T(8,128)(2,1)S(1)}, bf16[64,8192]{1,0:T(8,128)(2,1)}, u32[]{:S(2)}) copy-start(bf16[64,8192]{1,0:T(8,128)(2,1)} %param.10) | copy-start | bytes 3145732
  74.4 4.6 %copy-start.9 = (bf16[64,8192]{1,0:T(8,128)(2,1)S(1)}, bf16[64,8192]{1,0:T(8,128)(2,1)}, u32[]{:S(2)}) copy-start(bf16[64,8192]{1,0:T(8,128)(2,1)} %param.11) | copy-start | bytes 3145732
  75.5 28.7 %all-to-all-start.2 = ((bf16[64,4,2048]{2,0,1:T(8,128)(2,1)}), bf16[64,4,2048]{2,0,1:T(8,128)(2,1)S(1)}, u32[]{:S(2)}, u32[]{:S(2)}) async-start(bf16[64,4,2048]{2,0,1:T(8,128)(2,1)} %bitcast.161), calls=%async_computation.2 | async-start | bytes 2097152 | tf_op jit(solution)/shard_map/all_to_all | solution.py:58
  104.2 28.7 %all-to-all-start.1 = ((bf16[64,4,2048]{2,0,1:T(8,128)(2,1)}), bf16[64,4,2048]{2,0,1:T(8,128)(2,1)S(1)}, u32[]{:S(2)}, u32[]{:S(2)}) async-start(bf16[64,4,2048]{2,0,1:T(8,128)(2,1)} %bitcast.162), calls=%async_computation.1 | async-start | bytes 2097152 | tf_op jit(solution)/shard_map/all_to_all | solution.py:59
  107.7 82.8 %all-gather.6.cloned.1.call-start = ((), (), s32[]{:S(2)}) async-start(), calls=%async_computation.7 | async-start | bytes 9437184 | tf_op jit(solution)/shard_map/all_gather | solution.py:12
  133.1 1.0 copy-start.5
  148.7 1.3 copy-start
  173.8 35.1 %all-to-all-start.6 = ((bf16[4,64,2048]{2,1,0:T(8,128)(2,1)}), bf16[4,64,2048]{2,1,0:T(8,128)(2,1)}, u32[]{:S(2)}, u32[]{:S(2)}) async-start(bf16[4,64,2048]{2,1,0:T(8,128)(2,1)} %all_to_all.110), calls=%async_computation.6 | async-start | bytes 2097152 | tf_op jit(solution)/shard_map/all_to_all | solution.py:128
  190.6 12.0 %copy-start.4 = (bf16[32,8,16,128]{3,2,1,0:T(8,128)(2,1)S(1)}, bf16[32,8,16,128]{3,2,1,0:T(8,128)(2,1)}, u32[]{:S(2)}) copy-start(bf16[32,8,16,128]{3,2,1,0:T(8,128)(2,1)} %copy-done.3) | copy-start | bytes 3145732
  206.5 7.0 %copy-start.1 = (bf16[16,256,256]{2,1,0:T(8,128)(2,1)S(1)}, bf16[16,256,256]{2,1,0:T(8,128)(2,1)}, u32[]{:S(2)}) copy-start(bf16[16,256,256]{2,1,0:T(8,128)(2,1)} %copy-done) | copy-start | bytes 6291460
  208.9 30.9 %all-to-all-start.3 = ((bf16[4,64,2048]{2,1,0:T(8,128)(2,1)}), bf16[4,64,2048]{2,1,0:T(8,128)(2,1)}, u32[]{:S(2)}, u32[]{:S(2)}) async-start(bf16[4,64,2048]{2,1,0:T(8,128)(2,1)} %all_to_all.99), calls=%async_computation.3 | async-start | bytes 2097152 | tf_op jit(solution)/shard_map/all_to_all | solution.py:126
  213.5 2.1 copy-start.6
  239.8 28.8 %all-to-all-start.5 = ((bf16[4,64,2048]{2,1,0:T(8,128)(2,1)}), bf16[4,64,2048]{2,1,0:T(8,128)(2,1)S(1)}, u32[]{:S(2)}, u32[]{:S(2)}) async-start(bf16[4,64,2048]{2,1,0:T(8,128)(2,1)} %all_to_all.106), calls=%async_computation.5 | async-start | bytes 2097152 | tf_op jit(solution)/shard_map/all_to_all | solution.py:127
Sparse Core Ops, SparseCore 0:
  74.5 53.4 all-gather.7
  137.0 53.4 all-gather.5
where the time goes:
time: 278 us; the launch traced here: 276 us
  waiting for transfers between devices  152 us (55%)
  starting transfers between devices  29.5 us (11%)
  other arithmetic  24.5 us (9%)
  local copies, waits for them, and re-layouts  23.9 us (9%)
  matrix products  23.3 us (8%)
  between operations  14.4 us (5%)
  blocking collectives  8.76 us (3%)
    all_to_all x1, waiting for transfers between devices, local(): lax.all_to_all(value_rows, 'head', split_axis=1, concat_axis=0, tiled=True)  24.9 us
    all_to_all x1, waiting for transfers between devices, local(): lax.all_to_all(out_grad, 'head', split_axis=1, concat_axis=0, tiled=True)  24.7 us
    all_to_all x1, waiting for transfers between devices, local(): lax.all_to_all(key_rows, 'head', split_axis=1, concat_axis=0, tiled=True)  24.1 us
    select_n x16, other arithmetic, hop(): return jax.tree.map(lambda a, b: jnp.where(reached, a, b), new, before)  23.7 us
    all_to_all x1, waiting for transfers between devices, local(): lax.all_to_all(queries, 'head', split_axis=1, concat_axis=0, tiled=True)  23.7 us
    all_to_all x1, waiting for transfers between devices, local(): lax.all_to_all(query_grad, 'head', split_axis=0, concat_axis=1, tiled=True)  21.2 us
    all_to_all x1, waiting for transfers between devices, local(): lax.all_to_all(key_grad, 'head', split_axis=0, concat_axis=1, tiled=True)  20.7 us
    all_gather x2, waiting for transfers between devices, prefix(): everything = jax.tree.map(lambda part: lax.all_gather(part, axis), shard)  12.3 us
  transfers between devices with their start and end apart: 9, of which 7 were waited for; matrix products, arithmetic and copies ran while one was open for 21% of the time, Pallas kernels for 0%

commit v1 on v0

v1 whole, which is shorter than its diff:
```python
import functools

import jax
import jax.numpy as jnp
from jax import lax
from jax.experimental import pallas as pl
from jax.experimental.pallas import tpu as pltpu
from jax.sharding import PartitionSpec as P

HEAD_DIM = 128
PARTS = (4, 2)
VMEM = 48 * 1024 * 1024


def swap(x, axis, bit):
    return lax.ppermute(x, axis, [(i, i ^ bit) for i in range(lax.axis_size(axis))])


def params():
    return pltpu.CompilerParams(vmem_limit_bytes=VMEM)


def cost(flops, bytes_accessed):
    return pl.CostEstimate(flops=flops, bytes_accessed=bytes_accessed, transcendentals=0)


def dot(a, b, dims):
    return lax.dot_general(a, b, (dims, ((), ())), preferred_element_type=jnp.float32)


NN = ((1,), (0,))
NT = ((1,), (1,))
TN = ((0,), (0,))


def head_cols(h):
    return slice(h * HEAD_DIM, (h + 1) * HEAD_DIM)


def pack_kernel(cols_ref, q_ref, k_ref, v_ref, g_ref, out_ref):
    for a, ref in enumerate((q_ref, k_ref, v_ref, g_ref)):
        out_ref[0, a] = ref[...]


def pack(cols, arrays, hw, hb):
    rows = arrays[0].shape[0]
    width = hb * HEAD_DIM
    steps = hw // hb
    block = pl.BlockSpec((rows, width), lambda o, i, c: (0, c[o] + i))
    return pl.pallas_call(
        pack_kernel,
        grid_spec=pltpu.PrefetchScalarGridSpec(
            num_scalar_prefetch=1,
            grid=(2, steps),
            in_specs=[block] * 4,
            out_specs=pl.BlockSpec((1, 4, rows, width), lambda o, i, c: (o, 0, 0, i)),
        ),
        out_shape=jax.ShapeDtypeStruct((2, 4, rows, hw * HEAD_DIM), jnp.bfloat16),
        compiler_params=params(),
        cost_estimate=cost(0, 4 * 8 * rows * hw * HEAD_DIM),
        name="pack",
    )(cols, *arrays)


def states_kernel(half, hb, cols_ref, *refs):
    raw = (refs[:4], refs[4:8])
    recv = refs[8 : 8 + half - 1]
    qw_ref, kw_ref, own_ref, send_ref = refs[8 + half - 1 :]
    for o in range(2):
        for h in range(hb):
            c = head_cols(h)

            def rows(a):
                pieces = [raw[o][a][:, c]] + [r[o, a, :, c] for r in recv]
                return jnp.concatenate(pieces, axis=0) if len(pieces) > 1 else pieces[0]

            qw = qw_ref[0, o, :, h : h + 1]
            kw = kw_ref[0, o, :, h : h + 1]
            ks = (rows(1).astype(jnp.float32) * kw).astype(jnp.bfloat16)
            qs = (rows(0).astype(jnp.float32) * qw).astype(jnp.bfloat16)
            state = dot(ks, rows(2), TN)
            grad = dot(qs, rows(3), TN)
            if o == 0:
                own_ref[0, h] = state
                own_ref[1, h] = grad
            else:
                send_ref[0, h] = state.astype(jnp.bfloat16)
                send_ref[1, h] = grad.astype(jnp.bfloat16)


def block_states(cols, arrays, recv, qw, kw, hw, hb):
    rows = arrays[0].shape[0]
    half = len(recv) + 1
    width = hb * HEAD_DIM
    steps = hw // hb
    own_block = pl.BlockSpec((rows, width), lambda i, c: (0, c[0] + i))
    mirror_block = pl.BlockSpec((rows, width), lambda i, c: (0, c[1] + i))
    recv_block = pl.BlockSpec((2, 4, rows, width), lambda i, c: (0, 0, 0, i))
    weight_block = pl.BlockSpec((1, 2, half * rows, hb), lambda i, c: (i, 0, 0, 0))
    state_block = pl.BlockSpec((2, hb, HEAD_DIM, HEAD_DIM), lambda i, c: (0, i, 0, 0))
    shape = (2, hw, HEAD_DIM, HEAD_DIM)
    return pl.pallas_call(
        functools.partial(states_kernel, half, hb),
        grid_spec=pltpu.PrefetchScalarGridSpec(
            num_scalar_prefetch=1,
            grid=(steps,),
            in_specs=[own_block] * 4
            + [mirror_block] * 4
            + [recv_block] * (half - 1)
            + [weight_block] * 2,
            out_specs=[state_block, state_block],
        ),
        out_shape=[
            jax.ShapeDtypeStruct(shape, jnp.float32),
            jax.ShapeDtypeStruct(shape, jnp.bfloat16),
        ],
        compiler_params=params(),
        cost_estimate=cost(
            hw * 2 * 4 * half * rows * HEAD_DIM * HEAD_DIM, 16 * half * rows * hw * HEAD_DIM
        ),
        name="states",
    )(cols, *arrays, *arrays, *recv, qw, kw)


def grads_kernel(half, hb, aliased, cols_ref, *refs):
    raw = refs[:4]
    recv = refs[4 : 4 + half - 1]
    rest = refs[4 + half - 1 :]
    qw_ref, kw_ref, cumc_ref, cumr_ref, bias_ref, st_ref = rest[:6]
    rest = rest[6 + (3 if aliased else 0) :]
    outs = rest[:3]
    sends = rest[3:]
    n = raw[0].shape[0]
    bias = bias_ref[...]
    for h in range(hb):
        c = head_cols(h)

        def rows(a):
            pieces = [raw[a][:, c]] + [r[0, a, :, c] for r in recv]
            return jnp.concatenate(pieces, axis=0) if len(pieces) > 1 else pieces[0]

        q, k, v, g = rows(0), rows(1), rows(2), rows(3)
        qw = qw_ref[0, :, h : h + 1]
        kw = kw_ref[0, :, h : h + 1]
        decay = jnp.exp(cumc_ref[0, :, h : h + 1] - cumr_ref[0, h : h + 1, :] + bias)
        gs = (dot(g, v, NT) * decay).astype(jnp.bfloat16)
        sc = (dot(q, k, NT) * decay).astype(jnp.bfloat16)
        forward = st_ref[0, h]
        backward = st_ref[1, h]
        dq = dot(gs, k, NN) + qw * dot(g, forward, NT)
        dk = dot(gs, q, TN) + kw * dot(v, backward, NT)
        dv = dot(sc, g, TN) + kw * dot(k, backward, NN)
        for a, result in enumerate((dq, dk, dv)):
            result = result.astype(jnp.bfloat16)
            outs[a][:, c] = result[:n]
            for m, send in enumerate(sends):
                send[a, :, c] = result[(m + 1) * n : (m + 2) * n]


def grads(cols, arrays, recv, group, weights, states, outs, hw, hb):
    rows, full = arrays[0].shape
    half = len(recv) + 1
    span = half * rows
    width = hb * HEAD_DIM
    steps = hw // hb
    qw, kw, cumc, cumr, bias = weights
    raw_block = pl.BlockSpec((rows, width), lambda i, c: (0, c[group] + i))
    recv_block = pl.BlockSpec((1, 4, rows, width), lambda i, c: (group, 0, 0, i))
    column = pl.BlockSpec((1, span, hb), lambda i, c: (i, 0, 0))
    row = pl.BlockSpec((1, hb, span), lambda i, c: (i, 0, 0))
    whole = pl.BlockSpec((span, span), lambda i, c: (0, 0))
    state_block = pl.BlockSpec((2, hb, HEAD_DIM, HEAD_DIM), lambda i, c: (0, i, 0, 0))
    aliased = outs is not None
    first = 1 + 4 + (half - 1) + 6
    operands = (cols, *arrays, *recv, qw, kw, cumc, cumr, bias, states)
    results = pl.pallas_call(
        functools.partial(grads_kernel, half, hb, aliased),
        grid_spec=pltpu.PrefetchScalarGridSpec(
            num_scalar_prefetch=1,
            grid=(steps,),
            in_specs=[raw_block] * 4
            + [recv_block] * (half - 1)
            + [column] * 3
            + [row, whole, state_block]
            + ([pl.BlockSpec(memory_space=pl.ANY)] * 3 if aliased else []),
            out_specs=[raw_block] * 3
            + [pl.BlockSpec((3, rows, width), lambda i, c: (0, 0, i))] * (half - 1),
        ),
        out_shape=[jax.ShapeDtypeStruct((rows, full), jnp.bfloat16)] * 3
        + [jax.ShapeDtypeStruct((3, rows, hw * HEAD_DIM), jnp.bfloat16)] * (half - 1),
        input_output_aliases={first + a: a for a in range(3)} if aliased else {},
        compiler_params=params(),
        cost_estimate=cost(
            hw * 2 * (5 * span * span * HEAD_DIM + 3 * span * HEAD_DIM * HEAD_DIM),
            14 * span * hw * HEAD_DIM,
        ),
        name="grads",
    )(*operands, *(outs if aliased else ()))
    return (results[:3], results[3:])


def place_kernel(cols_ref, part_ref, *refs):
    for a in range(3):
        refs[3 + a][...] = part_ref[a]


def place(cols, group, part, outs, hw, hb):
    rows, full = outs[0].shape
    width = hb * HEAD_DIM
    return pl.pallas_call(
        place_kernel,
        grid_spec=pltpu.PrefetchScalarGridSpec(
            num_scalar_prefetch=1,
            grid=(hw // hb,),
            in_specs=[pl.BlockSpec((3, rows, width), lambda i, c: (0, 0, i))]
            + [pl.BlockSpec(memory_space=pl.ANY)] * 3,
            out_specs=[pl.BlockSpec((rows, width), lambda i, c: (0, c[group] + i))] * 3,
        ),
        out_shape=[jax.ShapeDtypeStruct((rows, full), jnp.bfloat16)] * 3,
        input_output_aliases={2 + a: a for a in range(3)},
        compiler_params=params(),
        cost_estimate=cost(0, 12 * rows * hw * HEAD_DIM),
        name="place",
    )(cols, part, *outs)


def seq_logs(block_log):
    every = block_log[None]
    place_ = lax.axis_index("seq")
    bit = 1
    while bit < lax.axis_size("seq"):
        other = swap(every, "seq", bit)
        mine_late = (place_ & bit) != 0
        every = jnp.where(
            mine_late,
            jnp.concatenate([other, every], axis=0),
            jnp.concatenate([every, other], axis=0),
        )
        bit *= 2
    return every


def scan_weights(every):
    peers = lax.axis_size("seq")
    me = lax.axis_index("seq")
    index = jnp.arange(peers)[:, None]

    def total(low, high):
        inside = (index >= low) & (index < high)
        return jnp.exp(jnp.sum(jnp.where(inside, every, 0.0), axis=0))

    result = []
    bit = 1
    while bit < peers:
        start = me - me % bit
        other = start ^ bit
        mine, theirs = total(start, start + bit), total(other, other + bit)
        result.append((total(start, me), total(me + 1, start + bit), mine, theirs))
        bit *= 2
    return result


def spread(gate):
    return gate[:, None, None]


def seq_scan(state_total, grad_total, weights):
    peers = lax.axis_size("seq")
    me = lax.axis_index("seq")
    before = jnp.zeros_like(state_total)
    after = jnp.zeros_like(grad_total)
    for level, (early, late, mine, theirs) in enumerate(weights):
        bit = 1 << level
        upper = (me & bit) != 0
        early = spread(jnp.where(upper, early, 0.0))
        late = spread(jnp.where(upper, 0.0, late))
        if 2 * bit == peers:
            other = swap(
                jnp.where(upper, grad_total, state_total).astype(jnp.bfloat16), "seq", bit
            ).astype(jnp.float32)
            before = before + early * other
            after = after + late * other
        else:
            other = swap(
                jnp.stack([state_total, grad_total]).astype(jnp.bfloat16), "seq", bit
            ).astype(jnp.float32)
            before = before + early * other[0]
            after = after + late * other[1]
            keep_state = spread(jnp.where(upper, 1.0, theirs))
            add_state = spread(jnp.where(upper, mine, 1.0))
            keep_grad = spread(jnp.where(upper, theirs, 1.0))
            add_grad = spread(jnp.where(upper, 1.0, mine))
            state_total = keep_state * state_total + add_state * other[0]
            grad_total = keep_grad * grad_total + add_grad * other[1]
    return (before, after)


def plan(heads):
    if heads % 8 == 0:
        return [(0, heads // 2), (heads // 2, heads // 2)]
    return [(0, heads)]


def local(queries, key_rows, value_rows, out_grad, log_decay):
    arrays = (queries, key_rows, value_rows, out_grad)
    rows = queries.shape[0]
    heads = log_decay.shape[0]
    n = lax.axis_size("head")
    half = n // 2
    z = lax.axis_index("head")
    slot = z % half
    low = z < half
    mirror = z ^ half
    span = half * rows

    logs = jnp.stack([log_decay, swap(log_decay, "head", half)])
    halves = logs.reshape(2, heads, 2, span)
    half_sums = jnp.sum(halves, axis=3)
    my_logs = lax.dynamic_index_in_dim(halves, z // half, axis=2, keepdims=False)
    cum = jnp.cumsum(my_logs, axis=2)
    last = cum[:, :, -1:]
    cum = cum.reshape(2, heads, half, rows)
    order = [slot ^ m for m in range(half)]
    cum = jnp.concatenate(
        [lax.dynamic_index_in_dim(cum, at, axis=2, keepdims=False) for at in order], axis=2
    )
    query_weight = jnp.exp(cum)
    key_weight = jnp.exp(last - cum)
    positions = jnp.concatenate([at * rows + jnp.arange(rows) for at in order])
    bias = jnp.where(positions[:, None] >= positions[None, :], 0.0, -1e30).astype(jnp.float32)
    gate_low = jnp.exp(half_sums[0, :, 0])
    gate_high = jnp.exp(half_sums[0, :, 1])
    weights = scan_weights(seq_logs(half_sums[0, :, 0] + half_sums[0, :, 1]))

    waves = plan(heads)
    received = []
    blocks = []
    for w0, hw in waves:
        hb = next(b for b in PARTS + (1,) if hw % b == 0 and w0 % b == 0 and heads % b == 0)

        def cols(at):
            return (jnp.stack([at, at ^ half]) * heads + w0).astype(jnp.int32) // hb

        blocks.append((hb, cols))
        got = []
        for m in range(1, half):
            got.append(swap(pack(cols(z ^ m), arrays, hw, hb), "head", m))
        received.append(got)

    outs = None
    for w, (w0, hw) in enumerate(waves):
        hb, cols = blocks[w]
        steps = hw // hb
        here = slice(w0, w0 + hw)

        def columns(x):
            x = x[:, here].reshape(2, steps, hb, span)
            return jnp.transpose(x, (1, 0, 3, 2))

        def lines(x):
            return x[:, here].reshape(2, steps, hb, span)

        qw, kw, cumc, cumr = (
            columns(query_weight),
            columns(key_weight),
            columns(cum),
            lines(cum),
        )
        own, send = block_states(cols(z), arrays, received[w], qw, kw, hw, hb)
        theirs = swap(send, "head", half).astype(jnp.float32)
        early = jnp.where(low, own, theirs)
        late = jnp.where(low, theirs, own)
        gl, gh = spread(gate_low[here]), spread(gate_high[here])
        state_total = gh * early[0] + late[0]
        grad_total = early[1] + gl * late[1]
        before, after = seq_scan(
            state_total, grad_total, [tuple(x[here] for x in level) for level in weights]
        )
        low_states = jnp.stack([before, gh * after + late[1]]).astype(jnp.bfloat16)
        high_states = jnp.stack([gl * before + early[0], after]).astype(jnp.bfloat16)
        own_states = jnp.where(low, low_states, high_states)
        mirror_states = swap(jnp.where(low, high_states, low_states), "head", half)
        for group, states in enumerate((own_states, mirror_states)):
            outs, sends = grads(
                cols(z),
                arrays,
                received[w],
                group,
                (qw[:, group], kw[:, group], cumc[:, group], cumr[group], bias),
                states,
                outs,
                hw,
                hb,
            )
            for m, part in enumerate(sends):
                part = swap(part, "head", m + 1)
                outs = place(cols(z ^ (m + 1)), group, part, outs, hw, hb)
    return tuple(outs)


def solution(mesh):
    rows = P(("seq", "head"), None)
    return jax.shard_map(
        local,
        mesh=mesh,
        in_specs=(rows, rows, rows, rows, P("head", "seq")),
        out_specs=(rows, rows, rows),
        check_vma=False,
    )
```

time: 278 us -> 214 us (0.77)
  Pallas kernels: 0 us -> 36.4 us
  waiting for transfers between devices: 152 us -> 116 us
  matrix products: 23.3 us -> 0 us
  between operations: 14.4 us -> 1.34 us
  starting transfers between devices: 29.5 us -> 20.2 us
  blocking collectives: 8.76 us -> 0 us
  other arithmetic: 24.5 us -> 18.7 us
  local copies, waits for them, and re-layouts: 23.9 us -> 20.4 us
    all_to_all x7 -> x0, waiting for transfers between devices: 139 us -> none  [the longest x1 24.9 us: local(): lax.all_to_all(value_rows, 'head', split_axis=1, concat_axis=0, tiled=True)]
    ppermute x0 -> x20, waiting for transfers between devices: none -> 116 us  [swap(): lax.ppermute(x, axis, [(i, i ^ bit) for i in range(lax.axis_size(axis))])]
    pallas_call x0 -> x12, Pallas kernels: none -> 36.4 us  [the longest x4 18.1 us: grads(): pl.pallas_call(functools.partial(grads_kernel, half, hb, aliased), grid_s...]
    all_to_all x7 -> x0, starting transfers between devices: 29.4 us -> none  [the longest x1 6.32 us: local(): lax.all_to_all(out_grad, 'head', split_axis=1, concat_axis=0, tiled=True)]
    dot_general x9 -> x0, matrix products: 23.3 us -> none  [the longest x1 5.16 us: local(): jnp.einsum('nhts,nhtj->nhsj', scores, grad_heads, preferred_element_type=...]
    ppermute x0 -> x20, starting transfers between devices: none -> 20.2 us  [swap(): lax.ppermute(x, axis, [(i, i ^ bit) for i in range(lax.axis_size(axis))])]
    select_n x16 -> x20, other arithmetic: 23.7 us -> 6.57 us  [the longest x3 2 us: seq_scan(): late = spread(jnp.where(upper, 0.0, late))]
    all_to_all x10 -> x0, local copies, waits for them, and re-layouts: 16.2 us -> none  [the longest x2 4.75 us: local(): lax.all_to_all(query_grad, 'head', split_axis=0, concat_axis=1, tiled=True)]
  transfers between devices with their start and end apart: 9 -> 20, of which waited for: 7 -> 10; matrix products, arithmetic and copies ran while one was open for 21% -> 13% of each run, Pallas kernels for 0% -> 12%
where the time goes in v1:
time: 214 us; the launch traced here: 213 us
  waiting for transfers between devices  116 us (54%)
  Pallas kernels  36.4 us (17%)
  local copies, waits for them, and re-layouts  20.4 us (10%)
  starting transfers between devices  20.2 us (9%)
  other arithmetic  18.7 us (9%)
    ppermute x20, waiting for transfers between devices, swap(): lax.ppermute(x, axis, [(i, i ^ bit) for i in range(lax.axis_size(axis))])  116 us
    ppermute x20, starting transfers between devices, swap(): lax.ppermute(x, axis, [(i, i ^ bit) for i in range(lax.axis_size(axis))])  20.2 us
    pallas_call x4, Pallas kernels, grads(): pl.pallas_call(functools.partial(grads_kernel, half, hb, aliased), grid_s...  18.1 us
    unnamed x97, local copies, waits for them, and re-layouts  11.2 us
    pallas_call x2, Pallas kernels, block_states(): pl.pallas_call(functools.partial(states_kernel, half, hb), grid_spec=pltp...  7.33 us
    pallas_call x4, Pallas kernels, place(): pl.pallas_call(place_kernel, grid_spec=pltpu.PrefetchScalarGridSpec(num_s...  6.43 us
    pallas_call x2, Pallas kernels, pack(): pl.pallas_call(pack_kernel, grid_spec=pltpu.PrefetchScalarGridSpec(num_sc...  4.48 us
  transfers between devices with their start and end apart: 20, of which 10 were waited for; matrix products, arithmetic and copies ran while one was open for 13% of the time, Pallas kernels for 12%

profile of v1, /device:TPU:0, one launch (start us, length us, event | category | flops | bytes accessed | tf_op | source)
XLA Modules:
  0.0 213.4 jit_solution(3594910388319972489)
XLA Ops:
  0.6 4.1 %collective-permute-start.1 = (f32[16,256]{1,0:T(8,128)}, f32[16,256]{1,0:T(8,128)S(1)}, u32[]{:S(2)}, u32[]{:S(2)}) collective-permute-start(f32[16,256]{1,0:T(8,128)} %param.9), channel_id=1, source_target_pairs={{0,2},{1,3},{2,0},{3,1},{4,6},{5,7},{6,4},{7,5},{8,10},{9,11},{10,... | collective-permute-start | bytes 49160 | tf_op jit(solution)/shard_map/ppermute | solution.py:16
  9.7 2.2 %pack.3 = bf16[2,4,64,1024]{3,2,1,0:T(8,128)(2,1)} custom-call(s32[2]{0:T(128)S(1)} %get-tuple-element.80.cols_ref, bf16[64,8192]{1,0:T(8,128)(2,1)S(1)} %copy-done, bf16[64,8192]{1,0:T(8,128)(2,1)S(1)} %copy-done.2, bf16[64,8192]{1,0:T(8,128)(2,1)S(1)} %copy-done.4, bf16[64,8192]{1,0:T(8,128)(2,1)S(1)} %copy-done.6), custom_call_target="tpu_custom_call" | custom-call | bytes 2097152 | tf_op jit(solution)/shard_map/pack/pallas_call | solution.py:50
  12.0 1.6 collective-permute-start.10
  14.9 2.2 %pack.2 = bf16[2,4,64,1024]{3,2,1,0:T(8,128)(2,1)} custom-call(s32[2]{0:T(128)S(1)} %get-tuple-element.167.cols_ref, bf16[64,8192]{1,0:T(8,128)(2,1)S(1)} %copy-done.1, bf16[64,8192]{1,0:T(8,128)(2,1)S(1)} %copy-done.3, bf16[64,8192]{1,0:T(8,128)(2,1)S(1)} %copy-done.5, bf16[64,8192]{1,0:T(8,128)(2,1)S(1)} %copy-done.7), custom_call_target="tpu_custom_call" | custom-call | bytes 2097152 | tf_op jit(solution)/shard_map/pack/pallas_call | solution.py:50
  22.0 1.3 add_reduce_fusion
  28.3 1.5 collective-permute-start.3
  32.0 1.6 collective-permute-start.4
  41.6 3.7 %states.3 = (f32[2,8,128,128]{3,2,1,0:T(8,128)S(1)}, bf16[2,8,128,128]{3,2,1,0:T(8,128)(2,1)S(1)}) custom-call(s32[2]{0:T(128)S(1)} %get-tuple-element.78.cols_ref, bf16[64,8192]{1,0:T(8,128)(2,1)S(1)} %copy-done.1, bf16[64,8192]{1,0:T(8,128)(2,1)S(1)} %copy-done.3, bf16[64,8192]{1,0:T(8,128)(2,1)S(1)} %copy-done.5, bf16[64,8192]{1,0:T(8,128)(2,1)} %refs_3_.11, ...), custom_call_target="tpu_custom_call" | custom-call | flops 134217728 | bytes 2097152 | tf_op jit(solution)/shard_map/states/pallas_call | solution.py:102
  46.3 23.9 %collective-permute-done.refs_8_.refs_4_ = bf16[2,4,64,1024]{3,2,1,0:T(8,128)(2,1)} collective-permute-done((bf16[2,4,64,1024]{3,2,1,0:T(8,128)(2,1)}, bf16[2,4,64,1024]{3,2,1,0:T(8,128)(2,1)}, u32[]{:S(2)}, u32[]{:S(2)}) %collective-permute-start) | collective-permute-done | bytes 1048608 | tf_op jit(solution)/shard_map/ppermute | solution.py:16
  70.2 3.7 %states.2 = (f32[2,8,128,128]{3,2,1,0:T(8,128)S(1)}, bf16[2,8,128,128]{3,2,1,0:T(8,128)(2,1)S(1)}) custom-call(s32[2]{0:T(128)S(1)} %and_select_fusion.2.cols_ref, bf16[64,8192]{1,0:T(8,128)(2,1)S(1)} %copy-done.1, bf16[64,8192]{1,0:T(8,128)(2,1)S(1)} %copy-done.3, bf16[64,8192]{1,0:T(8,128)(2,1)S(1)} %copy-done.5, bf16[64,8192]{1,0:T(8,128)(2,1)} %refs_3_.11, ...), custom_call_target="tpu_custom_call" | custom-call | flops 134217728 | bytes 2097152 | tf_op jit(solution)/shard_map/states/pallas_call | solution.py:102
  75.2 22.5 %collective-permute-done.5 = bf16[2,8,128,128]{3,2,1,0:T(8,128)(2,1)S(1)} collective-permute-done((bf16[2,8,128,128]{3,2,1,0:T(8,128)(2,1)S(1)}, bf16[2,8,128,128]{3,2,1,0:T(8,128)(2,1)S(1)}, u32[]{:S(2)}, u32[]{:S(2)}) %collective-permute-start.5) | collective-permute-done | bytes 524320 | tf_op jit(solution)/shard_map/ppermute | solution.py:16
  99.6 1.6 collective-permute-start.13
  102.9 11.5 %collective-permute-done.13 = bf16[2,8,128,128]{3,2,1,0:T(8,128)(2,1)S(1)} collective-permute-done((bf16[2,8,128,128]{3,2,1,0:T(8,128)(2,1)S(1)}, bf16[2,8,128,128]{3,2,1,0:T(8,128)(2,1)S(1)}, u32[]{:S(2)}, u32[]{:S(2)}) %collective-permute-start.13) | collective-permute-done | bytes 524320 | tf_op jit(solution)/shard_map/ppermute | solution.py:16
  115.0 1.8 collective-permute-start.14
  116.7 8.3 %collective-permute-done.7 = bf16[2,8,128,128]{3,2,1,0:T(8,128)(2,1)S(1)} collective-permute-done((bf16[2,8,128,128]{3,2,1,0:T(8,128)(2,1)S(1)}, bf16[2,8,128,128]{3,2,1,0:T(8,128)(2,1)S(1)}, u32[]{:S(2)}, u32[]{:S(2)}) %collective-permute-start.7) | collective-permute-done | bytes 524320 | tf_op jit(solution)/shard_map/ppermute | solution.py:16
  125.1 1.3 fusion.24
  126.4 1.7 collective-permute-start.8
  130.1 4.6 %grads.4 = (bf16[64,8192]{1,0:T(8,128)(2,1)}, bf16[64,8192]{1,0:T(8,128)(2,1)}, bf16[64,8192]{1,0:T(8,128)(2,1)}, bf16[3,64,1024]{2,1,0:T(8,128)(2,1)}) custom-call(s32[2]{0:T(128)S(1)} %get-tuple-element.78.cols_ref, bf16[64,8192]{1,0:T(8,128)(2,1)S(1)} %copy-done.1, bf16[64,8192]{1,0:T(8,128)(2,1)S(1)} %copy-done.3, bf16[64,8192]{1,0:T(8,128)(2,1)S(1)} %copy-done.5, ...), custom_call_target="tpu_custom_call" | custom-call | flops 268435456 | bytes 1835008 | tf_op jit(solution)/shard_map/grads/pallas_call | solution.py:176
  134.7 2.3 %collective-permute-start.16 = (bf16[3,64,1024]{2,1,0:T(8,128)(2,1)}, bf16[3,64,1024]{2,1,0:T(8,128)(2,1)}, u32[]{:S(2)}, u32[]{:S(2)}) collective-permute-start(bf16[3,64,1024]{2,1,0:T(8,128)(2,1)} %get-tuple-element.36), channel_id=1, source_target_pairs={{0,1},{1,0},{2,3},{3,2},{4,5},{5,4},{6,7},{7,6},{8,9},{9,8},{10,11... | collective-permute-start | bytes 1179656 | tf_op jit(solution)/shard_map/ppermute | solution.py:16
  138.6 2.1 %fusion.35 = (bf16[1,8,128,128]{3,2,1,0:T(8,128)(2,1)S(1)}, bf16[8,128,128]{2,1,0:T(8,128)(2,1)S(1)}, bf16[1,8,128,128]{3,2,1,0:T(8,128)(2,1)S(1)}, f32[8,128,128]{2,1,0:T(8,128)S(1)}) fusion(f32[2,8,128,128]{3,2,1,0:T(8,128)} %copy-done.23, f32[8]{0:T(128)S(1)} %get-tuple-element.172, bf16[8,128,128]{2,1,0:T(8,128)(2,1)} %collective-permute-done.8, ...), kind=kLoop, calls=%fused_computation.85 | loop fusion | flops 2097152 | bytes 4194528 | tf_op jit(solution)/shard_map/stack | solution.py:380
  140.7 15.9 %collective-permute-done.16.part_ref = bf16[3,64,1024]{2,1,0:T(8,128)(2,1)} collective-permute-done((bf16[3,64,1024]{2,1,0:T(8,128)(2,1)}, bf16[3,64,1024]{2,1,0:T(8,128)(2,1)}, u32[]{:S(2)}, u32[]{:S(2)}) %collective-permute-start.16) | collective-permute-done | bytes 393248 | tf_op jit(solution)/shard_map/ppermute | solution.py:16
  156.7 2.3 %place.4 = (bf16[64,8192]{1,0:T(8,128)(2,1)}, bf16[64,8192]{1,0:T(8,128)(2,1)}, bf16[64,8192]{1,0:T(8,128)(2,1)}) custom-call(s32[2]{0:T(128)S(1)} %get-tuple-element.80.cols_ref, bf16[3,64,1024]{2,1,0:T(8,128)(2,1)} %collective-permute-done.16.part_ref, ...), custom_call_target="tpu_custom_call", output_to_operand_aliasing={{0}: (2, {}), {1}: (3, {}), {2}: (4, {})} | custom-call | bytes 786432 | tf_op jit(solution)/shard_map/place/pallas_call | solution.py:210
  159.0 4.6 %grads.5 = (bf16[64,8192]{1,0:T(8,128)(2,1)}, bf16[64,8192]{1,0:T(8,128)(2,1)}, bf16[64,8192]{1,0:T(8,128)(2,1)}, bf16[3,64,1024]{2,1,0:T(8,128)(2,1)S(1)}) custom-call(s32[2]{0:T(128)S(1)} %get-tuple-element.78.cols_ref, bf16[64,8192]{1,0:T(8,128)(2,1)S(1)} %copy-done.1, ...), custom_call_target="tpu_custom_call", output_to_operand_aliasing={{0}: (12, {}), {1}: (13, {}), {2}: (14, {})} | custom-call | flops 268435456 | bytes 1835008 | tf_op jit(solution)/shard_map/grads/pallas_call | solution.py:176
  163.8 2.6 %collective-permute-start.9 = (bf16[2,8,128,128]{3,2,1,0:T(8,128)(2,1)S(1)}, bf16[2,8,128,128]{3,2,1,0:T(8,128)(2,1)S(1)}, u32[]{:S(2)}, u32[]{:S(2)}) collective-permute-start(bf16[2,8,128,128]{3,2,1,0:T(8,128)(2,1)S(1)} %get-tuple-element.105), channel_id=1, source_target_pairs={{0,2},{1,3},{2,0},{3,1},{4,6},{5,7},{6,4},{7,5},{8,10},{9,11},{10,... | collective-permute-start | bytes 1572872 | tf_op jit(solution)/shard_map/ppermute | solution.py:16
  166.4 13.9 %collective-permute-done.17.part_ref = bf16[3,64,1024]{2,1,0:T(8,128)(2,1)S(1)} collective-permute-done((bf16[3,64,1024]{2,1,0:T(8,128)(2,1)S(1)}, bf16[3,64,1024]{2,1,0:T(8,128)(2,1)S(1)}, u32[]{:S(2)}, u32[]{:S(2)}) %collective-permute-start.17) | collective-permute-done | bytes 393248 | tf_op jit(solution)/shard_map/ppermute | solution.py:16
  180.3 1.4 place.5
  181.7 4.5 %grads.6 = (bf16[64,8192]{1,0:T(8,128)(2,1)}, bf16[64,8192]{1,0:T(8,128)(2,1)}, bf16[64,8192]{1,0:T(8,128)(2,1)}, bf16[3,64,1024]{2,1,0:T(8,128)(2,1)S(1)}) custom-call(s32[2]{0:T(128)S(1)} %and_select_fusion.2.cols_ref, bf16[64,8192]{1,0:T(8,128)(2,1)S(1)} %copy-done.1, ...), custom_call_target="tpu_custom_call", output_to_operand_aliasing={{0}: (12, {}), {1}: (13, {}), {2}: (14, {})} | custom-call | flops 268435456 | bytes 1835008 | tf_op jit(solution)/shard_map/grads/pallas_call | solution.py:176
  186.2 10.4 %collective-permute-done.18.part_ref = bf16[3,64,1024]{2,1,0:T(8,128)(2,1)S(1)} collective-permute-done((bf16[3,64,1024]{2,1,0:T(8,128)(2,1)S(1)}, bf16[3,64,1024]{2,1,0:T(8,128)(2,1)S(1)}, u32[]{:S(2)}, u32[]{:S(2)}) %collective-permute-start.18) | collective-permute-done | bytes 393248 | tf_op jit(solution)/shard_map/ppermute | solution.py:16
  196.6 1.4 place.6
  198.0 4.5 %grads.7 = (bf16[64,8192]{1,0:T(8,128)(2,1)}, bf16[64,8192]{1,0:T(8,128)(2,1)}, bf16[64,8192]{1,0:T(8,128)(2,1)}, bf16[3,64,1024]{2,1,0:T(8,128)(2,1)S(1)}) custom-call(s32[2]{0:T(128)S(1)} %and_select_fusion.2.cols_ref, bf16[64,8192]{1,0:T(8,128)(2,1)S(1)} %copy-done.1, ...), custom_call_target="tpu_custom_call", output_to_operand_aliasing={{0}: (12, {}), {1}: (13, {}), {2}: (14, {})} | custom-call | flops 268435456 | bytes 1835008 | tf_op jit(solution)/shard_map/grads/pallas_call | solution.py:176
  202.5 9.5 %collective-permute-done.19.part_ref = bf16[3,64,1024]{2,1,0:T(8,128)(2,1)S(1)} collective-permute-done((bf16[3,64,1024]{2,1,0:T(8,128)(2,1)S(1)}, bf16[3,64,1024]{2,1,0:T(8,128)(2,1)S(1)}, u32[]{:S(2)}, u32[]{:S(2)}) %collective-permute-start.19) | collective-permute-done | bytes 393248 | tf_op jit(solution)/shard_map/ppermute | solution.py:16
  212.0 1.4 place.7
  (205 shorter events, 36.4 us)
Async XLA Ops:
  0.6 20.0 %collective-permute-start.1 = (f32[16,256]{1,0:T(8,128)}, f32[16,256]{1,0:T(8,128)S(1)}, u32[]{:S(2)}, u32[]{:S(2)}) collective-permute-start(f32[16,256]{1,0:T(8,128)} %param.9), channel_id=1, source_target_pairs={{0,2},{1,3},{2,0},{3,1},{4,6},{5,7},{6,4},{7,5},{8,10},{9,11},{10,... | collective-permute-start | bytes 49160 | tf_op jit(solution)/shard_map/ppermute | solution.py:16
  9.7 3.9 %copy-start.1 = (bf16[64,8192]{1,0:T(8,128)(2,1)S(1)}, bf16[64,8192]{1,0:T(8,128)(2,1)}, u32[]{:S(2)}) copy-start(bf16[64,8192]{1,0:T(8,128)(2,1)} %refs_0_.11) | copy-start | bytes 3145732
  9.7 3.9 %copy-start.3 = (bf16[64,8192]{1,0:T(8,128)(2,1)S(1)}, bf16[64,8192]{1,0:T(8,128)(2,1)}, u32[]{:S(2)}) copy-start(bf16[64,8192]{1,0:T(8,128)(2,1)} %refs_1_.11) | copy-start | bytes 3145732
  9.7 3.9 %copy-start.5 = (bf16[64,8192]{1,0:T(8,128)(2,1)S(1)}, bf16[64,8192]{1,0:T(8,128)(2,1)}, u32[]{:S(2)}) copy-start(bf16[64,8192]{1,0:T(8,128)(2,1)} %refs_2_.11) | copy-start | bytes 3145732
  12.0 27.7 %collective-permute-start.10 = (bf16[2,4,64,1024]{3,2,1,0:T(8,128)(2,1)}, bf16[2,4,64,1024]{3,2,1,0:T(8,128)(2,1)}, u32[]{:S(2)}, u32[]{:S(2)}) collective-permute-start(bf16[2,4,64,1024]{3,2,1,0:T(8,128)(2,1)} %pack.3), channel_id=1, source_target_pairs={{0,1},{1,0},{2,3},{3,2},{4,5},{5,4},{6,7},{7,6},{8,9},{9,8},{10,11... | collective-permute-start | bytes 3145736 | tf_op jit(solution)/shard_map/ppermute | solution.py:16
  14.9 2.7 %copy-start.30 = (f32[16,256]{1,0:T(8,128)S(1)}, f32[16,256]{1,0:T(8,128)}, u32[]{:S(2)}) copy-start(f32[16,256]{1,0:T(8,128)} %param.9) | copy-start | bytes 49156
  17.1 53.0 %collective-permute-start = (bf16[2,4,64,1024]{3,2,1,0:T(8,128)(2,1)}, bf16[2,4,64,1024]{3,2,1,0:T(8,128)(2,1)}, u32[]{:S(2)}, u32[]{:S(2)}) collective-permute-start(bf16[2,4,64,1024]{3,2,1,0:T(8,128)(2,1)} %pack.2), channel_id=1, source_target_pairs={{0,1},{1,0},{2,3},{3,2},{4,5},{5,4},{6,7},{7,6},{8,9},{9,8},{10,11... | collective-permute-start | bytes 3145736 | tf_op jit(solution)/shard_map/ppermute | solution.py:16
  23.3 4.3 %collective-permute-start.2 = (f32[1,16]{1,0:T(1,128)}, f32[1,16]{1,0:T(1,128)}, u32[]{:S(2)}, u32[]{:S(2)}) collective-permute-start(f32[1,16]{1,0:T(1,128)} %bitcast.63), channel_id=1, source_target_pairs={{0,4},{4,0},{8,12},{12,8},{16,20},{20,16},{24,28},{28,24},{1,5},{5... | collective-permute-start | bytes 200 | tf_op jit(solution)/shard_map/ppermute | solution.py:16
  28.3 3.6 %collective-permute-start.3 = (f32[2,16]{1,0:T(2,128)S(1)}, f32[2,16]{1,0:T(2,128)S(1)}, u32[]{:S(2)}, u32[]{:S(2)}) collective-permute-start(f32[2,16]{1,0:T(2,128)S(1)} %maximum_select_fusion.2), channel_id=1, source_target_pairs={{0,8},{4,12},{8,0},{12,4},{16,24},{20,28},{24,16},{28,20},{1,9},{5... | collective-permute-start | bytes 392 | tf_op jit(solution)/shard_map/ppermute | solution.py:16
  32.0 3.7 %collective-permute-start.4 = (f32[4,16]{1,0:T(4,128)S(1)}, f32[4,16]{1,0:T(4,128)S(1)}, u32[]{:S(2)}, u32[]{:S(2)}) collective-permute-start(f32[4,16]{1,0:T(4,128)S(1)} %maximum_select_fusion.1), channel_id=1, source_target_pairs={{0,16},{4,20},{8,24},{12,28},{16,0},{20,4},{24,8},{28,12},{1,17},{... | collective-permute-start | bytes 776 | tf_op jit(solution)/shard_map/ppermute | solution.py:16
  34.6 2.5 %copy-start.42 = (pred[8]{0:T(512)(128)(4,1)S(1)}, pred[8]{0:T(512)(128)(4,1)}, u32[]{:S(2)}) copy-start(pred[8]{0:T(512)(128)(4,1)} %get-tuple-element.179) | copy-start | bytes 28
  41.6 28.6 %copy-start.10 = (f32[2,2,4,128]{2,3,0,1:T(8,128)S(1)}, f32[2,2,4,128]{2,3,0,1:T(8,128)}, u32[]{:S(2)}) copy-start(f32[2,2,4,128]{2,3,0,1:T(8,128)} %copy.63) | copy-start | bytes 24580
  45.3 28.6 %collective-permute-start.11 = (bf16[2,8,128,128]{3,2,1,0:T(8,128)(2,1)S(1)}, bf16[2,8,128,128]{3,2,1,0:T(8,128)(2,1)S(1)}, u32[]{:S(2)}, u32[]{:S(2)}) collective-permute-start(bf16[2,8,128,128]{3,2,1,0:T(8,128)(2,1)S(1)} %get-tuple-element.35), channel_id=1, source_target_pairs={{0,2},{1,3},{2,0},{3,1},{4,6},{5,7},{6,4},{7,5},{8,10},{9,11},{10,... | collective-permute-start | bytes 1572872 | tf_op jit(solution)/shard_map/ppermute | solution.py:16
  73.8 23.8 %collective-permute-start.5 = (bf16[2,8,128,128]{3,2,1,0:T(8,128)(2,1)S(1)}, bf16[2,8,128,128]{3,2,1,0:T(8,128)(2,1)S(1)}, u32[]{:S(2)}, u32[]{:S(2)}) collective-permute-start(bf16[2,8,128,128]{3,2,1,0:T(8,128)(2,1)S(1)} %get-tuple-element.33), channel_id=1, source_target_pairs={{0,2},{1,3},{2,0},{3,1},{4,6},{5,7},{6,4},{7,5},{8,10},{9,11},{10,... | collective-permute-start | bytes 1572872 | tf_op jit(solution)/shard_map/ppermute | solution.py:16
  75.1 24.0 %collective-permute-start.12 = (bf16[2,8,128,128]{3,2,1,0:T(8,128)(2,1)S(1)}, bf16[2,8,128,128]{3,2,1,0:T(8,128)(2,1)S(1)}, u32[]{:S(2)}, u32[]{:S(2)}) collective-permute-start(bf16[2,8,128,128]{3,2,1,0:T(8,128)(2,1)S(1)} %pad_maximum_fusion.4), channel_id=1, source_target_pairs={{0,4},{4,0},{8,12},{12,8},{16,20},{20,16},{24,28},{28,24},{1,5},{5... | collective-permute-start | bytes 1572872 | tf_op jit(solution)/shard_map/ppermute | solution.py:16
  97.9 27.2 %copy-start.21 = (f32[2,8,128,128]{3,2,1,0:T(8,128)}, f32[2,8,128,128]{3,2,1,0:T(8,128)S(1)}, u32[]{:S(2)}) copy-start(f32[2,8,128,128]{3,2,1,0:T(8,128)S(1)} %get-tuple-element.101) | copy-start | bytes 3145732
  97.9 27.2 %copy-start.23 = (f32[2,8,128,128]{3,2,1,0:T(8,128)}, f32[2,8,128,128]{3,2,1,0:T(8,128)S(1)}, u32[]{:S(2)}) copy-start(f32[2,8,128,128]{3,2,1,0:T(8,128)S(1)} %get-tuple-element.100) | copy-start | bytes 3145732
  98.2 3.0 %collective-permute-start.6 = (bf16[2,8,128,128]{3,2,1,0:T(8,128)(2,1)S(1)}, bf16[2,8,128,128]{3,2,1,0:T(8,128)(2,1)S(1)}, u32[]{:S(2)}, u32[]{:S(2)}) collective-permute-start(bf16[2,8,128,128]{3,2,1,0:T(8,128)(2,1)S(1)} %pad_maximum_fusion), channel_id=1, source_target_pairs={{0,4},{4,0},{8,12},{12,8},{16,20},{20,16},{24,28},{28,24},{1,5},{5... | collective-permute-start | bytes 1572872 | tf_op jit(solution)/shard_map/ppermute | solution.py:16
  99.6 14.8 %collective-permute-start.13 = (bf16[2,8,128,128]{3,2,1,0:T(8,128)(2,1)S(1)}, bf16[2,8,128,128]{3,2,1,0:T(8,128)(2,1)S(1)}, u32[]{:S(2)}, u32[]{:S(2)}) collective-permute-start(bf16[2,8,128,128]{3,2,1,0:T(8,128)(2,1)S(1)} %pad_maximum_fusion.5), channel_id=1, source_target_pairs={{0,8},{4,12},{8,0},{12,4},{16,24},{20,28},{24,16},{28,20},{1,9},{5... | collective-permute-start | bytes 1572872 | tf_op jit(solution)/shard_map/ppermute | solution.py:16
  101.2 23.9 %copy-start.24 = (f32[2,8,128,128]{3,2,1,0:T(8,128)}, f32[2,8,128,128]{3,2,1,0:T(8,128)S(1)}, u32[]{:S(2)}) copy-start(f32[2,8,128,128]{3,2,1,0:T(8,128)S(1)} %convert_element_type.39) | copy-start | bytes 3145732
  101.6 23.3 %collective-permute-start.7 = (bf16[2,8,128,128]{3,2,1,0:T(8,128)(2,1)S(1)}, bf16[2,8,128,128]{3,2,1,0:T(8,128)(2,1)S(1)}, u32[]{:S(2)}, u32[]{:S(2)}) collective-permute-start(bf16[2,8,128,128]{3,2,1,0:T(8,128)(2,1)S(1)} %pad_maximum_fusion.1), channel_id=1, source_target_pairs={{0,8},{4,12},{8,0},{12,4},{16,24},{20,28},{24,16},{28,20},{1,9},{5... | collective-permute-start | bytes 1572872 | tf_op jit(solution)/shard_map/ppermute | solution.py:16
  115.0 13.1 %collective-permute-start.14 = (bf16[8,128,128]{2,1,0:T(8,128)(2,1)S(1)}, bf16[8,128,128]{2,1,0:T(8,128)(2,1)S(1)}, u32[]{:S(2)}, u32[]{:S(2)}) collective-permute-start(bf16[8,128,128]{2,1,0:T(8,128)(2,1)S(1)} %fusion.9), channel_id=1, source_target_pairs={{0,16},{4,20},{8,24},{12,28},{16,0},{20,4},{24,8},{28,12},{1,17},{... | collective-permute-start | bytes 786440 | tf_op jit(solution)/shard_map/ppermute | solution.py:16
  126.4 11.6 %collective-permute-start.8 = (bf16[8,128,128]{2,1,0:T(8,128)(2,1)}, bf16[8,128,128]{2,1,0:T(8,128)(2,1)}, u32[]{:S(2)}, u32[]{:S(2)}) collective-permute-start(bf16[8,128,128]{2,1,0:T(8,128)(2,1)} %fusion.24), channel_id=1, source_target_pairs={{0,16},{4,20},{8,24},{12,28},{16,0},{20,4},{24,8},{28,12},{1,17},{... | collective-permute-start | bytes 786440 | tf_op jit(solution)/shard_map/ppermute | solution.py:16
  129.6 29.3 %collective-permute-start.15 = (bf16[2,8,128,128]{3,2,1,0:T(8,128)(2,1)}, bf16[2,8,128,128]{3,2,1,0:T(8,128)(2,1)}, u32[]{:S(2)}, u32[]{:S(2)}) collective-permute-start(bf16[2,8,128,128]{3,2,1,0:T(8,128)(2,1)} %get-tuple-element.103), channel_id=1, source_target_pairs={{0,2},{1,3},{2,0},{3,1},{4,6},{5,7},{6,4},{7,5},{8,10},{9,11},{10,... | collective-permute-start | bytes 1572872 | tf_op jit(solution)/shard_map/ppermute | solution.py:16
  130.1 6.9 %copy-start.26 = (f32[2,2,4,128]{2,3,1,0:T(8,128)S(1)}, f32[2,2,4,128]{2,3,1,0:T(8,128)}, u32[]{:S(2)}) copy-start(f32[2,2,4,128]{2,3,1,0:T(8,128)} %copy.53) | copy-start | bytes 24580
  134.7 21.9 %collective-permute-start.16 = (bf16[3,64,1024]{2,1,0:T(8,128)(2,1)}, bf16[3,64,1024]{2,1,0:T(8,128)(2,1)}, u32[]{:S(2)}, u32[]{:S(2)}) collective-permute-start(bf16[3,64,1024]{2,1,0:T(8,128)(2,1)} %get-tuple-element.36), channel_id=1, source_target_pairs={{0,1},{1,0},{2,3},{3,2},{4,5},{5,4},{6,7},{7,6},{8,9},{9,8},{10,11... | collective-permute-start | bytes 1179656 | tf_op jit(solution)/shard_map/ppermute | solution.py:16
  159.0 4.6 %copy-start.22 = (f32[2,8,128,128]{3,2,1,0:T(8,128)S(1)}, f32[2,8,128,128]{3,2,1,0:T(8,128)}, u32[]{:S(2)}) copy-start(f32[2,8,128,128]{3,2,1,0:T(8,128)} %copy-done.21) | copy-start | bytes 3145732
  163.6 16.7 %collective-permute-start.17 = (bf16[3,64,1024]{2,1,0:T(8,128)(2,1)S(1)}, bf16[3,64,1024]{2,1,0:T(8,128)(2,1)S(1)}, u32[]{:S(2)}, u32[]{:S(2)}) collective-permute-start(bf16[3,64,1024]{2,1,0:T(8,128)(2,1)S(1)} %get-tuple-element.43), channel_id=1, source_target_pairs={{0,1},{1,0},{2,3},{3,2},{4,5},{5,4},{6,7},{7,6},{8,9},{9,8},{10,11... | collective-permute-start | bytes 1179656 | tf_op jit(solution)/shard_map/ppermute | solution.py:16
  163.7 2.7 %copy-start.27 = (f32[2,2,4,128]{2,3,1,0:T(8,128)S(1)}, f32[2,2,4,128]{2,3,1,0:T(8,128)}, u32[]{:S(2)}) copy-start(f32[2,2,4,128]{2,3,1,0:T(8,128)} %copy.55) | copy-start | bytes 24580
  163.8 34.1 %collective-permute-start.9 = (bf16[2,8,128,128]{3,2,1,0:T(8,128)(2,1)S(1)}, bf16[2,8,128,128]{3,2,1,0:T(8,128)(2,1)S(1)}, u32[]{:S(2)}, u32[]{:S(2)}) collective-permute-start(bf16[2,8,128,128]{3,2,1,0:T(8,128)(2,1)S(1)} %get-tuple-element.105), channel_id=1, source_target_pairs={{0,2},{1,3},{2,0},{3,1},{4,6},{5,7},{6,4},{7,5},{8,10},{9,11},{10,... | collective-permute-start | bytes 1572872 | tf_op jit(solution)/shard_map/ppermute | solution.py:16
  186.2 10.4 %collective-permute-start.18 = (bf16[3,64,1024]{2,1,0:T(8,128)(2,1)S(1)}, bf16[3,64,1024]{2,1,0:T(8,128)(2,1)S(1)}, u32[]{:S(2)}, u32[]{:S(2)}) collective-permute-start(bf16[3,64,1024]{2,1,0:T(8,128)(2,1)S(1)} %get-tuple-element.50), channel_id=1, source_target_pairs={{0,1},{1,0},{2,3},{3,2},{4,5},{5,4},{6,7},{7,6},{8,9},{9,8},{10,11... | collective-permute-start | bytes 1179656 | tf_op jit(solution)/shard_map/ppermute | solution.py:16
  202.5 9.5 %collective-permute-start.19 = (bf16[3,64,1024]{2,1,0:T(8,128)(2,1)S(1)}, bf16[3,64,1024]{2,1,0:T(8,128)(2,1)S(1)}, u32[]{:S(2)}, u32[]{:S(2)}) collective-permute-start(bf16[3,64,1024]{2,1,0:T(8,128)(2,1)S(1)} %get-tuple-element.57), channel_id=1, source_target_pairs={{0,1},{1,0},{2,3},{3,2},{4,5},{5,4},{6,7},{7,6},{8,9},{9,8},{10,11... | collective-permute-start | bytes 1179656 | tf_op jit(solution)/shard_map/ppermute | solution.py:16
  (36 other events, 40.7 us)

commit v2 on v0

v2 whole, which is shorter than its diff:
```python
import functools
import math

import jax
import jax.numpy as jnp
from jax import lax
from jax.experimental import pallas as pl
from jax.experimental.pallas import tpu as pltpu
from jax.sharding import PartitionSpec as P

HEAD_DIM = 128
PART = 4
STEP = 8
VMEM = 16 * 1024 * 1024
ANY = pl.BlockSpec(memory_space=pl.ANY)
FULL = pl.BlockSpec(memory_space=pltpu.VMEM)
SCALARS = pl.BlockSpec(memory_space=pltpu.SMEM)
NN = ((1,), (0,))
NT = ((1,), (1,))
TN = ((0,), (0,))
LOW = jnp.bfloat16
COST = pl.CostEstimate(flops=1, bytes_accessed=1, transcendentals=0)
WIDE = jnp.float32


def swap(x, axis, bit):
    return lax.ppermute(x, axis, [(i, i ^ bit) for i in range(lax.axis_size(axis))])


def dot(a, b, dims):
    return lax.dot_general(a, b, (dims, ((), ())), preferred_element_type=WIDE)


def head_cols(h):
    return slice(h * HEAD_DIM, (h + 1) * HEAD_DIM)


class Order:
    def __init__(self):
        self.token = None

    def call(
        self,
        kernel,
        name,
        scalars,
        inputs,
        in_specs,
        out_shape,
        out_specs,
        grid=(),
        scratch=(),
        aliases=None,
        after=(),
        vmem=VMEM,
    ):
        extra = list(after) + ([] if self.token is None else [self.token])
        n_scalars, n_in, n_out = len(scalars), len(inputs), len(out_shape)

        def body(*refs):
            first = n_scalars + n_in
            second = first + len(extra)
            kernel(*refs[:first], *refs[second : second + n_out], *refs[second + n_out + 1 :])

        *results, self.token = pl.pallas_call(
            body,
            grid_spec=pltpu.PrefetchScalarGridSpec(
                num_scalar_prefetch=n_scalars,
                grid=grid,
                in_specs=list(in_specs) + [ANY] * len(extra),
                out_specs=list(out_specs) + [ANY],
                scratch_shapes=scratch,
            ),
            out_shape=list(out_shape) + [jax.ShapeDtypeStruct((8, 128), WIDE)],
            input_output_aliases=aliases or {},
            compiler_params=pltpu.CompilerParams(vmem_limit_bytes=vmem),
            cost_estimate=COST,
            name=name,
        )(*scalars, *inputs, *extra)
        return results


def head_states(q, k, v, g, qw, kw):
    ks = (k.astype(WIDE) * kw).astype(LOW)
    qs = (q.astype(WIDE) * qw).astype(LOW)
    return dot(ks, v, TN), dot(qs, g, TN)


def head_grads(q, k, v, g, qw, kw, cumc, cumr, bias, forward, backward):
    decay = jnp.exp(cumc - cumr + bias)
    gs = (dot(g, v, NT) * decay).astype(LOW)
    sc = (dot(q, k, NT) * decay).astype(LOW)
    dq = dot(gs, k, NN) + qw * dot(g, forward, NT)
    dk = dot(gs, q, TN) + kw * dot(v, backward, NT)
    dv = dot(sc, g, TN) + kw * dot(k, backward, NN)
    return dq.astype(LOW), dk.astype(LOW), dv.astype(LOW)


def pack(order, target, arrays, hw, after=(), vmem=60 * 1024 * 1024):
    rows = arrays[0].shape[0]
    width = hw * HEAD_DIM
    groups = target.shape[0]

    def kernel(at_ref, *refs):
        ins, out, sems = refs[:4], refs[4], refs[5]
        copies = []
        for o in range(groups):
            columns = pl.ds(pl.multiple_of(at_ref[o] * HEAD_DIM, HEAD_DIM), width)
            for a, ref in enumerate(ins):
                copies.append(
                    pltpu.make_async_copy(
                        ref.at[:, columns], out.at[o, a], sems.at[len(copies)]
                    )
                )
        for copy in copies:
            copy.start()
        for copy in copies:
            copy.wait()

    (packed,) = order.call(
        kernel,
        "pack",
        [target],
        arrays,
        [pl.BlockSpec(memory_space=pltpu.HBM)] * 4,
        [jax.ShapeDtypeStruct((groups, 4, rows, width), LOW)],
        [FULL],
        scratch=[pltpu.SemaphoreType.DMA((4 * groups,))],
        after=after,
        vmem=vmem,
    )
    return packed


def decays(order, at, logs, rows, pieces, hb):
    heads, length = logs[0].shape
    span = pieces * rows
    groups = len(logs)
    steps = heads // hb

    def kernel(at_ref, *refs):
        sources = refs[:groups]
        cumr, cumc, qw, kw, bias = refs[groups:]
        slot, upper = at_ref[0], at_ref[1]

        def position(axis):
            p = lax.broadcasted_iota(jnp.int32, (span, span), axis)
            return ((p // rows) ^ slot) * rows + p % rows

        down, along = position(0), position(1)
        bias[...] = jnp.where(down >= along, 0.0, -1e30)
        source = lax.broadcasted_iota(jnp.int32, (span, span), 0)
        upto = (source <= along).astype(WIDE)
        ones = jnp.ones((span, span), WIDE)
        for o, ref in enumerate(sources):
            rows_in = ref[...]
            if span < length:
                rows_in = jnp.where(upper == 0, rows_in[:, :span], rows_in[:, span:])

            def exact(a, b, dims):
                return lax.dot_general(
                    a,
                    b,
                    (dims, ((), ())),
                    precision=lax.Precision.HIGHEST,
                    preferred_element_type=WIDE,
                )

            line = exact(rows_in, upto, NN)
            column = exact(upto, rows_in, ((0,), (1,)))
            total = exact(ones, rows_in, NT)
            query = jnp.exp(column)
            key = jnp.exp(total - column)
            for i in range(steps):
                part = slice(i * hb, (i + 1) * hb)
                cumr[i, o] = line[part]
                cumc[i, o] = column[:, part]
                qw[i, o] = query[:, part]
                kw[i, o] = key[:, part]

    columns = jax.ShapeDtypeStruct((steps, groups, span, hb), WIDE)
    return order.call(
        kernel,
        "decays",
        [at],
        logs,
        [FULL] * groups,
        [
            jax.ShapeDtypeStruct((steps, groups, hb, span), WIDE),
            columns,
            columns,
            columns,
            jax.ShapeDtypeStruct((span, span), WIDE),
        ],
        [FULL] * 5,
    )


def states(order, pieces, decay, w0, hw, hb):
    groups, _, rows, _ = pieces[0].shape
    count = len(pieces)
    width = hb * HEAD_DIM

    def kernel(*refs):
        got = refs[:count]
        qw_ref, kw_ref, *results = refs[count:]
        for o in range(groups):
            for h in range(hb):
                c = head_cols(h)
                q, k, v, g = (
                    jnp.concatenate([r[o, a, :, c] for r in got], axis=0) for a in range(4)
                )
                pair = head_states(
                    q, k, v, g, qw_ref[0, o, :, h : h + 1], kw_ref[0, o, :, h : h + 1]
                )
                for t in range(2):
                    results[o][t, h] = pair[t].astype(results[o].dtype)

    piece = pl.BlockSpec((groups, 4, rows, width), lambda i: (0, 0, 0, i))
    weight = pl.BlockSpec((1, groups, count * rows, hb), lambda i: (w0 // hb + i, 0, 0, 0))
    shape = (2, hw, HEAD_DIM, HEAD_DIM)
    return order.call(
        kernel,
        "states",
        [],
        [*pieces, decay[2], decay[3]],
        [piece] * count + [weight] * 2,
        [jax.ShapeDtypeStruct(shape, kind) for kind in (WIDE, LOW)[:groups]],
        [pl.BlockSpec((2, hb, HEAD_DIM, HEAD_DIM), lambda i: (0, i, 0, 0))] * groups,
        grid=(hw // hb,),
    )


def step(order, table, flags, w0, hw, own, parts, around, keep=None, add=None, reach=None,
         single=False, both=False, selects=0, total=False, final=None, extras=()):
    shape = (2, hw, HEAD_DIM, HEAD_DIM)
    hs = math.gcd(hw, STEP)
    inputs = ([] if own is None else [own]) + list(parts)
    inputs += ([] if around is None else [around]) + list(extras)
    out_shape = []
    if total:
        out_shape.append(jax.ShapeDtypeStruct(shape, WIDE))
    if both:
        out_shape.append(jax.ShapeDtypeStruct(shape, LOW))
    out_shape += [jax.ShapeDtypeStruct(shape[1:], LOW)] * selects
    if reach is not None and final is None:
        out_shape.append(jax.ShapeDtypeStruct(shape, WIDE))
    if final is not None:
        out_shape += [jax.ShapeDtypeStruct(shape, LOW)] * (len(final) // 4)

    def kernel(table_ref, flags_ref, *refs):
        refs = list(refs)
        own_ref = None if own is None else refs.pop(0)
        part_refs = [refs.pop(0) for _ in parts]
        around_ref = None if around is None else refs.pop(0)
        extra_refs = [refs.pop(0) for _ in extras]

        first = w0 + pl.program_id(0) * hs

        for h in range(hs):
            out = list(refs)

            def weight(row):
                return table_ref[row, first + h]

            got = [
                [r[h].astype(WIDE)] * 2 if single else [r[t, h].astype(WIDE) for t in range(2)]
                for r in part_refs
            ]
            if keep is not None:
                sums = []
                for t in range(2):
                    value = weight(keep[t]) * own_ref[t, h]
                    for p, part in enumerate(got):
                        value = value + weight(add[p][t]) * part[t]
                    sums.append(value)
                if total:
                    ref = out.pop(0)
                    for t in range(2):
                        ref[t, h] = sums[t]
                if both:
                    ref = out.pop(0)
                    for t in range(2):
                        ref[t, h] = sums[t].astype(LOW)
                for j in range(selects):
                    ref = out.pop(0)
                    ref[h] = jnp.where(flags_ref[j] != 0, sums[1], sums[0]).astype(LOW)
            if reach is not None:
                sides = []
                for t in range(2):
                    value = None if around_ref is None else around_ref[t, h]
                    for p, part in enumerate(got):
                        term = weight(reach[p][t]) * part[t]
                        value = term if value is None else value + term
                    sides.append(value)
                if final is None:
                    ref = out.pop(0)
                    for t in range(2):
                        ref[t, h] = sides[t]
                else:
                    for i, ref in enumerate(out):
                        for t in range(2):
                            value = sides[t]
                            if extra_refs:
                                a, b = final[4 * i + 2 * t : 4 * i + 2 * t + 2]
                                value = weight(a) * value + weight(b) * extra_refs[i][
                                    t, h
                                ].astype(WIDE)
                            ref[t, h] = value.astype(LOW)

    def block(x):
        if len(x.shape) == 3:
            return pl.BlockSpec((hs, HEAD_DIM, HEAD_DIM), lambda i, *_: (i, 0, 0))
        return pl.BlockSpec((2, hs, HEAD_DIM, HEAD_DIM), lambda i, *_: (0, i, 0, 0))

    return order.call(
        kernel,
        "step",
        [table, flags],
        inputs,
        [block(x) for x in inputs],
        out_shape,
        [block(x) for x in out_shape],
        grid=(hw // hs,),
    )


def grads(order, cols, pieces, group, decay, st, outs, full, w0, hw, hb):
    _, _, rows, _ = pieces[0].shape
    count = len(pieces)
    span = count * rows
    width = hb * HEAD_DIM
    aliased = outs is not None
    cumr, cumc, qw, kw, bias = decay
    n_in = count + 6

    def kernel(cols_ref, *refs):
        got = refs[:count]
        qw_ref, kw_ref, cumc_ref, cumr_ref, bias_ref, st_ref = refs[count:n_in]
        results = refs[n_in + (3 if aliased else 0) :]
        kept, sends = results[:3], results[3:]
        for h in range(hb):
            c = head_cols(h)
            q, k, v, g = (
                jnp.concatenate([r[0, a, :, c] for r in got], axis=0) for a in range(4)
            )
            at = (0, 0, slice(None), slice(h, h + 1))
            outputs = head_grads(
                q, k, v, g, qw_ref[at], kw_ref[at], cumc_ref[at],
                cumr_ref[0, 0, h : h + 1, :], bias_ref[...], st_ref[0, h], st_ref[1, h],
            )
            for a, result in enumerate(outputs):
                kept[a][:, c] = result[:rows]
                for m, send in enumerate(sends):
                    send[a, :, c] = result[(m + 1) * rows : (m + 2) * rows]

    piece = pl.BlockSpec((1, 4, rows, width), lambda i, c: (group, 0, 0, i))
    column = pl.BlockSpec((1, 1, span, hb), lambda i, c: (w0 // hb + i, group, 0, 0))
    row = pl.BlockSpec((1, 1, hb, span), lambda i, c: (w0 // hb + i, group, 0, 0))
    whole = pl.BlockSpec((span, span), lambda i, c: (0, 0))
    state_block = pl.BlockSpec((2, hb, HEAD_DIM, HEAD_DIM), lambda i, c: (0, i, 0, 0))
    results = order.call(
        kernel,
        "grads",
        [cols],
        [*pieces, qw, kw, cumc, cumr, bias, st] + (list(outs) if aliased else []),
        [piece] * count
        + [column] * 3
        + [row, whole, state_block]
        + ([ANY] * 3 if aliased else []),
        [jax.ShapeDtypeStruct((rows, full), LOW)] * 3
        + [jax.ShapeDtypeStruct((3, rows, hw * HEAD_DIM), LOW)] * (count - 1),
        [pl.BlockSpec((rows, width), lambda i, c: (0, c[group] + i))] * 3
        + [pl.BlockSpec((3, rows, width), lambda i, c: (0, 0, i))] * (count - 1),
        grid=(hw // hb,),
        aliases={1 + n_in + a: a for a in range(3)} if aliased else {},
    )
    return (results[:3], results[3:])


def place(order, ats, parts, outs):
    rows, full = outs[0].shape
    count = len(parts)

    def kernel(at_ref, *refs):
        ins, results = refs[:count], refs[count + 3 : count + 6]
        buffers, sems = refs[count + 6 : -1], refs[-1]
        loads, stores = [], []
        for p, ref in enumerate(ins):
            columns = pl.ds(pl.multiple_of(at_ref[p] * HEAD_DIM, HEAD_DIM), ref.shape[2])
            loads.append(pltpu.make_async_copy(ref, buffers[p], sems.at[4 * p + 3]))
            for a in range(3):
                stores.append(
                    pltpu.make_async_copy(
                        buffers[p].at[a], results[a].at[:, columns], sems.at[4 * p + a]
                    )
                )
        for load in loads:
            load.start()
        for p, load in enumerate(loads):
            load.wait()
            for store in stores[3 * p : 3 * p + 3]:
                store.start()
        for store in stores:
            store.wait()

    return order.call(
        kernel,
        "place",
        [jnp.stack(ats)],
        [*parts, *outs],
        [ANY] * (count + 3),
        [jax.ShapeDtypeStruct((rows, full), LOW)] * 3,
        [ANY] * 3,
        scratch=[pltpu.VMEM(p.shape, LOW) for p in parts]
        + [pltpu.SemaphoreType.DMA((4 * count,))],
        aliases={1 + count + a: a for a in range(3)},
    )


class Table:
    def __init__(self, log_decay, low):
        self.peers = lax.axis_size("seq")
        self.me = lax.axis_index("seq")
        sums = jnp.sum(log_decay.reshape(log_decay.shape[0], 2, -1), axis=2)
        self.lo, self.hi, self.on, self.gate = [], [], [], []
        self.sums = sums
        every = (sums[:, 0] + sums[:, 1])[None]
        bit = 1
        while bit < self.peers:
            other = swap(every, "seq", bit)
            late = (self.me & bit) != 0
            every = jnp.where(
                late,
                jnp.concatenate([other, every], axis=0),
                jnp.concatenate([every, other], axis=0),
            )
            bit *= 2
        self.every = jnp.concatenate([every, sums.T], axis=0)

    def row(self, a, b, on=True):
        self.lo.append(jnp.asarray(a, jnp.int32))
        self.hi.append(jnp.asarray(b, jnp.int32))
        self.on.append(jnp.asarray(on, jnp.bool_))
        return len(self.lo) - 1

    def one_if(self, on):
        return self.row(0, 0, on)

    def half_if(self, which, use):
        at = self.peers + which
        return self.row(jnp.where(use, at, 0), jnp.where(use, at + 1, 0))

    def build(self):
        index = jnp.arange(self.peers + 2)[None, :]
        inside = (index >= jnp.stack(self.lo)[:, None]) & (index < jnp.stack(self.hi)[:, None])
        total = jnp.sum(jnp.where(inside[:, :, None], self.every[None], 0.0), axis=1)
        return jnp.where(jnp.stack(self.on)[:, None], jnp.exp(total), 0.0)


def seq_levels(table):
    bits = table.peers.bit_length() - 1
    me = table.me
    levels = []
    base = 0
    while base < bits:
        nb = min(1 if base == 0 else 2, bits - base)
        size = 1 << base
        start = me - me % size
        above = me - me % (size << nb)
        end = above + (size << nb)
        last = base + nb == bits
        level = dict(base=base, nb=nb, last=last, reach=[], add=[], keep=None)
        if not last:
            level["keep"] = (table.row(start + size, end), table.row(above, start))
        for p in range(1, 1 << nb):
            other = start ^ (p << base)
            level["reach"].append(
                (
                    table.row(other + size, me, other < start),
                    table.row(me + 1, other, other > start),
                )
            )
            if not last:
                level["add"].append((table.row(other + size, end), table.row(above, other)))
        levels.append(level)
        base += nb
    return levels


class Wave:
    def __init__(self, env, mode, w0, hw):
        self.env, self.mode, self.w0, self.hw = env, mode, w0, hw
        self.peers = range(1, env.n // 2 if mode == "P" else env.n)
        self.parts = []

    def columns(self, device):
        at = [device, device ^ (self.env.n // 2)] if self.mode == "P" else [device]
        return (jnp.stack(at) * self.env.heads + self.w0).astype(jnp.int32)

    def pack(self):
        e = self.env
        self.received = [None] * len(self.peers)
        for m in sorted(self.peers, reverse=True):
            packed = pack(e.order, self.columns(e.z ^ m), e.arrays, self.hw, e.after)
            self.received[m - 1] = swap(packed, "head", m)

    def keep(self):
        e = self.env
        self.kept = pack(e.order, self.columns(e.z), e.arrays, self.hw, vmem=VMEM)
        self.pieces = [self.kept] + self.received

    def states(self):
        e = self.env
        self.decay = e.decay[self.mode]
        self.level = 0
        self.around = None
        self.own, *send = states(e.order, self.pieces, self.decay, self.w0, self.hw, e.hb)
        if send:
            self.theirs = swap(send[0], "head", e.n // 2)

    def begin(self):
        e = self.env
        levels = e.levels
        if not levels:
            return
        level = levels[0]
        result = step(
            e.order, e.table, e.flags, self.w0, self.hw, self.own,
            [self.theirs] if self.mode == "P" else [], None,
            keep=e.comb[0] if self.mode == "P" else e.ones,
            add=[e.comb[1]] if self.mode == "P" else [],
            total=not level["last"], both=not level["last"],
            selects=level["nb"] if level["last"] else 0,
        )
        self.exchange(result, level)

    def exchange(self, result, level):
        if level["last"]:
            sends = result
        else:
            self.total = result[0]
            sends = [result[1]]
        self.got = []
        for p in range(1, 1 << level["nb"]):
            send = sends[p.bit_length() - 1] if level["last"] else sends[0]
            self.got.append(swap(send, "seq", p << level["base"]))

    def advance(self):
        e = self.env
        level, after = e.levels[self.level], e.levels[self.level + 1]
        result = step(
            e.order, e.table, e.flags, self.w0, self.hw, self.total, self.got, self.around,
            keep=level["keep"], add=level["add"], reach=level["reach"],
            total=not after["last"], both=not after["last"],
            selects=after["nb"] if after["last"] else 0,
        )
        self.around = result.pop()
        self.level += 1
        self.exchange(result, after)

    def finish(self):
        e = self.env
        level = e.levels[-1] if e.levels else None
        zero = jnp.zeros((2, self.hw, HEAD_DIM, HEAD_DIM), WIDE)
        result = step(
            e.order, e.table, e.flags, self.w0, self.hw, None,
            self.got if level else [], self.around if level and len(e.levels) > 1 else zero,
            reach=level["reach"] if level else [], single=True,
            final=e.final if self.mode == "P" else e.ones * 2,
            extras=[self.theirs, self.own] if self.mode == "P" else [],
        )
        self.own_states = result[0]
        if self.mode == "P":
            self.mirror_states = swap(result[1], "head", e.n // 2)

    def touch(self):
        self.env.order.call(lambda *refs: None, "touch", [], [self.mirror_states], [ANY], [], [])

    def grads(self, group):
        e = self.env
        st = self.mirror_states if group else self.own_states
        e.outs, sends = grads(
            e.order, self.columns(e.z) // e.hb, self.pieces, group, self.decay, st, e.outs,
            e.arrays[0].shape[1], self.w0, self.hw, e.hb,
        )
        for m in sorted(self.peers, reverse=True):
            at = self.columns(e.z ^ m)[group]
            self.parts.append((at, swap(sends[m - 1], "head", m)))

    def place(self):
        e = self.env
        if self.parts:
            e.outs = place(
                e.order, [t[0] for t in self.parts], [t[1] for t in self.parts], e.outs
            )
            self.parts = []


class Env:
    pass


def local(queries, key_rows, value_rows, out_grad, log_decay):
    e = Env()
    e.arrays = (queries, key_rows, value_rows, out_grad)
    rows = queries.shape[0]
    e.heads = heads = log_decay.shape[0]
    e.hb = math.gcd(heads, PART)
    e.n = n = lax.axis_size("head")
    e.z = z = lax.axis_index("head")
    e.order = Order()
    e.outs = None
    e.decay = {}
    e.after = ()
    half = n // 2
    low = z < half

    def prepare(modes):
        table = Table(log_decay, low)
        e.levels = seq_levels(table)
        e.ones = (table.one_if(True),) * 2
        e.comb = (
            (table.half_if(1, low), table.half_if(0, ~low)),
            (table.half_if(1, ~low), table.half_if(0, low)),
        )
        off, on = table.one_if(~low), table.one_if(low)
        e.final = (
            table.half_if(0, ~low), off, table.half_if(1, low), on,
            table.half_if(0, low), on, table.half_if(1, ~low), off,
        )
        e.table = table.build()
        e.after = (e.table,)
        top = e.levels[-1] if e.levels else dict(base=0, nb=1)
        e.flags = jnp.stack(
            [(table.me >> (top["base"] + j)) & 1 for j in range(top["nb"])]
        ).astype(jnp.int32)
        if "P" in modes:
            at = jnp.stack([z % half, z // half]).astype(jnp.int32)
            mirror = swap(log_decay, "head", half)
            e.decay["P"] = decays(e.order, at, [log_decay, mirror], rows, half, e.hb)
        if "X" in modes:
            at = jnp.stack([z, z * 0]).astype(jnp.int32)
            e.decay["X"] = decays(e.order, at, [log_decay], rows, n, e.hb)

    schedule(e, heads, prepare)
    return tuple(e.outs)


WAVES = ("P8", "P8")
STEPS = ("pa", "pb", "x", "ka", "sa", "kb", "sb", "ba", "va", "fa", "bb", "vb", "ga", "ta", "fb", "gb", "ha", "hb", "la", "lb")


def schedule(e, heads, prepare):
    sizes, steps = WAVES, STEPS
    if heads % 16:
        sizes, steps = ("P16",), ("pa", "x", "ka", "sa", "ba", "va", "fa", "ga", "ha", "la")
    waves, w0 = {}, 0
    for name, size in zip("abcdef", sizes):
        hw = int(size[1:]) * heads // 16
        waves[name] = Wave(e, size[0], w0, hw)
        w0 += hw
    for code in steps:
        if code == "x":
            prepare({size[0] for size in sizes})
            continue
        wave = waves[code[1]]
        if code[0] == "p":
            wave.pack()
        elif code[0] == "k":
            wave.keep()
        elif code[0] == "s":
            wave.states()
        elif code[0] == "b":
            wave.begin()
        elif code[0] == "v":
            for _ in e.levels[1:]:
                wave.advance()
        elif code[0] == "f":
            wave.finish()
        elif code[0] == "g":
            wave.grads(0)
        elif code[0] == "h":
            wave.grads(1)
        elif code[0] == "l":
            wave.place()
        elif code[0] == "t":
            wave.touch()


def solution(mesh):
    rows = P(("seq", "head"), None)
    return jax.shard_map(
        local,
        mesh=mesh,
        in_specs=(rows, rows, rows, rows, P("head", "seq")),
        out_specs=(rows, rows, rows),
        check_vma=False,
    )
```

time: 278 us -> 177 us (0.64)
  waiting for transfers between devices: 152 us -> 98.9 us
  Pallas kernels: 0 us -> 45.6 us
  matrix products: 23.3 us -> 0 us
  other arithmetic: 24.5 us -> 1.37 us
  local copies, waits for them, and re-layouts: 23.9 us -> 8.5 us
  between operations: 14.4 us -> 0.93 us
  blocking collectives: 8.76 us -> 0 us
  starting transfers between devices: 29.5 us -> 21.1 us
    all_to_all x7 -> x0, waiting for transfers between devices: 139 us -> none  [the longest x1 24.9 us: local(): lax.all_to_all(value_rows, 'head', split_axis=1, concat_axis=0, tiled=True)]
    ppermute x0 -> x22, waiting for transfers between devices: none -> 98.9 us  [swap(): lax.ppermute(x, axis, [(i, i ^ bit) for i in range(lax.axis_size(axis))])]
    pallas_call x0 -> x20, Pallas kernels: none -> 45.6 us  [call(): pl.pallas_call(body, grid_spec=pltpu.PrefetchScalarGridSpec(num_scalar_pr...]
    all_to_all x7 -> x0, starting transfers between devices: 29.4 us -> none  [the longest x1 6.32 us: local(): lax.all_to_all(out_grad, 'head', split_axis=1, concat_axis=0, tiled=True)]
    select_n x16 -> x5, other arithmetic: 23.7 us -> 0.18 us  [the longest x1 0.08 us: grads(): self.columns(e.z) // e.hb]
    dot_general x9 -> x0, matrix products: 23.3 us -> none  [the longest x1 5.16 us: local(): jnp.einsum('nhts,nhtj->nhsj', scores, grad_heads, preferred_element_type=...]
    ppermute x0 -> x22, starting transfers between devices: none -> 21.1 us  [swap(): lax.ppermute(x, axis, [(i, i ^ bit) for i in range(lax.axis_size(axis))])]
    all_to_all x10 -> x0, local copies, waits for them, and re-layouts: 16.2 us -> none  [the longest x2 4.75 us: local(): lax.all_to_all(query_grad, 'head', split_axis=0, concat_axis=1, tiled=True)]
  transfers between devices with their start and end apart: 9 -> 22, of which waited for: 7 -> 13; matrix products, arithmetic and copies ran while one was open for 21% -> 1% of each run, Pallas kernels for 0% -> 22%
where the time goes in v2:
time: 177 us; the launch traced here: 176 us
  waiting for transfers between devices  98.9 us (56%)
  Pallas kernels  45.6 us (26%)
  starting transfers between devices  21.1 us (12%)
  local copies, waits for them, and re-layouts  8.5 us (5%)
    ppermute x22, waiting for transfers between devices, swap(): lax.ppermute(x, axis, [(i, i ^ bit) for i in range(lax.axis_size(axis))])  98.9 us
    pallas_call x20, Pallas kernels, call(): pl.pallas_call(body, grid_spec=pltpu.PrefetchScalarGridSpec(num_scalar_pr...  45.6 us
    ppermute x22, starting transfers between devices, swap(): lax.ppermute(x, axis, [(i, i ^ bit) for i in range(lax.axis_size(axis))])  21.1 us
    unnamed x32, local copies, waits for them, and re-layouts  7.99 us
  transfers between devices with their start and end apart: 22, of which 13 were waited for; matrix products, arithmetic and copies ran while one was open for 1% of the time, Pallas kernels for 22%

profile of v2, /device:TPU:0, one launch (start us, length us, event | category | flops | bytes accessed | tf_op | source)
XLA Modules:
  0.0 176.4 jit_solution(6603185769573760501)
XLA Ops:
  0.6 4.1 %collective-permute-start = (f32[16,256]{1,0:T(8,128)}, f32[16,256]{1,0:T(8,128)S(1)}, u32[]{:S(2)}, u32[]{:S(2)}) collective-permute-start(f32[16,256]{1,0:T(8,128)} %refs_1_.7), channel_id=1, source_target_pairs={{0,2},{1,3},{2,0},{3,1},{4,6},{5,7},{6,4},{7,5},{8,10},{9,11},{10,... | collective-permute-start | bytes 49160 | tf_op jit(solution)/shard_map/ppermute | solution.py:27
  5.4 3.1 %pack.4 = (bf16[2,4,64,1024]{3,2,1,0:T(8,128)(2,1)}, f32[8,128]{1,0:T(8,128)}) custom-call(s32[2]{0:T(128)} %get-tuple-element.140.refs_0_, bf16[64,8192]{1,0:T(8,128)(2,1)} %refs_1_.9, bf16[64,8192]{1,0:T(8,128)(2,1)} %refs_2_.7, bf16[64,8192]{1,0:T(8,128)(2,1)} %refs_3_.7, bf16[64,8192]{1,0:T(8,128)(2,1)} %refs_4_.7), custom_call_target="tpu_custom_call" | custom-call | flops 1 | bytes 1 | tf_op jit(solution)/shard_map/pack/pallas_call | solution.py:65
  8.5 1.6 collective-permute-start.1
  10.6 3.1 %pack.5 = (bf16[2,4,64,1024]{3,2,1,0:T(8,128)(2,1)}, f32[8,128]{1,0:T(8,128)}) custom-call(s32[2]{0:T(128)} %get-tuple-element.139.refs_0_, bf16[64,8192]{1,0:T(8,128)(2,1)} %refs_1_.9, bf16[64,8192]{1,0:T(8,128)(2,1)} %refs_2_.7, bf16[64,8192]{1,0:T(8,128)(2,1)} %refs_3_.7, bf16[64,8192]{1,0:T(8,128)(2,1)} %refs_4_.7, f32[8,128]{1,0:T(8,128)} %get-tuple-element.70.refs_5_), custom_call_target="tpu_custom_call" | custom-call | flops 1 | bytes 1 | tf_op jit(solution)/shard_map/pack/pallas_call | solution.py:65
  14.8 1.6 collective-permute-start.4
  16.5 1.9 %collective-permute-done.4 = f32[2,16]{1,0:T(2,128)S(1)} collective-permute-done((f32[2,16]{1,0:T(2,128)S(1)}, f32[2,16]{1,0:T(2,128)S(1)}, u32[]{:S(2)}, u32[]{:S(2)}) %collective-permute-start.4) | collective-permute-done | bytes 160 | tf_op jit(solution)/shard_map/ppermute | solution.py:27
  18.4 1.6 collective-permute-start.5
  25.4 9.6 %collective-permute-done.1.refs_1_.refs_2_ = bf16[2,4,64,1024]{3,2,1,0:T(8,128)(2,1)} collective-permute-done((bf16[2,4,64,1024]{3,2,1,0:T(8,128)(2,1)}, bf16[2,4,64,1024]{3,2,1,0:T(8,128)(2,1)}, u32[]{:S(2)}, u32[]{:S(2)}) %collective-permute-start.1) | collective-permute-done | bytes 1048608 | tf_op jit(solution)/shard_map/ppermute | solution.py:27
  35.0 3.5 %states.2 = (f32[2,8,128,128]{3,2,1,0:T(8,128)S(1)}, bf16[2,8,128,128]{3,2,1,0:T(8,128)(2,1)}, f32[8,128]{1,0:T(8,128)S(1)}) custom-call(bf16[2,4,64,1024]{3,2,1,0:T(8,128)(2,1)S(1)} %get-tuple-element.73.refs_0_.refs_1_, bf16[2,4,64,1024]{3,2,1,0:T(8,128)(2,1)} %collective-permute-done.1.refs_1_.refs_2_, ...), custom_call_target="tpu_custom_call" | custom-call | flops 1 | bytes 1 | tf_op jit(solution)/shard_map/states/pallas_call | solution.py:65
  43.1 24.2 %collective-permute-done.2.refs_1_.refs_2_ = bf16[2,4,64,1024]{3,2,1,0:T(8,128)(2,1)} collective-permute-done((bf16[2,4,64,1024]{3,2,1,0:T(8,128)(2,1)}, bf16[2,4,64,1024]{3,2,1,0:T(8,128)(2,1)}, u32[]{:S(2)}, u32[]{:S(2)}) %collective-permute-start.2) | collective-permute-done | bytes 1048608 | tf_op jit(solution)/shard_map/ppermute | solution.py:27
  67.2 3.0 %states.3 = (f32[2,8,128,128]{3,2,1,0:T(8,128)S(1)}, bf16[2,8,128,128]{3,2,1,0:T(8,128)(2,1)S(1)}, f32[8,128]{1,0:T(8,128)S(1)}) custom-call(bf16[2,4,64,1024]{3,2,1,0:T(8,128)(2,1)S(1)} %get-tuple-element.79.refs_0_.refs_1_, bf16[2,4,64,1024]{3,2,1,0:T(8,128)(2,1)} %collective-permute-done.2.refs_1_.refs_2_, ...), custom_call_target="tpu_custom_call" | custom-call | flops 1 | bytes 1 | tf_op jit(solution)/shard_map/states/pallas_call | solution.py:65
  70.2 2.0 %step.6 = (f32[2,8,128,128]{3,2,1,0:T(8,128)S(1)}, bf16[2,8,128,128]{3,2,1,0:T(8,128)(2,1)S(1)}, f32[8,128]{1,0:T(8,128)S(1)}) custom-call(f32[23,16]{1,0:T(8,128)S(1)} %exponential_select_fusion.refs_0_, s32[2]{0:T(128)S(1)} %pad_add_fusion.1.refs_1_, f32[2,8,128,128]{3,2,1,0:T(8,128)S(1)} %copy-done.11, ...), custom_call_target="tpu_custom_call" | custom-call | flops 1 | bytes 1 | tf_op jit(solution)/shard_map/step/pallas_call | solution.py:65
  72.4 1.8 %collective-permute-done.8.refs_3_ = bf16[2,8,128,128]{3,2,1,0:T(8,128)(2,1)S(1)} collective-permute-done((bf16[2,8,128,128]{3,2,1,0:T(8,128)(2,1)S(1)}, bf16[2,8,128,128]{3,2,1,0:T(8,128)(2,1)S(1)}, u32[]{:S(2)}, u32[]{:S(2)}) %collective-permute-start.8) | collective-permute-done | bytes 524320 | tf_op jit(solution)/shard_map/ppermute | solution.py:27
  75.2 1.6 collective-permute-start.9
  78.7 5.7 %collective-permute-done.9.refs_2_ = bf16[8,128,128]{2,1,0:T(8,128)(2,1)S(1)} collective-permute-done((bf16[8,128,128]{2,1,0:T(8,128)(2,1)S(1)}, bf16[8,128,128]{2,1,0:T(8,128)(2,1)S(1)}, u32[]{:S(2)}, u32[]{:S(2)}) %collective-permute-start.9) | collective-permute-done | bytes 262176 | tf_op jit(solution)/shard_map/ppermute | solution.py:27
  84.4 5.9 %collective-permute-done.11.refs_4_ = bf16[8,128,128]{2,1,0:T(8,128)(2,1)S(1)} collective-permute-done((bf16[8,128,128]{2,1,0:T(8,128)(2,1)S(1)}, bf16[8,128,128]{2,1,0:T(8,128)(2,1)S(1)}, u32[]{:S(2)}, u32[]{:S(2)}) %collective-permute-start.11) | collective-permute-done | bytes 262176 | tf_op jit(solution)/shard_map/ppermute | solution.py:27
  91.6 2.4 %step.8 = (bf16[2,8,128,128]{3,2,1,0:T(8,128)(2,1)S(1)}, bf16[2,8,128,128]{3,2,1,0:T(8,128)(2,1)S(1)}, f32[8,128]{1,0:T(8,128)S(1)}) custom-call(f32[23,16]{1,0:T(8,128)S(1)} %exponential_select_fusion.refs_0_, s32[2]{0:T(128)S(1)} %pad_add_fusion.1.refs_1_, bf16[8,128,128]{2,1,0:T(8,128)(2,1)S(1)} %collective-permute-done.9.refs_2_, ...), custom_call_target="tpu_custom_call" | custom-call | flops 1 | bytes 1 | tf_op jit(solution)/shard_map/step/pallas_call | solution.py:65
  94.0 3.7 %collective-permute-done.6.refs_3_.refs_6_ = bf16[2,8,128,128]{3,2,1,0:T(8,128)(2,1)S(1)} collective-permute-done((bf16[2,8,128,128]{3,2,1,0:T(8,128)(2,1)S(1)}, bf16[2,8,128,128]{3,2,1,0:T(8,128)(2,1)S(1)}, u32[]{:S(2)}, u32[]{:S(2)}) %collective-permute-start.6) | collective-permute-done | bytes 524320 | tf_op jit(solution)/shard_map/ppermute | solution.py:27
  98.8 1.8 %collective-permute-done.12.refs_3_ = bf16[2,8,128,128]{3,2,1,0:T(8,128)(2,1)S(1)} collective-permute-done((bf16[2,8,128,128]{3,2,1,0:T(8,128)(2,1)S(1)}, bf16[2,8,128,128]{3,2,1,0:T(8,128)(2,1)S(1)}, u32[]{:S(2)}, u32[]{:S(2)}) %collective-permute-start.12) | collective-permute-done | bytes 524320 | tf_op jit(solution)/shard_map/ppermute | solution.py:27
  101.6 1.6 collective-permute-start.13
  105.2 4.4 %grads.4 = (bf16[64,8192]{1,0:T(8,128)(2,1)}, bf16[64,8192]{1,0:T(8,128)(2,1)}, bf16[64,8192]{1,0:T(8,128)(2,1)}, bf16[3,64,1024]{2,1,0:T(8,128)(2,1)S(1)}, f32[8,128]{1,0:T(8,128)S(1)}) custom-call(s32[2]{0:T(128)S(1)} %get-tuple-element.137.refs_0_, bf16[2,4,64,1024]{3,2,1,0:T(8,128)(2,1)S(1)} %copy-done.7, ...), custom_call_target="tpu_custom_call" | custom-call | flops 1 | bytes 1 | tf_op jit(solution)/shard_map/grads/pallas_call | solution.py:65
  109.6 15.1 %collective-permute-done.16.refs_0_.refs_8_ = bf16[2,8,128,128]{3,2,1,0:T(8,128)(2,1)S(1)} collective-permute-done((bf16[2,8,128,128]{3,2,1,0:T(8,128)(2,1)S(1)}, bf16[2,8,128,128]{3,2,1,0:T(8,128)(2,1)S(1)}, u32[]{:S(2)}, u32[]{:S(2)}) %collective-permute-start.16) | collective-permute-done | bytes 524320 | tf_op jit(solution)/shard_map/ppermute | solution.py:27
  126.2 2.2 %collective-permute-start.20 = (bf16[3,64,1024]{2,1,0:T(8,128)(2,1)S(1)}, bf16[3,64,1024]{2,1,0:T(8,128)(2,1)S(1)}, u32[]{:S(2)}, u32[]{:S(2)}) collective-permute-start(bf16[3,64,1024]{2,1,0:T(8,128)(2,1)S(1)} %get-tuple-element.124), channel_id=1, source_target_pairs={{0,1},{1,0},{2,3},{3,2},{4,5},{5,4},{6,7},{7,6},{8,9},{9,8},{10,11... | collective-permute-start | bytes 1179656 | tf_op jit(solution)/shard_map/ppermute | solution.py:27
  128.4 4.4 %grads.5 = (bf16[64,8192]{1,0:T(8,128)(2,1)}, bf16[64,8192]{1,0:T(8,128)(2,1)}, bf16[64,8192]{1,0:T(8,128)(2,1)}, bf16[3,64,1024]{2,1,0:T(8,128)(2,1)S(1)}, f32[8,128]{1,0:T(8,128)S(1)}) custom-call(s32[2]{0:T(128)S(1)} %get-tuple-element.142.refs_0_, ...), custom_call_target="tpu_custom_call", output_to_operand_aliasing={{0}: (9, {}), {1}: (10, {}), {2}: (11, {})} | custom-call | flops 1 | bytes 1 | tf_op jit(solution)/shard_map/grads/pallas_call | solution.py:65
  132.8 4.4 %grads.6 = (bf16[64,8192]{1,0:T(8,128)(2,1)}, bf16[64,8192]{1,0:T(8,128)(2,1)}, bf16[64,8192]{1,0:T(8,128)(2,1)}, bf16[3,64,1024]{2,1,0:T(8,128)(2,1)S(1)}, f32[8,128]{1,0:T(8,128)S(1)}) custom-call(s32[2]{0:T(128)S(1)} %get-tuple-element.137.refs_0_, ...), custom_call_target="tpu_custom_call", output_to_operand_aliasing={{0}: (9, {}), {1}: (10, {}), {2}: (11, {})} | custom-call | flops 1 | bytes 1 | tf_op jit(solution)/shard_map/grads/pallas_call | solution.py:65
  137.2 2.0 %collective-permute-start.21 = (bf16[3,64,1024]{2,1,0:T(8,128)(2,1)S(1)}, bf16[3,64,1024]{2,1,0:T(8,128)(2,1)S(1)}, u32[]{:S(2)}, u32[]{:S(2)}) collective-permute-start(bf16[3,64,1024]{2,1,0:T(8,128)(2,1)S(1)} %get-tuple-element.125), channel_id=1, source_target_pairs={{0,1},{1,0},{2,3},{3,2},{4,5},{5,4},{6,7},{7,6},{8,9},{9,8},{10,11... | collective-permute-start | bytes 1179656 | tf_op jit(solution)/shard_map/ppermute | solution.py:27
  139.2 12.1 %collective-permute-done.18.refs_8_ = bf16[2,8,128,128]{3,2,1,0:T(8,128)(2,1)S(1)} collective-permute-done((bf16[2,8,128,128]{3,2,1,0:T(8,128)(2,1)S(1)}, bf16[2,8,128,128]{3,2,1,0:T(8,128)(2,1)S(1)}, u32[]{:S(2)}, u32[]{:S(2)}) %collective-permute-start.18) | collective-permute-done | bytes 524320 | tf_op jit(solution)/shard_map/ppermute | solution.py:27
  151.3 4.4 %grads.7 = (bf16[64,8192]{1,0:T(8,128)(2,1)}, bf16[64,8192]{1,0:T(8,128)(2,1)}, bf16[64,8192]{1,0:T(8,128)(2,1)}, bf16[3,64,1024]{2,1,0:T(8,128)(2,1)S(1)}, f32[8,128]{1,0:T(8,128)S(1)}) custom-call(s32[2]{0:T(128)S(1)} %get-tuple-element.142.refs_0_, ...), custom_call_target="tpu_custom_call", output_to_operand_aliasing={{0}: (9, {}), {1}: (10, {}), {2}: (11, {})} | custom-call | flops 1 | bytes 1 | tf_op jit(solution)/shard_map/grads/pallas_call | solution.py:65
  155.7 10.7 %collective-permute-done.21.refs_2_ = bf16[3,64,1024]{2,1,0:T(8,128)(2,1)S(1)} collective-permute-done((bf16[3,64,1024]{2,1,0:T(8,128)(2,1)S(1)}, bf16[3,64,1024]{2,1,0:T(8,128)(2,1)S(1)}, u32[]{:S(2)}, u32[]{:S(2)}) %collective-permute-start.21) | collective-permute-done | bytes 393248 | tf_op jit(solution)/shard_map/ppermute | solution.py:27
  167.0 1.9 %place.2 = (bf16[64,8192]{1,0:T(8,128)(2,1)}, bf16[64,8192]{1,0:T(8,128)(2,1)}, bf16[64,8192]{1,0:T(8,128)(2,1)}, f32[8,128]{1,0:T(8,128)S(1)}) custom-call(s32[2]{0:T(128)S(1)} %copy-done.14, bf16[3,64,1024]{2,1,0:T(8,128)(2,1)S(1)} %collective-permute-done.20.refs_1_, ...), custom_call_target="tpu_custom_call", output_to_operand_aliasing={{0}: (3, {}), {1}: (4, {}), {2}: (5, {})} | custom-call | flops 1 | bytes 1 | tf_op jit(solution)/shard_map/place/pallas_call | solution.py:65
  168.9 5.0 %collective-permute-done.19.refs_2_ = bf16[3,64,1024]{2,1,0:T(8,128)(2,1)S(1)} collective-permute-done((bf16[3,64,1024]{2,1,0:T(8,128)(2,1)S(1)}, bf16[3,64,1024]{2,1,0:T(8,128)(2,1)S(1)}, u32[]{:S(2)}, u32[]{:S(2)}) %collective-permute-start.19) | collective-permute-done | bytes 393248 | tf_op jit(solution)/shard_map/ppermute | solution.py:27
  174.6 1.9 %place.3 = (bf16[64,8192]{1,0:T(8,128)(2,1)}, bf16[64,8192]{1,0:T(8,128)(2,1)}, bf16[64,8192]{1,0:T(8,128)(2,1)}, f32[8,128]{1,0:T(8,128)}) custom-call(s32[2]{0:T(128)S(1)} %copy-done.13, bf16[3,64,1024]{2,1,0:T(8,128)(2,1)S(1)} %collective-permute-done.17.refs_1_, ...), custom_call_target="tpu_custom_call", output_to_operand_aliasing={{0}: (3, {}), {1}: (4, {}), {2}: (5, {})} | custom-call | flops 1 | bytes 1 | tf_op jit(solution)/shard_map/place/pallas_call | solution.py:65
  (87 shorter events, 23.3 us)
Async XLA Ops:
  0.6 19.4 %collective-permute-start = (f32[16,256]{1,0:T(8,128)}, f32[16,256]{1,0:T(8,128)S(1)}, u32[]{:S(2)}, u32[]{:S(2)}) collective-permute-start(f32[16,256]{1,0:T(8,128)} %refs_1_.7), channel_id=1, source_target_pairs={{0,2},{1,3},{2,0},{3,1},{4,6},{5,7},{6,4},{7,5},{8,10},{9,11},{10,... | collective-permute-start | bytes 49160 | tf_op jit(solution)/shard_map/ppermute | solution.py:27
  5.4 4.8 %copy-start.12 = (f32[16,256]{1,0:T(8,128)S(1)}, f32[16,256]{1,0:T(8,128)}, u32[]{:S(2)}) copy-start(f32[16,256]{1,0:T(8,128)} %refs_1_.7) | copy-start | bytes 49156
  8.5 26.5 %collective-permute-start.1 = (bf16[2,4,64,1024]{3,2,1,0:T(8,128)(2,1)}, bf16[2,4,64,1024]{3,2,1,0:T(8,128)(2,1)}, u32[]{:S(2)}, u32[]{:S(2)}) collective-permute-start(bf16[2,4,64,1024]{3,2,1,0:T(8,128)(2,1)} %get-tuple-element.74), channel_id=1, source_target_pairs={{0,1},{1,0},{2,3},{3,2},{4,5},{5,4},{6,7},{7,6},{8,9},{9,8},{10,11... | collective-permute-start | bytes 3145736 | tf_op jit(solution)/shard_map/ppermute | solution.py:27
  10.5 4.3 %collective-permute-start.3 = (f32[1,16]{1,0:T(1,128)S(1)}, f32[1,16]{1,0:T(1,128)S(1)}, u32[]{:S(2)}, u32[]{:S(2)}) collective-permute-start(f32[1,16]{1,0:T(1,128)S(1)} %bitcast.39), channel_id=1, source_target_pairs={{0,4},{4,0},{8,12},{12,8},{16,20},{20,16},{24,28},{28,24},{1,5},{5... | collective-permute-start | bytes 200 | tf_op jit(solution)/shard_map/ppermute | solution.py:27
  10.5 11.6 %copy-start = (bf16[64,8192]{1,0:T(8,128)(2,1)S(1)}, bf16[64,8192]{1,0:T(8,128)(2,1)}, u32[]{:S(2)}) copy-start(bf16[64,8192]{1,0:T(8,128)(2,1)} %refs_1_.9) | copy-start | bytes 3145732
  10.5 11.5 %copy-start.1 = (bf16[64,8192]{1,0:T(8,128)(2,1)S(1)}, bf16[64,8192]{1,0:T(8,128)(2,1)}, u32[]{:S(2)}) copy-start(bf16[64,8192]{1,0:T(8,128)(2,1)} %refs_2_.7) | copy-start | bytes 3145732
  13.7 53.5 %collective-permute-start.2 = (bf16[2,4,64,1024]{3,2,1,0:T(8,128)(2,1)}, bf16[2,4,64,1024]{3,2,1,0:T(8,128)(2,1)}, u32[]{:S(2)}, u32[]{:S(2)}) collective-permute-start(bf16[2,4,64,1024]{3,2,1,0:T(8,128)(2,1)} %get-tuple-element.80), channel_id=1, source_target_pairs={{0,1},{1,0},{2,3},{3,2},{4,5},{5,4},{6,7},{7,6},{8,9},{9,8},{10,11... | collective-permute-start | bytes 3145736 | tf_op jit(solution)/shard_map/ppermute | solution.py:27
  14.8 3.6 %collective-permute-start.4 = (f32[2,16]{1,0:T(2,128)S(1)}, f32[2,16]{1,0:T(2,128)S(1)}, u32[]{:S(2)}, u32[]{:S(2)}) collective-permute-start(f32[2,16]{1,0:T(2,128)S(1)} %maximum_select_fusion.2), channel_id=1, source_target_pairs={{0,8},{4,12},{8,0},{12,4},{16,24},{20,28},{24,16},{28,20},{1,9},{5... | collective-permute-start | bytes 392 | tf_op jit(solution)/shard_map/ppermute | solution.py:27
  16.5 3.6 %copy-start.15 = (f32[8,128]{1,0:T(8,128)S(1)}, f32[8,128]{1,0:T(8,128)}, u32[]{:S(2)}) copy-start(f32[8,128]{1,0:T(8,128)} %get-tuple-element.71.refs_3_) | copy-start | bytes 12292
  18.4 21.1 %collective-permute-start.5 = (f32[4,16]{1,0:T(4,128)S(1)}, f32[4,16]{1,0:T(4,128)S(1)}, u32[]{:S(2)}, u32[]{:S(2)}) collective-permute-start(f32[4,16]{1,0:T(4,128)S(1)} %maximum_select_fusion.1), channel_id=1, source_target_pairs={{0,16},{4,20},{8,24},{12,28},{16,0},{20,4},{24,8},{28,12},{1,17},{... | collective-permute-start | bytes 776 | tf_op jit(solution)/shard_map/ppermute | solution.py:27
  22.1 1.2 copy-start.2
  25.3 13.2 %copy-start.6 = (bf16[2,4,64,1024]{3,2,1,0:T(8,128)(2,1)}, bf16[2,4,64,1024]{3,2,1,0:T(8,128)(2,1)S(1)}, u32[]{:S(2)}) copy-start(bf16[2,4,64,1024]{3,2,1,0:T(8,128)(2,1)S(1)} %get-tuple-element.73.refs_0_.refs_1_) | copy-start | bytes 3145732
  39.5 30.7 %collective-permute-start.7 = (bf16[2,8,128,128]{3,2,1,0:T(8,128)(2,1)}, bf16[2,8,128,128]{3,2,1,0:T(8,128)(2,1)}, u32[]{:S(2)}, u32[]{:S(2)}) collective-permute-start(bf16[2,8,128,128]{3,2,1,0:T(8,128)(2,1)} %get-tuple-element.88), channel_id=1, source_target_pairs={{0,2},{1,3},{2,0},{3,1},{4,6},{5,7},{6,4},{7,5},{8,10},{9,11},{10,... | collective-permute-start | bytes 1572872 | tf_op jit(solution)/shard_map/ppermute | solution.py:27
  39.8 1.2 copy-start.3
  67.2 3.0 %copy-start.11 = (f32[2,8,128,128]{3,2,1,0:T(8,128)S(1)}, f32[2,8,128,128]{3,2,1,0:T(8,128)}, u32[]{:S(2)}) copy-start(f32[2,8,128,128]{3,2,1,0:T(8,128)} %copy-done.10) | copy-start | bytes 3145732
  72.2 2.0 %collective-permute-start.8 = (bf16[2,8,128,128]{3,2,1,0:T(8,128)(2,1)S(1)}, bf16[2,8,128,128]{3,2,1,0:T(8,128)(2,1)S(1)}, u32[]{:S(2)}, u32[]{:S(2)}) collective-permute-start(bf16[2,8,128,128]{3,2,1,0:T(8,128)(2,1)S(1)} %get-tuple-element.91), channel_id=1, source_target_pairs={{0,4},{4,0},{8,12},{12,8},{16,20},{20,16},{24,28},{28,24},{1,5},{5... | collective-permute-start | bytes 1572872 | tf_op jit(solution)/shard_map/ppermute | solution.py:27
  72.3 25.5 %collective-permute-start.6 = (bf16[2,8,128,128]{3,2,1,0:T(8,128)(2,1)S(1)}, bf16[2,8,128,128]{3,2,1,0:T(8,128)(2,1)S(1)}, u32[]{:S(2)}, u32[]{:S(2)}) collective-permute-start(bf16[2,8,128,128]{3,2,1,0:T(8,128)(2,1)S(1)} %get-tuple-element.86), channel_id=1, source_target_pairs={{0,2},{1,3},{2,0},{3,1},{4,6},{5,7},{6,4},{7,5},{8,10},{9,11},{10,... | collective-permute-start | bytes 1572872 | tf_op jit(solution)/shard_map/ppermute | solution.py:27
  75.2 9.2 %collective-permute-start.9 = (bf16[8,128,128]{2,1,0:T(8,128)(2,1)S(1)}, bf16[8,128,128]{2,1,0:T(8,128)(2,1)S(1)}, u32[]{:S(2)}, u32[]{:S(2)}) collective-permute-start(bf16[8,128,128]{2,1,0:T(8,128)(2,1)S(1)} %get-tuple-element.93), channel_id=1, source_target_pairs={{0,8},{4,12},{8,0},{12,4},{16,24},{20,28},{24,16},{28,20},{1,9},{5... | collective-permute-start | bytes 786440 | tf_op jit(solution)/shard_map/ppermute | solution.py:27
  76.7 13.5 %collective-permute-start.11 = (bf16[8,128,128]{2,1,0:T(8,128)(2,1)S(1)}, bf16[8,128,128]{2,1,0:T(8,128)(2,1)S(1)}, u32[]{:S(2)}, u32[]{:S(2)}) collective-permute-start(bf16[8,128,128]{2,1,0:T(8,128)(2,1)S(1)} %get-tuple-element.94), channel_id=1, source_target_pairs={{0,24},{4,28},{8,16},{12,20},{16,8},{20,12},{24,0},{28,4},{1,25},{... | collective-permute-start | bytes 786440 | tf_op jit(solution)/shard_map/ppermute | solution.py:27
  78.2 13.4 %collective-permute-start.10 = (bf16[8,128,128]{2,1,0:T(8,128)(2,1)S(1)}, bf16[8,128,128]{2,1,0:T(8,128)(2,1)S(1)}, u32[]{:S(2)}, u32[]{:S(2)}) collective-permute-start(bf16[8,128,128]{2,1,0:T(8,128)(2,1)S(1)} %get-tuple-element.94), channel_id=1, source_target_pairs={{0,16},{4,20},{8,24},{12,28},{16,0},{20,4},{24,8},{28,12},{1,17},{... | collective-permute-start | bytes 786440 | tf_op jit(solution)/shard_map/ppermute | solution.py:27
  98.6 6.6 %copy-start.7 = (bf16[2,4,64,1024]{3,2,1,0:T(8,128)(2,1)S(1)}, bf16[2,4,64,1024]{3,2,1,0:T(8,128)(2,1)}, u32[]{:S(2)}) copy-start(bf16[2,4,64,1024]{3,2,1,0:T(8,128)(2,1)} %copy-done.6) | copy-start | bytes 3145732
  98.7 2.0 %collective-permute-start.12 = (bf16[2,8,128,128]{3,2,1,0:T(8,128)(2,1)S(1)}, bf16[2,8,128,128]{3,2,1,0:T(8,128)(2,1)S(1)}, u32[]{:S(2)}, u32[]{:S(2)}) collective-permute-start(bf16[2,8,128,128]{3,2,1,0:T(8,128)(2,1)S(1)} %get-tuple-element.99), channel_id=1, source_target_pairs={{0,4},{4,0},{8,12},{12,8},{16,20},{20,16},{24,28},{28,24},{1,5},{5... | collective-permute-start | bytes 1572872 | tf_op jit(solution)/shard_map/ppermute | solution.py:27
  98.8 26.0 %collective-permute-start.16 = (bf16[2,8,128,128]{3,2,1,0:T(8,128)(2,1)S(1)}, bf16[2,8,128,128]{3,2,1,0:T(8,128)(2,1)S(1)}, u32[]{:S(2)}, u32[]{:S(2)}) collective-permute-start(bf16[2,8,128,128]{3,2,1,0:T(8,128)(2,1)S(1)} %get-tuple-element.104), channel_id=1, source_target_pairs={{0,2},{1,3},{2,0},{3,1},{4,6},{5,7},{6,4},{7,5},{8,10},{9,11},{10,... | collective-permute-start | bytes 1572872 | tf_op jit(solution)/shard_map/ppermute | solution.py:27
  100.6 4.6 %copy-start.9 = (f32[4,2,128,4]{3,2,1,0:T(8,128)S(1)}, f32[4,2,128,4]{3,2,1,0:T(8,128)}, u32[]{:S(2)}) copy-start(f32[4,2,128,4]{3,2,1,0:T(8,128)} %copy-done.8) | copy-start | bytes 49156
  101.6 23.1 %collective-permute-start.13 = (bf16[8,128,128]{2,1,0:T(8,128)(2,1)S(1)}, bf16[8,128,128]{2,1,0:T(8,128)(2,1)S(1)}, u32[]{:S(2)}, u32[]{:S(2)}) collective-permute-start(bf16[8,128,128]{2,1,0:T(8,128)(2,1)S(1)} %get-tuple-element.101), channel_id=1, source_target_pairs={{0,8},{4,12},{8,0},{12,4},{16,24},{20,28},{24,16},{28,20},{1,9},{5... | collective-permute-start | bytes 786440 | tf_op jit(solution)/shard_map/ppermute | solution.py:27
  103.2 21.5 %collective-permute-start.15 = (bf16[8,128,128]{2,1,0:T(8,128)(2,1)S(1)}, bf16[8,128,128]{2,1,0:T(8,128)(2,1)S(1)}, u32[]{:S(2)}, u32[]{:S(2)}) collective-permute-start(bf16[8,128,128]{2,1,0:T(8,128)(2,1)S(1)} %get-tuple-element.102), channel_id=1, source_target_pairs={{0,24},{4,28},{8,16},{12,20},{16,8},{20,12},{24,0},{28,4},{1,25},{... | collective-permute-start | bytes 786440 | tf_op jit(solution)/shard_map/ppermute | solution.py:27
  104.7 20.1 %collective-permute-start.14 = (bf16[8,128,128]{2,1,0:T(8,128)(2,1)S(1)}, bf16[8,128,128]{2,1,0:T(8,128)(2,1)S(1)}, u32[]{:S(2)}, u32[]{:S(2)}) collective-permute-start(bf16[8,128,128]{2,1,0:T(8,128)(2,1)S(1)} %get-tuple-element.102), channel_id=1, source_target_pairs={{0,16},{4,20},{8,24},{12,28},{16,0},{20,4},{24,8},{28,12},{1,17},{... | collective-permute-start | bytes 786440 | tf_op jit(solution)/shard_map/ppermute | solution.py:27
  126.1 25.2 %collective-permute-start.18 = (bf16[2,8,128,128]{3,2,1,0:T(8,128)(2,1)S(1)}, bf16[2,8,128,128]{3,2,1,0:T(8,128)(2,1)S(1)}, u32[]{:S(2)}, u32[]{:S(2)}) collective-permute-start(bf16[2,8,128,128]{3,2,1,0:T(8,128)(2,1)S(1)} %get-tuple-element.114), channel_id=1, source_target_pairs={{0,2},{1,3},{2,0},{3,1},{4,6},{5,7},{6,4},{7,5},{8,10},{9,11},{10,... | collective-permute-start | bytes 1572872 | tf_op jit(solution)/shard_map/ppermute | solution.py:27
  126.2 29.5 %collective-permute-start.20 = (bf16[3,64,1024]{2,1,0:T(8,128)(2,1)S(1)}, bf16[3,64,1024]{2,1,0:T(8,128)(2,1)S(1)}, u32[]{:S(2)}, u32[]{:S(2)}) collective-permute-start(bf16[3,64,1024]{2,1,0:T(8,128)(2,1)S(1)} %get-tuple-element.124), channel_id=1, source_target_pairs={{0,1},{1,0},{2,3},{3,2},{4,5},{5,4},{6,7},{7,6},{8,9},{9,8},{10,11... | collective-permute-start | bytes 1179656 | tf_op jit(solution)/shard_map/ppermute | solution.py:27
  132.8 36.1 %collective-permute-start.17 = (bf16[3,64,1024]{2,1,0:T(8,128)(2,1)S(1)}, bf16[3,64,1024]{2,1,0:T(8,128)(2,1)S(1)}, u32[]{:S(2)}, u32[]{:S(2)}) collective-permute-start(bf16[3,64,1024]{2,1,0:T(8,128)(2,1)S(1)} %get-tuple-element.113), channel_id=1, source_target_pairs={{0,1},{1,0},{2,3},{3,2},{4,5},{5,4},{6,7},{7,6},{8,9},{9,8},{10,11... | collective-permute-start | bytes 1179656 | tf_op jit(solution)/shard_map/ppermute | solution.py:27
  137.2 29.2 %collective-permute-start.21 = (bf16[3,64,1024]{2,1,0:T(8,128)(2,1)S(1)}, bf16[3,64,1024]{2,1,0:T(8,128)(2,1)S(1)}, u32[]{:S(2)}, u32[]{:S(2)}) collective-permute-start(bf16[3,64,1024]{2,1,0:T(8,128)(2,1)S(1)} %get-tuple-element.125), channel_id=1, source_target_pairs={{0,1},{1,0},{2,3},{3,2},{4,5},{5,4},{6,7},{7,6},{8,9},{9,8},{10,11... | collective-permute-start | bytes 1179656 | tf_op jit(solution)/shard_map/ppermute | solution.py:27
  155.7 18.2 %collective-permute-start.19 = (bf16[3,64,1024]{2,1,0:T(8,128)(2,1)S(1)}, bf16[3,64,1024]{2,1,0:T(8,128)(2,1)S(1)}, u32[]{:S(2)}, u32[]{:S(2)}) collective-permute-start(bf16[3,64,1024]{2,1,0:T(8,128)(2,1)S(1)} %get-tuple-element.123), channel_id=1, source_target_pairs={{0,1},{1,0},{2,3},{3,2},{4,5},{5,4},{6,7},{7,6},{8,9},{9,8},{10,11... | collective-permute-start | bytes 1179656 | tf_op jit(solution)/shard_map/ppermute | solution.py:27
  (6 other events, 5.5 us)

commit v3 on v2

--- a/solution.py
+++ b/solution.py
@@ -20,6 +20,7 @@
 TN = ((0,), (0,))
 LOW = jnp.bfloat16
 COST = pl.CostEstimate(flops=1, bytes_accessed=1, transcendentals=0)
+GRADS_COST = pl.CostEstimate(flops=4000000000, bytes_accessed=1, transcendentals=0)
 WIDE = jnp.float32
 
 
@@ -74,7 +75,7 @@
             out_shape=list(out_shape) + [jax.ShapeDtypeStruct((8, 128), WIDE)],
             input_output_aliases=aliases or {},
             compiler_params=pltpu.CompilerParams(vmem_limit_bytes=vmem),
-            cost_estimate=COST,
+            cost_estimate=GRADS_COST if name == "grads" else COST,
             name=name,
         )(*scalars, *inputs, *extra)
         return results
@@ -383,37 +384,30 @@
     count = len(parts)
 
     def kernel(at_ref, *refs):
-        ins, results = refs[:count], refs[count + 3 : count + 6]
-        buffers, sems = refs[count + 6 : -1], refs[-1]
-        loads, stores = [], []
+        ins, results, sems = refs[:count], refs[count + 3 : count + 6], refs[count + 6]
+        copies = []
         for p, ref in enumerate(ins):
             columns = pl.ds(pl.multiple_of(at_ref[p] * HEAD_DIM, HEAD_DIM), ref.shape[2])
-            loads.append(pltpu.make_async_copy(ref, buffers[p], sems.at[4 * p + 3]))
             for a in range(3):
-                stores.append(
+                copies.append(
                     pltpu.make_async_copy(
-                        buffers[p].at[a], results[a].at[:, columns], sems.at[4 * p + a]
+                        ref.at[a], results[a].at[:, columns], sems.at[len(copies)]
                     )
                 )
-        for load in loads:
-            load.start()
-        for p, load in enumerate(loads):
-            load.wait()
-            for store in stores[3 * p : 3 * p + 3]:
-                store.start()
-        for store in stores:
-            store.wait()
+        for copy in copies:
+            copy.start()
+        for copy in copies:
+            copy.wait()
 
     return order.call(
         kernel,
         "place",
         [jnp.stack(ats)],
         [*parts, *outs],
-        [ANY] * (count + 3),
+        [FULL] * count + [ANY] * 3,
         [jax.ShapeDtypeStruct((rows, full), LOW)] * 3,
         [ANY] * 3,
-        scratch=[pltpu.VMEM(p.shape, LOW) for p in parts]
-        + [pltpu.SemaphoreType.DMA((4 * count,))],
+        scratch=[pltpu.SemaphoreType.DMA((3 * count,))],
         aliases={1 + count + a: a for a in range(3)},
     )
 
@@ -577,6 +571,11 @@
     def touch(self):
         self.env.order.call(lambda *refs: None, "touch", [], [self.mirror_states], [ANY], [], [])
 
+    def arrive(self):
+        e = self.env
+        count = len(self.received)
+        e.order.call(lambda *refs: None, "arrive", [], self.received, [ANY] * count, [], [])
+
     def grads(self, group):
         e = self.env
         st = self.mirror_states if group else self.own_states
@@ -648,7 +647,7 @@
 
 
 WAVES = ("P8", "P8")
-STEPS = ("pa", "pb", "x", "ka", "sa", "kb", "sb", "ba", "va", "fa", "bb", "vb", "ga", "ta", "fb", "gb", "ha", "hb", "la", "lb")
+STEPS = ("pa", "pb", "ua", "x", "ka", "kb", "sa", "sb", "ba", "va", "fa", "bb", "vb", "ga", "ta", "fb", "gb", "la", "ha", "hb", "la", "lb")
 
 
 def schedule(e, heads, prepare):
@@ -686,6 +685,8 @@
             wave.place()
         elif code[0] == "t":
             wave.touch()
+        elif code[0] == "u":
+            wave.arrive()
 
 
 def solution(mesh):

time: 177 us -> 171 us (0.966)
  waiting for transfers between devices: 98.9 us -> 93.4 us
    ppermute x22, waiting for transfers between devices: 98.9 us -> 93.4 us  [swap(): lax.ppermute(x, axis, [(i, i ^ bit) for i in range(lax.axis_size(axis))])]
    pallas_call x20 -> x22, Pallas kernels: 45.6 us -> 44.1 us  [call(): pl.pallas_call(body, grid_spec=pltpu.PrefetchScalarGridSpec(num_scalar_pr...]
    unnamed x32 -> x40, local copies, waits for them, and re-layouts: 7.99 us -> 6.82 us
where the time goes in v3:
time: 171 us; the launch traced here: 170 us
  waiting for transfers between devices  93.4 us (55%)
  Pallas kernels  44.1 us (26%)
  starting transfers between devices  22.7 us (13%)
  local copies, waits for them, and re-layouts  7.92 us (5%)
    ppermute x22, waiting for transfers between devices, swap(): lax.ppermute(x, axis, [(i, i ^ bit) for i in range(lax.axis_size(axis))])  93.4 us
    pallas_call x22, Pallas kernels, call(): pl.pallas_call(body, grid_spec=pltpu.PrefetchScalarGridSpec(num_scalar_pr...  44.1 us
    ppermute x22, starting transfers between devices, swap(): lax.ppermute(x, axis, [(i, i ^ bit) for i in range(lax.axis_size(axis))])  22.7 us
    unnamed x40, local copies, waits for them, and re-layouts  6.82 us
  transfers between devices with their start and end apart: 22, of which 13 were waited for; matrix products, arithmetic and copies ran while one was open for 1% of the time, Pallas kernels for 22%

profile of v3, /device:TPU:0, one launch (start us, length us, event | category | flops | bytes accessed | tf_op | source)
XLA Modules:
  0.0 170.5 jit_solution(15145118718475726758)
XLA Ops:
  1.3 3.1 %pack.4 = (bf16[2,4,64,1024]{3,2,1,0:T(8,128)(2,1)}, f32[8,128]{1,0:T(8,128)}) custom-call(s32[2]{0:T(128)} %get-tuple-element.148.refs_0_, bf16[64,8192]{1,0:T(8,128)(2,1)} %refs_1_.9, bf16[64,8192]{1,0:T(8,128)(2,1)} %refs_2_.7, bf16[64,8192]{1,0:T(8,128)(2,1)} %refs_3_.7, bf16[64,8192]{1,0:T(8,128)(2,1)} %refs_4_.7), custom_call_target="tpu_custom_call" | custom-call | flops 1 | bytes 1 | tf_op jit(solution)/shard_map/pack/pallas_call | solution.py:66
  4.4 3.1 %collective-permute-start.1 = (bf16[2,4,64,1024]{3,2,1,0:T(8,128)(2,1)}, bf16[2,4,64,1024]{3,2,1,0:T(8,128)(2,1)}, u32[]{:S(2)}, u32[]{:S(2)}) collective-permute-start(bf16[2,4,64,1024]{3,2,1,0:T(8,128)(2,1)} %get-tuple-element.74), channel_id=1, source_target_pairs={{0,1},{1,0},{2,3},{3,2},{4,5},{5,4},{6,7},{7,6},{8,9},{9,8},{10,11... | collective-permute-start | bytes 3145736 | tf_op jit(solution)/shard_map/ppermute | solution.py:28
  7.5 2.6 %collective-permute-start = (f32[16,256]{1,0:T(8,128)S(1)}, f32[16,256]{1,0:T(8,128)S(1)}, u32[]{:S(2)}, u32[]{:S(2)}) collective-permute-start(f32[16,256]{1,0:T(8,128)S(1)} %copy-done.14), channel_id=1, source_target_pairs={{0,2},{1,3},{2,0},{3,1},{4,6},{5,7},{6,4},{7,5},{8,10},{9,11},{10,... | collective-permute-start | bytes 49160 | tf_op jit(solution)/shard_map/ppermute | solution.py:28
  10.1 3.1 %pack.5 = (bf16[2,4,64,1024]{3,2,1,0:T(8,128)(2,1)}, f32[8,128]{1,0:T(8,128)}) custom-call(s32[2]{0:T(128)} %get-tuple-element.147.refs_0_, bf16[64,8192]{1,0:T(8,128)(2,1)} %refs_1_.9, bf16[64,8192]{1,0:T(8,128)(2,1)} %refs_2_.7, bf16[64,8192]{1,0:T(8,128)(2,1)} %refs_3_.7, bf16[64,8192]{1,0:T(8,128)(2,1)} %refs_4_.7, f32[8,128]{1,0:T(8,128)} %get-tuple-element.75.refs_5_), custom_call_target="tpu_custom_call" | custom-call | flops 1 | bytes 1 | tf_op jit(solution)/shard_map/pack/pallas_call | solution.py:66
  15.2 1.6 collective-permute-start.4
  16.9 2.0 %collective-permute-done.4 = f32[2,16]{1,0:T(2,128)S(1)} collective-permute-done((f32[2,16]{1,0:T(2,128)S(1)}, f32[2,16]{1,0:T(2,128)S(1)}, u32[]{:S(2)}, u32[]{:S(2)}) %collective-permute-start.4) | collective-permute-done | bytes 160 | tf_op jit(solution)/shard_map/ppermute | solution.py:28
  18.9 1.6 collective-permute-start.5
  20.5 11.7 %collective-permute-done.1.refs_0_.refs_1_.refs_2_ = bf16[2,4,64,1024]{3,2,1,0:T(8,128)(2,1)} collective-permute-done((bf16[2,4,64,1024]{3,2,1,0:T(8,128)(2,1)}, bf16[2,4,64,1024]{3,2,1,0:T(8,128)(2,1)}, u32[]{:S(2)}, u32[]{:S(2)}) %collective-permute-start.1) | collective-permute-done | bytes 1048608 | tf_op jit(solution)/shard_map/ppermute | solution.py:28
  34.9 1.6 copy-done.3
  39.2 3.7 %states.2 = (f32[2,8,128,128]{3,2,1,0:T(8,128)S(1)}, bf16[2,8,128,128]{3,2,1,0:T(8,128)(2,1)}, f32[8,128]{1,0:T(8,128)S(1)}) custom-call(bf16[2,4,64,1024]{3,2,1,0:T(8,128)(2,1)S(1)} %get-tuple-element.86.refs_0_.refs_1_, bf16[2,4,64,1024]{3,2,1,0:T(8,128)(2,1)} %collective-permute-done.1.refs_0_.refs_1_.refs_2_, ...), custom_call_target="tpu_custom_call" | custom-call | flops 1 | bytes 1 | tf_op jit(solution)/shard_map/states/pallas_call | solution.py:66
  42.8 2.7 %collective-permute-start.7 = (bf16[2,8,128,128]{3,2,1,0:T(8,128)(2,1)}, bf16[2,8,128,128]{3,2,1,0:T(8,128)(2,1)S(1)}, u32[]{:S(2)}, u32[]{:S(2)}) collective-permute-start(bf16[2,8,128,128]{3,2,1,0:T(8,128)(2,1)} %get-tuple-element.92), channel_id=1, source_target_pairs={{0,2},{1,3},{2,0},{3,1},{4,6},{5,7},{6,4},{7,5},{8,10},{9,11},{10,... | collective-permute-start | bytes 1572872 | tf_op jit(solution)/shard_map/ppermute | solution.py:28
  45.8 18.9 %collective-permute-done.2.refs_1_.refs_2_ = bf16[2,4,64,1024]{3,2,1,0:T(8,128)(2,1)} collective-permute-done((bf16[2,4,64,1024]{3,2,1,0:T(8,128)(2,1)}, bf16[2,4,64,1024]{3,2,1,0:T(8,128)(2,1)}, u32[]{:S(2)}, u32[]{:S(2)}) %collective-permute-start.2) | collective-permute-done | bytes 1048608 | tf_op jit(solution)/shard_map/ppermute | solution.py:28
  66.9 2.9 %states.3 = (f32[2,8,128,128]{3,2,1,0:T(8,128)S(1)}, bf16[2,8,128,128]{3,2,1,0:T(8,128)(2,1)S(1)}, f32[8,128]{1,0:T(8,128)S(1)}) custom-call(bf16[2,4,64,1024]{3,2,1,0:T(8,128)(2,1)S(1)} %copy-done.11, bf16[2,4,64,1024]{3,2,1,0:T(8,128)(2,1)} %collective-permute-done.2.refs_1_.refs_2_, f32[4,2,128,4]{3,2,1,0:T(8,128)S(1)} %copy-done.5, ...), custom_call_target="tpu_custom_call" | custom-call | flops 1 | bytes 1 | tf_op jit(solution)/shard_map/states/pallas_call | solution.py:66
  70.8 1.8 %collective-permute-done.8.refs_3_ = bf16[2,8,128,128]{3,2,1,0:T(8,128)(2,1)S(1)} collective-permute-done((bf16[2,8,128,128]{3,2,1,0:T(8,128)(2,1)S(1)}, bf16[2,8,128,128]{3,2,1,0:T(8,128)(2,1)S(1)}, u32[]{:S(2)}, u32[]{:S(2)}) %collective-permute-start.8) | collective-permute-done | bytes 524320 | tf_op jit(solution)/shard_map/ppermute | solution.py:28
  73.7 1.9 %collective-permute-start.10 = (bf16[8,128,128]{2,1,0:T(8,128)(2,1)S(1)}, bf16[8,128,128]{2,1,0:T(8,128)(2,1)S(1)}, u32[]{:S(2)}, u32[]{:S(2)}) collective-permute-start(bf16[8,128,128]{2,1,0:T(8,128)(2,1)S(1)} %get-tuple-element.98), channel_id=1, source_target_pairs={{0,16},{4,20},{8,24},{12,28},{16,0},{20,4},{24,8},{28,12},{1,17},{... | collective-permute-start | bytes 786440 | tf_op jit(solution)/shard_map/ppermute | solution.py:28
  75.6 1.4 collective-permute-start.11
  77.2 10.6 %collective-permute-done.10.refs_3_ = bf16[8,128,128]{2,1,0:T(8,128)(2,1)S(1)} collective-permute-done((bf16[8,128,128]{2,1,0:T(8,128)(2,1)S(1)}, bf16[8,128,128]{2,1,0:T(8,128)(2,1)S(1)}, u32[]{:S(2)}, u32[]{:S(2)}) %collective-permute-start.10) | collective-permute-done | bytes 262176 | tf_op jit(solution)/shard_map/ppermute | solution.py:28
  90.4 5.8 %collective-permute-done.6.refs_3_.refs_6_ = bf16[2,8,128,128]{3,2,1,0:T(8,128)(2,1)S(1)} collective-permute-done((bf16[2,8,128,128]{3,2,1,0:T(8,128)(2,1)S(1)}, bf16[2,8,128,128]{3,2,1,0:T(8,128)(2,1)S(1)}, u32[]{:S(2)}, u32[]{:S(2)}) %collective-permute-start.6) | collective-permute-done | bytes 524320 | tf_op jit(solution)/shard_map/ppermute | solution.py:28
  97.3 1.8 %collective-permute-done.12.refs_3_ = bf16[2,8,128,128]{3,2,1,0:T(8,128)(2,1)S(1)} collective-permute-done((bf16[2,8,128,128]{3,2,1,0:T(8,128)(2,1)S(1)}, bf16[2,8,128,128]{3,2,1,0:T(8,128)(2,1)S(1)}, u32[]{:S(2)}, u32[]{:S(2)}) %collective-permute-start.12) | collective-permute-done | bytes 524320 | tf_op jit(solution)/shard_map/ppermute | solution.py:28
  100.1 1.9 %collective-permute-start.14 = (bf16[8,128,128]{2,1,0:T(8,128)(2,1)S(1)}, bf16[8,128,128]{2,1,0:T(8,128)(2,1)S(1)}, u32[]{:S(2)}, u32[]{:S(2)}) collective-permute-start(bf16[8,128,128]{2,1,0:T(8,128)(2,1)S(1)} %get-tuple-element.106), channel_id=1, source_target_pairs={{0,16},{4,20},{8,24},{12,28},{16,0},{20,4},{24,8},{28,12},{1,17},{... | collective-permute-start | bytes 786440 | tf_op jit(solution)/shard_map/ppermute | solution.py:28
  102.0 1.4 collective-permute-start.15
  103.7 4.4 %grads.4 = (bf16[64,8192]{1,0:T(8,128)(2,1)}, bf16[64,8192]{1,0:T(8,128)(2,1)}, bf16[64,8192]{1,0:T(8,128)(2,1)}, bf16[3,64,1024]{2,1,0:T(8,128)(2,1)S(1)}, f32[8,128]{1,0:T(8,128)S(1)}) custom-call(s32[2]{0:T(128)S(1)} %get-tuple-element.145.refs_0_, bf16[2,4,64,1024]{3,2,1,0:T(8,128)(2,1)S(1)} %copy-done.13, ...), custom_call_target="tpu_custom_call" | custom-call | flops 4000000000 | bytes 1 | tf_op jit(solution)/shard_map/grads/pallas_call | solution.py:66
  109.6 13.7 %collective-permute-done.16.refs_0_.refs_8_ = bf16[2,8,128,128]{3,2,1,0:T(8,128)(2,1)S(1)} collective-permute-done((bf16[2,8,128,128]{3,2,1,0:T(8,128)(2,1)S(1)}, bf16[2,8,128,128]{3,2,1,0:T(8,128)(2,1)S(1)}, u32[]{:S(2)}, u32[]{:S(2)}) %collective-permute-start.16) | collective-permute-done | bytes 524320 | tf_op jit(solution)/shard_map/ppermute | solution.py:28
  124.8 4.4 %grads.5 = (bf16[64,8192]{1,0:T(8,128)(2,1)}, bf16[64,8192]{1,0:T(8,128)(2,1)}, bf16[64,8192]{1,0:T(8,128)(2,1)}, bf16[3,64,1024]{2,1,0:T(8,128)(2,1)S(1)}, f32[8,128]{1,0:T(8,128)S(1)}) custom-call(s32[2]{0:T(128)S(1)} %get-tuple-element.152.refs_0_, ...), custom_call_target="tpu_custom_call", output_to_operand_aliasing={{0}: (9, {}), {1}: (10, {}), {2}: (11, {})} | custom-call | flops 4000000000 | bytes 1 | tf_op jit(solution)/shard_map/grads/pallas_call | solution.py:66
  129.2 2.2 %collective-permute-start.17 = (bf16[3,64,1024]{2,1,0:T(8,128)(2,1)S(1)}, bf16[3,64,1024]{2,1,0:T(8,128)(2,1)S(1)}, u32[]{:S(2)}, u32[]{:S(2)}) collective-permute-start(bf16[3,64,1024]{2,1,0:T(8,128)(2,1)S(1)} %get-tuple-element.117), channel_id=1, source_target_pairs={{0,1},{1,0},{2,3},{3,2},{4,5},{5,4},{6,7},{7,6},{8,9},{9,8},{10,11... | collective-permute-start | bytes 1179656 | tf_op jit(solution)/shard_map/ppermute | solution.py:28
  131.4 1.5 place.3
  132.8 4.4 %grads.6 = (bf16[64,8192]{1,0:T(8,128)(2,1)}, bf16[64,8192]{1,0:T(8,128)(2,1)}, bf16[64,8192]{1,0:T(8,128)(2,1)}, bf16[3,64,1024]{2,1,0:T(8,128)(2,1)S(1)}, f32[8,128]{1,0:T(8,128)S(1)}) custom-call(s32[2]{0:T(128)S(1)} %get-tuple-element.145.refs_0_, ...), custom_call_target="tpu_custom_call", output_to_operand_aliasing={{0}: (9, {}), {1}: (10, {}), {2}: (11, {})} | custom-call | flops 4000000000 | bytes 1 | tf_op jit(solution)/shard_map/grads/pallas_call | solution.py:66
  137.3 12.6 %collective-permute-done.18.refs_8_ = bf16[2,8,128,128]{3,2,1,0:T(8,128)(2,1)S(1)} collective-permute-done((bf16[2,8,128,128]{3,2,1,0:T(8,128)(2,1)S(1)}, bf16[2,8,128,128]{3,2,1,0:T(8,128)(2,1)S(1)}, u32[]{:S(2)}, u32[]{:S(2)}) %collective-permute-start.18) | collective-permute-done | bytes 524320 | tf_op jit(solution)/shard_map/ppermute | solution.py:28
  149.8 4.4 %grads.7 = (bf16[64,8192]{1,0:T(8,128)(2,1)}, bf16[64,8192]{1,0:T(8,128)(2,1)}, bf16[64,8192]{1,0:T(8,128)(2,1)}, bf16[3,64,1024]{2,1,0:T(8,128)(2,1)S(1)}, f32[8,128]{1,0:T(8,128)S(1)}) custom-call(s32[2]{0:T(128)S(1)} %get-tuple-element.152.refs_0_, ...), custom_call_target="tpu_custom_call", output_to_operand_aliasing={{0}: (9, {}), {1}: (10, {}), {2}: (11, {})} | custom-call | flops 4000000000 | bytes 1 | tf_op jit(solution)/shard_map/grads/pallas_call | solution.py:66
  154.2 6.6 %collective-permute-done.21.refs_1_ = bf16[3,64,1024]{2,1,0:T(8,128)(2,1)S(1)} collective-permute-done((bf16[3,64,1024]{2,1,0:T(8,128)(2,1)S(1)}, bf16[3,64,1024]{2,1,0:T(8,128)(2,1)S(1)}, u32[]{:S(2)}, u32[]{:S(2)}) %collective-permute-start.21) | collective-permute-done | bytes 393248 | tf_op jit(solution)/shard_map/ppermute | solution.py:28
  162.2 6.1 %collective-permute-done.20.refs_2_ = bf16[3,64,1024]{2,1,0:T(8,128)(2,1)S(1)} collective-permute-done((bf16[3,64,1024]{2,1,0:T(8,128)(2,1)S(1)}, bf16[3,64,1024]{2,1,0:T(8,128)(2,1)S(1)}, u32[]{:S(2)}, u32[]{:S(2)}) %collective-permute-start.20) | collective-permute-done | bytes 393248 | tf_op jit(solution)/shard_map/ppermute | solution.py:28
  169.0 1.5 place.5
  (98 shorter events, 22.5 us)
Async XLA Ops:
  1.3 6.2 %copy-start.14 = (f32[16,256]{1,0:T(8,128)S(1)}, f32[16,256]{1,0:T(8,128)}, u32[]{:S(2)}) copy-start(f32[16,256]{1,0:T(8,128)} %refs_1_.7) | copy-start | bytes 49156
  4.4 27.7 %collective-permute-start.1 = (bf16[2,4,64,1024]{3,2,1,0:T(8,128)(2,1)}, bf16[2,4,64,1024]{3,2,1,0:T(8,128)(2,1)}, u32[]{:S(2)}, u32[]{:S(2)}) collective-permute-start(bf16[2,4,64,1024]{3,2,1,0:T(8,128)(2,1)} %get-tuple-element.74), channel_id=1, source_target_pairs={{0,1},{1,0},{2,3},{3,2},{4,5},{5,4},{6,7},{7,6},{8,9},{9,8},{10,11... | collective-permute-start | bytes 3145736 | tf_op jit(solution)/shard_map/ppermute | solution.py:28
  7.5 25.3 %collective-permute-start = (f32[16,256]{1,0:T(8,128)S(1)}, f32[16,256]{1,0:T(8,128)S(1)}, u32[]{:S(2)}, u32[]{:S(2)}) collective-permute-start(f32[16,256]{1,0:T(8,128)S(1)} %copy-done.14), channel_id=1, source_target_pairs={{0,2},{1,3},{2,0},{3,1},{4,6},{5,7},{6,4},{7,5},{8,10},{9,11},{10,... | collective-permute-start | bytes 49160 | tf_op jit(solution)/shard_map/ppermute | solution.py:28
  10.1 24.8 %copy-start.1 = (bf16[64,8192]{1,0:T(8,128)(2,1)S(1)}, bf16[64,8192]{1,0:T(8,128)(2,1)}, u32[]{:S(2)}) copy-start(bf16[64,8192]{1,0:T(8,128)(2,1)} %refs_2_.7) | copy-start | bytes 3145732
  10.1 24.8 %copy-start.2 = (bf16[64,8192]{1,0:T(8,128)(2,1)S(1)}, bf16[64,8192]{1,0:T(8,128)(2,1)}, u32[]{:S(2)}) copy-start(bf16[64,8192]{1,0:T(8,128)(2,1)} %refs_3_.7) | copy-start | bytes 3145732
  13.2 21.7 %copy-start = (bf16[64,8192]{1,0:T(8,128)(2,1)S(1)}, bf16[64,8192]{1,0:T(8,128)(2,1)}, u32[]{:S(2)}) copy-start(bf16[64,8192]{1,0:T(8,128)(2,1)} %refs_1_.9) | copy-start | bytes 3145732
  13.2 51.5 %collective-permute-start.2 = (bf16[2,4,64,1024]{3,2,1,0:T(8,128)(2,1)}, bf16[2,4,64,1024]{3,2,1,0:T(8,128)(2,1)}, u32[]{:S(2)}, u32[]{:S(2)}) collective-permute-start(bf16[2,4,64,1024]{3,2,1,0:T(8,128)(2,1)} %get-tuple-element.80), channel_id=1, source_target_pairs={{0,1},{1,0},{2,3},{3,2},{4,5},{5,4},{6,7},{7,6},{8,9},{9,8},{10,11... | collective-permute-start | bytes 3145736 | tf_op jit(solution)/shard_map/ppermute | solution.py:28
  14.0 1.2 collective-permute-start.3
  15.2 3.6 %collective-permute-start.4 = (f32[2,16]{1,0:T(2,128)S(1)}, f32[2,16]{1,0:T(2,128)S(1)}, u32[]{:S(2)}, u32[]{:S(2)}) collective-permute-start(f32[2,16]{1,0:T(2,128)S(1)} %maximum_select_fusion.2), channel_id=1, source_target_pairs={{0,8},{4,12},{8,0},{12,4},{16,24},{20,28},{24,16},{28,20},{1,9},{5... | collective-permute-start | bytes 392 | tf_op jit(solution)/shard_map/ppermute | solution.py:28
  18.9 26.7 %collective-permute-start.5 = (f32[4,16]{1,0:T(4,128)S(1)}, f32[4,16]{1,0:T(4,128)S(1)}, u32[]{:S(2)}, u32[]{:S(2)}) collective-permute-start(f32[4,16]{1,0:T(4,128)S(1)} %maximum_select_fusion.1), channel_id=1, source_target_pairs={{0,16},{4,20},{8,24},{12,28},{16,0},{20,4},{24,8},{28,12},{1,17},{... | collective-permute-start | bytes 776 | tf_op jit(solution)/shard_map/ppermute | solution.py:28
  34.9 4.2 %copy-start.7 = (f32[4,2,128,4]{3,2,1,0:T(8,128)}, f32[4,2,128,4]{3,2,1,0:T(8,128)S(1)}, u32[]{:S(2)}) copy-start(f32[4,2,128,4]{3,2,1,0:T(8,128)S(1)} %get-tuple-element.82.refs_3_.refs_4_) | copy-start | bytes 49156
  39.1 25.6 %copy-start.11 = (bf16[2,4,64,1024]{3,2,1,0:T(8,128)(2,1)S(1)}, bf16[2,4,64,1024]{3,2,1,0:T(8,128)(2,1)}, u32[]{:S(2)}) copy-start(bf16[2,4,64,1024]{3,2,1,0:T(8,128)(2,1)} %copy-done.10) | copy-start | bytes 3145732
  42.8 26.9 %collective-permute-start.7 = (bf16[2,8,128,128]{3,2,1,0:T(8,128)(2,1)}, bf16[2,8,128,128]{3,2,1,0:T(8,128)(2,1)S(1)}, u32[]{:S(2)}, u32[]{:S(2)}) collective-permute-start(bf16[2,8,128,128]{3,2,1,0:T(8,128)(2,1)} %get-tuple-element.92), channel_id=1, source_target_pairs={{0,2},{1,3},{2,0},{3,1},{4,6},{5,7},{6,4},{7,5},{8,10},{9,11},{10,... | collective-permute-start | bytes 1572872 | tf_op jit(solution)/shard_map/ppermute | solution.py:28
  70.7 2.0 %collective-permute-start.8 = (bf16[2,8,128,128]{3,2,1,0:T(8,128)(2,1)S(1)}, bf16[2,8,128,128]{3,2,1,0:T(8,128)(2,1)S(1)}, u32[]{:S(2)}, u32[]{:S(2)}) collective-permute-start(bf16[2,8,128,128]{3,2,1,0:T(8,128)(2,1)S(1)} %get-tuple-element.95), channel_id=1, source_target_pairs={{0,4},{4,0},{8,12},{12,8},{16,20},{20,16},{24,28},{28,24},{1,5},{5... | collective-permute-start | bytes 1572872 | tf_op jit(solution)/shard_map/ppermute | solution.py:28
  70.8 25.5 %collective-permute-start.6 = (bf16[2,8,128,128]{3,2,1,0:T(8,128)(2,1)S(1)}, bf16[2,8,128,128]{3,2,1,0:T(8,128)(2,1)S(1)}, u32[]{:S(2)}, u32[]{:S(2)}) collective-permute-start(bf16[2,8,128,128]{3,2,1,0:T(8,128)(2,1)S(1)} %get-tuple-element.90), channel_id=1, source_target_pairs={{0,2},{1,3},{2,0},{3,1},{4,6},{5,7},{6,4},{7,5},{8,10},{9,11},{10,... | collective-permute-start | bytes 1572872 | tf_op jit(solution)/shard_map/ppermute | solution.py:28
  73.7 14.1 %collective-permute-start.10 = (bf16[8,128,128]{2,1,0:T(8,128)(2,1)S(1)}, bf16[8,128,128]{2,1,0:T(8,128)(2,1)S(1)}, u32[]{:S(2)}, u32[]{:S(2)}) collective-permute-start(bf16[8,128,128]{2,1,0:T(8,128)(2,1)S(1)} %get-tuple-element.98), channel_id=1, source_target_pairs={{0,16},{4,20},{8,24},{12,28},{16,0},{20,4},{24,8},{28,12},{1,17},{... | collective-permute-start | bytes 786440 | tf_op jit(solution)/shard_map/ppermute | solution.py:28
  75.6 12.2 %collective-permute-start.11 = (bf16[8,128,128]{2,1,0:T(8,128)(2,1)S(1)}, bf16[8,128,128]{2,1,0:T(8,128)(2,1)S(1)}, u32[]{:S(2)}, u32[]{:S(2)}) collective-permute-start(bf16[8,128,128]{2,1,0:T(8,128)(2,1)S(1)} %get-tuple-element.98), channel_id=1, source_target_pairs={{0,24},{4,28},{8,16},{12,20},{16,8},{20,12},{24,0},{28,4},{1,25},{... | collective-permute-start | bytes 786440 | tf_op jit(solution)/shard_map/ppermute | solution.py:28
  77.0 12.1 %collective-permute-start.9 = (bf16[8,128,128]{2,1,0:T(8,128)(2,1)S(1)}, bf16[8,128,128]{2,1,0:T(8,128)(2,1)S(1)}, u32[]{:S(2)}, u32[]{:S(2)}) collective-permute-start(bf16[8,128,128]{2,1,0:T(8,128)(2,1)S(1)} %get-tuple-element.97), channel_id=1, source_target_pairs={{0,8},{4,12},{8,0},{12,4},{16,24},{20,28},{24,16},{28,20},{1,9},{5... | collective-permute-start | bytes 786440 | tf_op jit(solution)/shard_map/ppermute | solution.py:28
  96.2 7.5 %copy-start.13 = (bf16[2,4,64,1024]{3,2,1,0:T(8,128)(2,1)S(1)}, bf16[2,4,64,1024]{3,2,1,0:T(8,128)(2,1)}, u32[]{:S(2)}) copy-start(bf16[2,4,64,1024]{3,2,1,0:T(8,128)(2,1)} %copy-done.12) | copy-start | bytes 3145732
  97.1 2.0 %collective-permute-start.12 = (bf16[2,8,128,128]{3,2,1,0:T(8,128)(2,1)S(1)}, bf16[2,8,128,128]{3,2,1,0:T(8,128)(2,1)S(1)}, u32[]{:S(2)}, u32[]{:S(2)}) collective-permute-start(bf16[2,8,128,128]{3,2,1,0:T(8,128)(2,1)S(1)} %get-tuple-element.103), channel_id=1, source_target_pairs={{0,4},{4,0},{8,12},{12,8},{16,20},{20,16},{24,28},{28,24},{1,5},{5... | collective-permute-start | bytes 1572872 | tf_op jit(solution)/shard_map/ppermute | solution.py:28
  97.3 26.1 %collective-permute-start.16 = (bf16[2,8,128,128]{3,2,1,0:T(8,128)(2,1)S(1)}, bf16[2,8,128,128]{3,2,1,0:T(8,128)(2,1)S(1)}, u32[]{:S(2)}, u32[]{:S(2)}) collective-permute-start(bf16[2,8,128,128]{3,2,1,0:T(8,128)(2,1)S(1)} %get-tuple-element.108), channel_id=1, source_target_pairs={{0,2},{1,3},{2,0},{3,1},{4,6},{5,7},{6,4},{7,5},{8,10},{9,11},{10,... | collective-permute-start | bytes 1572872 | tf_op jit(solution)/shard_map/ppermute | solution.py:28
  99.1 4.6 %copy-start.6 = (f32[4,2,128,4]{3,2,1,0:T(8,128)S(1)}, f32[4,2,128,4]{3,2,1,0:T(8,128)}, u32[]{:S(2)}) copy-start(f32[4,2,128,4]{3,2,1,0:T(8,128)} %copy-done.4) | copy-start | bytes 49156
  99.1 4.6 %copy-start.9 = (f32[4,2,128,4]{3,2,1,0:T(8,128)S(1)}, f32[4,2,128,4]{3,2,1,0:T(8,128)}, u32[]{:S(2)}) copy-start(f32[4,2,128,4]{3,2,1,0:T(8,128)} %copy-done.7) | copy-start | bytes 49156
  99.1 4.6 %copy-start.18 = (f32[4,2,128,4]{3,2,1,0:T(8,128)S(1)}, f32[4,2,128,4]{3,2,1,0:T(8,128)}, u32[]{:S(2)}) copy-start(f32[4,2,128,4]{3,2,1,0:T(8,128)} %copy-done.17) | copy-start | bytes 49156
  100.1 23.2 %collective-permute-start.14 = (bf16[8,128,128]{2,1,0:T(8,128)(2,1)S(1)}, bf16[8,128,128]{2,1,0:T(8,128)(2,1)S(1)}, u32[]{:S(2)}, u32[]{:S(2)}) collective-permute-start(bf16[8,128,128]{2,1,0:T(8,128)(2,1)S(1)} %get-tuple-element.106), channel_id=1, source_target_pairs={{0,16},{4,20},{8,24},{12,28},{16,0},{20,4},{24,8},{28,12},{1,17},{... | collective-permute-start | bytes 786440 | tf_op jit(solution)/shard_map/ppermute | solution.py:28
  102.0 21.3 %collective-permute-start.15 = (bf16[8,128,128]{2,1,0:T(8,128)(2,1)S(1)}, bf16[8,128,128]{2,1,0:T(8,128)(2,1)S(1)}, u32[]{:S(2)}, u32[]{:S(2)}) collective-permute-start(bf16[8,128,128]{2,1,0:T(8,128)(2,1)S(1)} %get-tuple-element.106), channel_id=1, source_target_pairs={{0,24},{4,28},{8,16},{12,20},{16,8},{20,12},{24,0},{28,4},{1,25},{... | collective-permute-start | bytes 786440 | tf_op jit(solution)/shard_map/ppermute | solution.py:28
  103.5 19.9 %collective-permute-start.13 = (bf16[8,128,128]{2,1,0:T(8,128)(2,1)S(1)}, bf16[8,128,128]{2,1,0:T(8,128)(2,1)S(1)}, u32[]{:S(2)}, u32[]{:S(2)}) collective-permute-start(bf16[8,128,128]{2,1,0:T(8,128)(2,1)S(1)} %get-tuple-element.105), channel_id=1, source_target_pairs={{0,8},{4,12},{8,0},{12,4},{16,24},{20,28},{24,16},{28,20},{1,9},{5... | collective-permute-start | bytes 786440 | tf_op jit(solution)/shard_map/ppermute | solution.py:28
  108.1 23.2 %collective-permute-start.19 = (bf16[3,64,1024]{2,1,0:T(8,128)(2,1)S(1)}, bf16[3,64,1024]{2,1,0:T(8,128)(2,1)S(1)}, u32[]{:S(2)}, u32[]{:S(2)}) collective-permute-start(bf16[3,64,1024]{2,1,0:T(8,128)(2,1)S(1)} %get-tuple-element.119), channel_id=1, source_target_pairs={{0,1},{1,0},{2,3},{3,2},{4,5},{5,4},{6,7},{7,6},{8,9},{9,8},{10,11... | collective-permute-start | bytes 1179656 | tf_op jit(solution)/shard_map/ppermute | solution.py:28
  124.7 25.1 %collective-permute-start.18 = (bf16[2,8,128,128]{3,2,1,0:T(8,128)(2,1)S(1)}, bf16[2,8,128,128]{3,2,1,0:T(8,128)(2,1)S(1)}, u32[]{:S(2)}, u32[]{:S(2)}) collective-permute-start(bf16[2,8,128,128]{3,2,1,0:T(8,128)(2,1)S(1)} %get-tuple-element.118), channel_id=1, source_target_pairs={{0,2},{1,3},{2,0},{3,1},{4,6},{5,7},{6,4},{7,5},{8,10},{9,11},{10,... | collective-permute-start | bytes 1572872 | tf_op jit(solution)/shard_map/ppermute | solution.py:28
  129.2 33.0 %collective-permute-start.17 = (bf16[3,64,1024]{2,1,0:T(8,128)(2,1)S(1)}, bf16[3,64,1024]{2,1,0:T(8,128)(2,1)S(1)}, u32[]{:S(2)}, u32[]{:S(2)}) collective-permute-start(bf16[3,64,1024]{2,1,0:T(8,128)(2,1)S(1)} %get-tuple-element.117), channel_id=1, source_target_pairs={{0,1},{1,0},{2,3},{3,2},{4,5},{5,4},{6,7},{7,6},{8,9},{9,8},{10,11... | collective-permute-start | bytes 1179656 | tf_op jit(solution)/shard_map/ppermute | solution.py:28
  137.3 23.6 %collective-permute-start.21 = (bf16[3,64,1024]{2,1,0:T(8,128)(2,1)S(1)}, bf16[3,64,1024]{2,1,0:T(8,128)(2,1)S(1)}, u32[]{:S(2)}, u32[]{:S(2)}) collective-permute-start(bf16[3,64,1024]{2,1,0:T(8,128)(2,1)S(1)} %get-tuple-element.133), channel_id=1, source_target_pairs={{0,1},{1,0},{2,3},{3,2},{4,5},{5,4},{6,7},{7,6},{8,9},{9,8},{10,11... | collective-permute-start | bytes 1179656 | tf_op jit(solution)/shard_map/ppermute | solution.py:28
  154.2 14.1 %collective-permute-start.20 = (bf16[3,64,1024]{2,1,0:T(8,128)(2,1)S(1)}, bf16[3,64,1024]{2,1,0:T(8,128)(2,1)S(1)}, u32[]{:S(2)}, u32[]{:S(2)}) collective-permute-start(bf16[3,64,1024]{2,1,0:T(8,128)(2,1)S(1)} %get-tuple-element.132), channel_id=1, source_target_pairs={{0,1},{1,0},{2,3},{3,2},{4,5},{5,4},{6,7},{7,6},{8,9},{9,8},{10,11... | collective-permute-start | bytes 1179656 | tf_op jit(solution)/shard_map/ppermute | solution.py:28
  (10 other events, 13.8 us)

commit v4 on v3

--- a/solution.py
+++ b/solution.py
@@ -20,6 +20,7 @@
 TN = ((0,), (0,))
 LOW = jnp.bfloat16
 COST = pl.CostEstimate(flops=1, bytes_accessed=1, transcendentals=0)
+TOUCH_COST = pl.CostEstimate(flops=1, bytes_accessed=1, transcendentals=0)
 GRADS_COST = pl.CostEstimate(flops=4000000000, bytes_accessed=1, transcendentals=0)
 WIDE = jnp.float32
 
@@ -75,7 +76,7 @@
             out_shape=list(out_shape) + [jax.ShapeDtypeStruct((8, 128), WIDE)],
             input_output_aliases=aliases or {},
             compiler_params=pltpu.CompilerParams(vmem_limit_bytes=vmem),
-            cost_estimate=GRADS_COST if name == "grads" else COST,
+            cost_estimate={"grads": GRADS_COST, "touch": TOUCH_COST}.get(name, COST),
             name=name,
         )(*scalars, *inputs, *extra)
         return results
@@ -97,7 +98,7 @@
     return dq.astype(LOW), dk.astype(LOW), dv.astype(LOW)
 
 
-def pack(order, target, arrays, hw, after=(), vmem=60 * 1024 * 1024):
+def pack(order, target, arrays, hw):
     rows = arrays[0].shape[0]
     width = hw * HEAD_DIM
     groups = target.shape[0]
@@ -127,8 +128,47 @@
         [jax.ShapeDtypeStruct((groups, 4, rows, width), LOW)],
         [FULL],
         scratch=[pltpu.SemaphoreType.DMA((4 * groups,))],
-        after=after,
-        vmem=vmem,
+    )
+    return packed
+
+
+def pack_away(order, target, arrays, hw):
+    rows = arrays[0].shape[0]
+    width = hw * HEAD_DIM
+    groups = target.shape[0]
+    shape = (groups, 4, rows, width)
+
+    def kernel(at_ref, *refs):
+        ins, out, buffer, sems = refs[:4], refs[4], refs[5], refs[6]
+        loads, stores = [], []
+        for o in range(groups):
+            columns = pl.ds(pl.multiple_of(at_ref[o] * HEAD_DIM, HEAD_DIM), width)
+            for a, ref in enumerate(ins):
+                n = len(loads)
+                loads.append(
+                    pltpu.make_async_copy(ref.at[:, columns], buffer.at[o, a], sems.at[0, n])
+                )
+                stores.append(
+                    pltpu.make_async_copy(buffer.at[o, a], out.at[o, a], sems.at[1, n])
+                )
+        for load in loads:
+            load.start()
+        for load, store in zip(loads, stores):
+            load.wait()
+            store.start()
+        for store in stores:
+            store.wait()
+
+    (packed,) = order.call(
+        kernel,
+        "pack",
+        [target],
+        arrays,
+        [ANY] * 4,
+        [jax.ShapeDtypeStruct(shape, LOW)],
+        [ANY],
+        scratch=[pltpu.VMEM(shape, LOW), pltpu.SemaphoreType.DMA((2, 4 * groups))],
+        vmem=60 * 1024 * 1024,
     )
     return packed
 
@@ -141,7 +181,7 @@
 
     def kernel(at_ref, *refs):
         sources = refs[:groups]
-        cumr, cumc, qw, kw, bias = refs[groups:]
+        cumr, cols, bias = refs[groups:]
         slot, upper = at_ref[0], at_ref[1]
 
         def position(axis):
@@ -175,11 +215,10 @@
             for i in range(steps):
                 part = slice(i * hb, (i + 1) * hb)
                 cumr[i, o] = line[part]
-                cumc[i, o] = column[:, part]
-                qw[i, o] = query[:, part]
-                kw[i, o] = key[:, part]
-
-    columns = jax.ShapeDtypeStruct((steps, groups, span, hb), WIDE)
+                for j, value in enumerate((column, query, key)):
+                    cols[i, o, :, j * hb : (j + 1) * hb] = value[:, part]
+
+    columns = jax.ShapeDtypeStruct((steps, groups, span, 3 * hb), WIDE)
     return order.call(
         kernel,
         "decays",
@@ -189,11 +228,9 @@
         [
             jax.ShapeDtypeStruct((steps, groups, hb, span), WIDE),
             columns,
-            columns,
-            columns,
             jax.ShapeDtypeStruct((span, span), WIDE),
         ],
-        [FULL] * 5,
+        [FULL] * 3,
     )
 
 
@@ -204,28 +241,28 @@
 
     def kernel(*refs):
         got = refs[:count]
-        qw_ref, kw_ref, *results = refs[count:]
+        cols_ref, *results = refs[count:]
         for o in range(groups):
             for h in range(hb):
                 c = head_cols(h)
                 q, k, v, g = (
                     jnp.concatenate([r[o, a, :, c] for r in got], axis=0) for a in range(4)
                 )
-                pair = head_states(
-                    q, k, v, g, qw_ref[0, o, :, h : h + 1], kw_ref[0, o, :, h : h + 1]
-                )
+                qw = cols_ref[0, o, :, hb + h : hb + h + 1]
+                kw = cols_ref[0, o, :, 2 * hb + h : 2 * hb + h + 1]
+                pair = head_states(q, k, v, g, qw, kw)
                 for t in range(2):
                     results[o][t, h] = pair[t].astype(results[o].dtype)
 
     piece = pl.BlockSpec((groups, 4, rows, width), lambda i: (0, 0, 0, i))
-    weight = pl.BlockSpec((1, groups, count * rows, hb), lambda i: (w0 // hb + i, 0, 0, 0))
+    weight = pl.BlockSpec((1, groups, count * rows, 3 * hb), lambda i: (w0 // hb + i, 0, 0, 0))
     shape = (2, hw, HEAD_DIM, HEAD_DIM)
     return order.call(
         kernel,
         "states",
         [],
-        [*pieces, decay[2], decay[3]],
-        [piece] * count + [weight] * 2,
+        [*pieces, decay[1]],
+        [piece] * count + [weight],
         [jax.ShapeDtypeStruct(shape, kind) for kind in (WIDE, LOW)[:groups]],
         [pl.BlockSpec((2, hb, HEAD_DIM, HEAD_DIM), lambda i: (0, i, 0, 0))] * groups,
         grid=(hw // hb,),
@@ -332,12 +369,12 @@
     span = count * rows
     width = hb * HEAD_DIM
     aliased = outs is not None
-    cumr, cumc, qw, kw, bias = decay
-    n_in = count + 6
+    cumr, weights, bias = decay
+    n_in = count + 4
 
     def kernel(cols_ref, *refs):
         got = refs[:count]
-        qw_ref, kw_ref, cumc_ref, cumr_ref, bias_ref, st_ref = refs[count:n_in]
+        w_ref, cumr_ref, bias_ref, st_ref = refs[count:n_in]
         results = refs[n_in + (3 if aliased else 0) :]
         kept, sends = results[:3], results[3:]
         for h in range(hb):
@@ -345,9 +382,11 @@
             q, k, v, g = (
                 jnp.concatenate([r[0, a, :, c] for r in got], axis=0) for a in range(4)
             )
-            at = (0, 0, slice(None), slice(h, h + 1))
+            cumc, qw, kw = (
+                w_ref[0, 0, :, j * hb + h : j * hb + h + 1] for j in range(3)
+            )
             outputs = head_grads(
-                q, k, v, g, qw_ref[at], kw_ref[at], cumc_ref[at],
+                q, k, v, g, qw, kw, cumc,
                 cumr_ref[0, 0, h : h + 1, :], bias_ref[...], st_ref[0, h], st_ref[1, h],
             )
             for a, result in enumerate(outputs):
@@ -356,7 +395,7 @@
                     send[a, :, c] = result[(m + 1) * rows : (m + 2) * rows]
 
     piece = pl.BlockSpec((1, 4, rows, width), lambda i, c: (group, 0, 0, i))
-    column = pl.BlockSpec((1, 1, span, hb), lambda i, c: (w0 // hb + i, group, 0, 0))
+    column = pl.BlockSpec((1, 1, span, 3 * hb), lambda i, c: (w0 // hb + i, group, 0, 0))
     row = pl.BlockSpec((1, 1, hb, span), lambda i, c: (w0 // hb + i, group, 0, 0))
     whole = pl.BlockSpec((span, span), lambda i, c: (0, 0))
     state_block = pl.BlockSpec((2, hb, HEAD_DIM, HEAD_DIM), lambda i, c: (0, i, 0, 0))
@@ -364,10 +403,9 @@
         kernel,
         "grads",
         [cols],
-        [*pieces, qw, kw, cumc, cumr, bias, st] + (list(outs) if aliased else []),
+        [*pieces, weights, cumr, bias, st] + (list(outs) if aliased else []),
         [piece] * count
-        + [column] * 3
-        + [row, whole, state_block]
+        + [column, row, whole, state_block]
         + ([ANY] * 3 if aliased else []),
         [jax.ShapeDtypeStruct((rows, full), LOW)] * 3
         + [jax.ShapeDtypeStruct((3, rows, hw * HEAD_DIM), LOW)] * (count - 1),
@@ -496,12 +534,13 @@
         e = self.env
         self.received = [None] * len(self.peers)
         for m in sorted(self.peers, reverse=True):
-            packed = pack(e.order, self.columns(e.z ^ m), e.arrays, self.hw, e.after)
+            first = pack_away if self.w0 == 0 else pack
+            packed = first(e.order, self.columns(e.z ^ m), e.arrays, self.hw)
             self.received[m - 1] = swap(packed, "head", m)
 
     def keep(self):
         e = self.env
-        self.kept = pack(e.order, self.columns(e.z), e.arrays, self.hw, vmem=VMEM)
+        self.kept = pack(e.order, self.columns(e.z), e.arrays, self.hw)
         self.pieces = [self.kept] + self.received
 
     def states(self):
@@ -611,7 +650,6 @@
     e.order = Order()
     e.outs = None
     e.decay = {}
-    e.after = ()
     half = n // 2
     low = z < half
 
@@ -629,7 +667,6 @@
             table.half_if(0, low), on, table.half_if(1, ~low), off,
         )
         e.table = table.build()
-        e.after = (e.table,)
         top = e.levels[-1] if e.levels else dict(base=0, nb=1)
         e.flags = jnp.stack(
             [(table.me >> (top["base"] + j)) & 1 for j in range(top["nb"])]
@@ -647,7 +684,7 @@
 
 
 WAVES = ("P8", "P8")
-STEPS = ("pa", "pb", "ua", "x", "ka", "kb", "sa", "sb", "ba", "va", "fa", "bb", "vb", "ga", "ta", "fb", "gb", "la", "ha", "hb", "la", "lb")
+STEPS = ("pa", "pb", "ua", "x", "ka", "sa", "kb", "sb", "ba", "va", "fa", "bb", "vb", "ga", "ta", "fb", "gb", "la", "ha", "hb", "la", "lb")
 
 
 def schedule(e, heads, prepare):

time: 171 us -> 171 us (level)
  local copies, waits for them, and re-layouts: 7.92 us -> 4.59 us
  starting transfers between devices: 22.7 us -> 25.1 us
    unnamed x40 -> x30, local copies, waits for them, and re-layouts: 6.82 us -> 3.47 us
    ppermute x22, starting transfers between devices: 22.7 us -> 25.1 us  [swap(): lax.ppermute(x, axis, [(i, i ^ bit) for i in range(lax.axis_size(axis))])]
  transfers between devices with their start and end apart: 22 -> 22, of which waited for: 13 -> 12; matrix products, arithmetic and copies ran while one was open for 1% -> 1% of each run, Pallas kernels for 22% -> 22%
where the time goes in v4:
time: 171 us; the launch traced here: 170 us
  waiting for transfers between devices  93.4 us (55%)
  Pallas kernels  44.9 us (26%)
  starting transfers between devices  25.1 us (15%)
  local copies, waits for them, and re-layouts  4.59 us (3%)
    ppermute x22, waiting for transfers between devices, swap(): lax.ppermute(x, axis, [(i, i ^ bit) for i in range(lax.axis_size(axis))])  93.4 us
    pallas_call x22, Pallas kernels, call(): pl.pallas_call(body, grid_spec=pltpu.PrefetchScalarGridSpec(num_scalar_pr...  44.9 us
    ppermute x22, starting transfers between devices, swap(): lax.ppermute(x, axis, [(i, i ^ bit) for i in range(lax.axis_size(axis))])  25.1 us
    unnamed x30, local copies, waits for them, and re-layouts  3.47 us
  transfers between devices with their start and end apart: 22, of which 12 were waited for; matrix products, arithmetic and copies ran while one was open for 1% of the time, Pallas kernels for 22%

profile of v4, /device:TPU:0, one launch (start us, length us, event | category | flops | bytes accessed | tf_op | source)
XLA Modules:
  0.0 170.2 jit_solution(15672692028096525244)
XLA Ops:
  1.3 3.0 %pack.4 = (bf16[2,4,64,1024]{3,2,1,0:T(8,128)(2,1)}, f32[8,128]{1,0:T(8,128)}) custom-call(s32[2]{0:T(128)} %get-tuple-element.144.refs_0_, bf16[64,8192]{1,0:T(8,128)(2,1)} %refs_1_.9, bf16[64,8192]{1,0:T(8,128)(2,1)} %refs_2_.7, bf16[64,8192]{1,0:T(8,128)(2,1)} %refs_3_.7, bf16[64,8192]{1,0:T(8,128)(2,1)} %refs_4_.7), custom_call_target="tpu_custom_call" | custom-call | flops 1 | bytes 1 | tf_op jit(solution)/shard_map/pack/pallas_call | solution.py:67
  4.4 3.1 %collective-permute-start.1 = (bf16[2,4,64,1024]{3,2,1,0:T(8,128)(2,1)}, bf16[2,4,64,1024]{3,2,1,0:T(8,128)(2,1)}, u32[]{:S(2)}, u32[]{:S(2)}) collective-permute-start(bf16[2,4,64,1024]{3,2,1,0:T(8,128)(2,1)} %get-tuple-element.72), channel_id=1, source_target_pairs={{0,1},{1,0},{2,3},{3,2},{4,5},{5,4},{6,7},{7,6},{8,9},{9,8},{10,11... | collective-permute-start | bytes 3145736 | tf_op jit(solution)/shard_map/ppermute | solution.py:29
  7.4 2.6 %collective-permute-start = (f32[16,256]{1,0:T(8,128)S(1)}, f32[16,256]{1,0:T(8,128)S(1)}, u32[]{:S(2)}, u32[]{:S(2)}) collective-permute-start(f32[16,256]{1,0:T(8,128)S(1)} %copy-done.12), channel_id=1, source_target_pairs={{0,2},{1,3},{2,0},{3,1},{4,6},{5,7},{6,4},{7,5},{8,10},{9,11},{10,... | collective-permute-start | bytes 49160 | tf_op jit(solution)/shard_map/ppermute | solution.py:29
  11.3 1.8 %pack.5 = (bf16[2,4,64,1024]{3,2,1,0:T(8,128)(2,1)}, f32[8,128]{1,0:T(8,128)S(1)}) custom-call(s32[2]{0:T(128)S(1)} %get-tuple-element.143.refs_0_, bf16[64,8192]{1,0:T(8,128)(2,1)S(1)} %copy-done, bf16[64,8192]{1,0:T(8,128)(2,1)S(1)} %copy-done.1, bf16[64,8192]{1,0:T(8,128)(2,1)S(1)} %copy-done.2, bf16[64,8192]{1,0:T(8,128)(2,1)S(1)} %copy-done.3, ...), custom_call_target="tpu_custom_call" | custom-call | flops 1 | bytes 1 | tf_op jit(solution)/shard_map/pack/pallas_call | solution.py:67
  15.1 1.6 collective-permute-start.4
  16.7 1.9 %collective-permute-done.4 = f32[2,16]{1,0:T(2,128)S(1)} collective-permute-done((f32[2,16]{1,0:T(2,128)S(1)}, f32[2,16]{1,0:T(2,128)S(1)}, u32[]{:S(2)}, u32[]{:S(2)}) %collective-permute-start.4) | collective-permute-done | bytes 160 | tf_op jit(solution)/shard_map/ppermute | solution.py:29
  18.7 1.6 collective-permute-start.5
  20.3 11.8 %collective-permute-done.1.refs_0_.refs_1_.refs_2_ = bf16[2,4,64,1024]{3,2,1,0:T(8,128)(2,1)} collective-permute-done((bf16[2,4,64,1024]{3,2,1,0:T(8,128)(2,1)}, bf16[2,4,64,1024]{3,2,1,0:T(8,128)(2,1)}, u32[]{:S(2)}, u32[]{:S(2)}) %collective-permute-start.1) | collective-permute-done | bytes 1048608 | tf_op jit(solution)/shard_map/ppermute | solution.py:29
  34.2 3.9 %states.2 = (f32[2,8,128,128]{3,2,1,0:T(8,128)S(1)}, bf16[2,8,128,128]{3,2,1,0:T(8,128)(2,1)}, f32[8,128]{1,0:T(8,128)S(1)}) custom-call(bf16[2,4,64,1024]{3,2,1,0:T(8,128)(2,1)S(1)} %get-tuple-element.76.refs_0_.refs_1_, bf16[2,4,64,1024]{3,2,1,0:T(8,128)(2,1)} %collective-permute-done.1.refs_0_.refs_1_.refs_2_, ...), custom_call_target="tpu_custom_call" | custom-call | flops 1 | bytes 1 | tf_op jit(solution)/shard_map/states/pallas_call | solution.py:67
  39.1 2.8 %collective-permute-start.7 = (bf16[2,8,128,128]{3,2,1,0:T(8,128)(2,1)}, bf16[2,8,128,128]{3,2,1,0:T(8,128)(2,1)}, u32[]{:S(2)}, u32[]{:S(2)}) collective-permute-start(bf16[2,8,128,128]{3,2,1,0:T(8,128)(2,1)} %get-tuple-element.88), channel_id=1, source_target_pairs={{0,2},{1,3},{2,0},{3,1},{4,6},{5,7},{6,4},{7,5},{8,10},{9,11},{10,... | collective-permute-start | bytes 1572872 | tf_op jit(solution)/shard_map/ppermute | solution.py:29
  44.2 20.7 %collective-permute-done.2.refs_1_.refs_2_ = bf16[2,4,64,1024]{3,2,1,0:T(8,128)(2,1)} collective-permute-done((bf16[2,4,64,1024]{3,2,1,0:T(8,128)(2,1)}, bf16[2,4,64,1024]{3,2,1,0:T(8,128)(2,1)}, u32[]{:S(2)}, u32[]{:S(2)}) %collective-permute-start.2) | collective-permute-done | bytes 1048608 | tf_op jit(solution)/shard_map/ppermute | solution.py:29
  65.0 3.0 %states.3 = (f32[2,8,128,128]{3,2,1,0:T(8,128)S(1)}, bf16[2,8,128,128]{3,2,1,0:T(8,128)(2,1)S(1)}, f32[8,128]{1,0:T(8,128)S(1)}) custom-call(bf16[2,4,64,1024]{3,2,1,0:T(8,128)(2,1)S(1)} %get-tuple-element.80.refs_0_.refs_1_, bf16[2,4,64,1024]{3,2,1,0:T(8,128)(2,1)} %collective-permute-done.2.refs_1_.refs_2_, f32[4,2,128,12]{3,2,1,0:T(8,128)S(1)} %copy-done.9, ...), custom_call_target="tpu_custom_call" | custom-call | flops 1 | bytes 1 | tf_op jit(solution)/shard_map/states/pallas_call | solution.py:67
  68.0 1.9 %step.6 = (f32[2,8,128,128]{3,2,1,0:T(8,128)S(1)}, bf16[2,8,128,128]{3,2,1,0:T(8,128)(2,1)S(1)}, f32[8,128]{1,0:T(8,128)S(1)}) custom-call(f32[23,16]{1,0:T(8,128)S(1)} %exponential_select_fusion.refs_0_, s32[2]{0:T(128)S(1)} %pad_add_fusion.1.refs_1_, f32[2,8,128,128]{3,2,1,0:T(8,128)S(1)} %copy-done.7, ...), custom_call_target="tpu_custom_call" | custom-call | flops 1 | bytes 1 | tf_op jit(solution)/shard_map/step/pallas_call | solution.py:67
  70.0 1.9 %collective-permute-start.6 = (bf16[2,8,128,128]{3,2,1,0:T(8,128)(2,1)S(1)}, bf16[2,8,128,128]{3,2,1,0:T(8,128)(2,1)S(1)}, u32[]{:S(2)}, u32[]{:S(2)}) collective-permute-start(bf16[2,8,128,128]{3,2,1,0:T(8,128)(2,1)S(1)} %get-tuple-element.86), channel_id=1, source_target_pairs={{0,2},{1,3},{2,0},{3,1},{4,6},{5,7},{6,4},{7,5},{8,10},{9,11},{10,... | collective-permute-start | bytes 1572872 | tf_op jit(solution)/shard_map/ppermute | solution.py:29
  72.9 1.7 %collective-permute-start.10 = (bf16[8,128,128]{2,1,0:T(8,128)(2,1)S(1)}, bf16[8,128,128]{2,1,0:T(8,128)(2,1)S(1)}, u32[]{:S(2)}, u32[]{:S(2)}) collective-permute-start(bf16[8,128,128]{2,1,0:T(8,128)(2,1)S(1)} %get-tuple-element.94), channel_id=1, source_target_pairs={{0,16},{4,20},{8,24},{12,28},{16,0},{20,4},{24,8},{28,12},{1,17},{... | collective-permute-start | bytes 786440 | tf_op jit(solution)/shard_map/ppermute | solution.py:29
  76.5 10.5 %collective-permute-done.10.refs_3_ = bf16[8,128,128]{2,1,0:T(8,128)(2,1)S(1)} collective-permute-done((bf16[8,128,128]{2,1,0:T(8,128)(2,1)S(1)}, bf16[8,128,128]{2,1,0:T(8,128)(2,1)S(1)}, u32[]{:S(2)}, u32[]{:S(2)}) %collective-permute-start.10) | collective-permute-done | bytes 262176 | tf_op jit(solution)/shard_map/ppermute | solution.py:29
  88.2 2.4 %step.8 = (bf16[2,8,128,128]{3,2,1,0:T(8,128)(2,1)S(1)}, bf16[2,8,128,128]{3,2,1,0:T(8,128)(2,1)S(1)}, f32[8,128]{1,0:T(8,128)S(1)}) custom-call(f32[23,16]{1,0:T(8,128)S(1)} %exponential_select_fusion.refs_0_, s32[2]{0:T(128)S(1)} %pad_add_fusion.1.refs_1_, bf16[8,128,128]{2,1,0:T(8,128)(2,1)S(1)} %collective-permute-done.9.refs_2_, ...), custom_call_target="tpu_custom_call" | custom-call | flops 1 | bytes 1 | tf_op jit(solution)/shard_map/step/pallas_call | solution.py:67
  90.6 5.9 %collective-permute-done.6.refs_3_.refs_6_ = bf16[2,8,128,128]{3,2,1,0:T(8,128)(2,1)S(1)} collective-permute-done((bf16[2,8,128,128]{3,2,1,0:T(8,128)(2,1)S(1)}, bf16[2,8,128,128]{3,2,1,0:T(8,128)(2,1)S(1)}, u32[]{:S(2)}, u32[]{:S(2)}) %collective-permute-start.6) | collective-permute-done | bytes 524320 | tf_op jit(solution)/shard_map/ppermute | solution.py:29
  97.5 1.8 %collective-permute-done.12.refs_3_ = bf16[2,8,128,128]{3,2,1,0:T(8,128)(2,1)S(1)} collective-permute-done((bf16[2,8,128,128]{3,2,1,0:T(8,128)(2,1)S(1)}, bf16[2,8,128,128]{3,2,1,0:T(8,128)(2,1)S(1)}, u32[]{:S(2)}, u32[]{:S(2)}) %collective-permute-start.12) | collective-permute-done | bytes 524320 | tf_op jit(solution)/shard_map/ppermute | solution.py:29
  100.4 1.7 %collective-permute-start.14 = (bf16[8,128,128]{2,1,0:T(8,128)(2,1)S(1)}, bf16[8,128,128]{2,1,0:T(8,128)(2,1)S(1)}, u32[]{:S(2)}, u32[]{:S(2)}) collective-permute-start(bf16[8,128,128]{2,1,0:T(8,128)(2,1)S(1)} %get-tuple-element.102), channel_id=1, source_target_pairs={{0,16},{4,20},{8,24},{12,28},{16,0},{20,4},{24,8},{28,12},{1,17},{... | collective-permute-start | bytes 786440 | tf_op jit(solution)/shard_map/ppermute | solution.py:29
  102.1 1.4 collective-permute-start.15
  103.9 4.4 %grads.4 = (bf16[64,8192]{1,0:T(8,128)(2,1)}, bf16[64,8192]{1,0:T(8,128)(2,1)}, bf16[64,8192]{1,0:T(8,128)(2,1)}, bf16[3,64,1024]{2,1,0:T(8,128)(2,1)S(1)}, f32[8,128]{1,0:T(8,128)S(1)}) custom-call(s32[2]{0:T(128)S(1)} %get-tuple-element.141.refs_0_, bf16[2,4,64,1024]{3,2,1,0:T(8,128)(2,1)S(1)} %copy-done.11, ...), custom_call_target="tpu_custom_call" | custom-call | flops 4000000000 | bytes 1 | tf_op jit(solution)/shard_map/grads/pallas_call | solution.py:67
  108.3 1.5 collective-permute-start.19
  110.4 13.6 %collective-permute-done.16.refs_0_.refs_6_ = bf16[2,8,128,128]{3,2,1,0:T(8,128)(2,1)S(1)} collective-permute-done((bf16[2,8,128,128]{3,2,1,0:T(8,128)(2,1)S(1)}, bf16[2,8,128,128]{3,2,1,0:T(8,128)(2,1)S(1)}, u32[]{:S(2)}, u32[]{:S(2)}) %collective-permute-start.16) | collective-permute-done | bytes 524320 | tf_op jit(solution)/shard_map/ppermute | solution.py:29
  125.5 4.4 %grads.5 = (bf16[64,8192]{1,0:T(8,128)(2,1)}, bf16[64,8192]{1,0:T(8,128)(2,1)}, bf16[64,8192]{1,0:T(8,128)(2,1)}, bf16[3,64,1024]{2,1,0:T(8,128)(2,1)S(1)}, f32[8,128]{1,0:T(8,128)S(1)}) custom-call(s32[2]{0:T(128)S(1)} %get-tuple-element.148.refs_0_, ...), custom_call_target="tpu_custom_call", output_to_operand_aliasing={{0}: (7, {}), {1}: (8, {}), {2}: (9, {})} | custom-call | flops 4000000000 | bytes 1 | tf_op jit(solution)/shard_map/grads/pallas_call | solution.py:67
  129.9 1.7 %collective-permute-start.17 = (bf16[3,64,1024]{2,1,0:T(8,128)(2,1)S(1)}, bf16[3,64,1024]{2,1,0:T(8,128)(2,1)S(1)}, u32[]{:S(2)}, u32[]{:S(2)}) collective-permute-start(bf16[3,64,1024]{2,1,0:T(8,128)(2,1)S(1)} %get-tuple-element.113), channel_id=1, source_target_pairs={{0,1},{1,0},{2,3},{3,2},{4,5},{5,4},{6,7},{7,6},{8,9},{9,8},{10,11... | collective-permute-start | bytes 1179656 | tf_op jit(solution)/shard_map/ppermute | solution.py:29
  132.9 4.4 %grads.6 = (bf16[64,8192]{1,0:T(8,128)(2,1)}, bf16[64,8192]{1,0:T(8,128)(2,1)}, bf16[64,8192]{1,0:T(8,128)(2,1)}, bf16[3,64,1024]{2,1,0:T(8,128)(2,1)S(1)}, f32[8,128]{1,0:T(8,128)S(1)}) custom-call(s32[2]{0:T(128)S(1)} %get-tuple-element.141.refs_0_, ...), custom_call_target="tpu_custom_call", output_to_operand_aliasing={{0}: (7, {}), {1}: (8, {}), {2}: (9, {})} | custom-call | flops 4000000000 | bytes 1 | tf_op jit(solution)/shard_map/grads/pallas_call | solution.py:67
  137.7 12.4 %collective-permute-done.18.refs_6_ = bf16[2,8,128,128]{3,2,1,0:T(8,128)(2,1)S(1)} collective-permute-done((bf16[2,8,128,128]{3,2,1,0:T(8,128)(2,1)S(1)}, bf16[2,8,128,128]{3,2,1,0:T(8,128)(2,1)S(1)}, u32[]{:S(2)}, u32[]{:S(2)}) %collective-permute-start.18) | collective-permute-done | bytes 524320 | tf_op jit(solution)/shard_map/ppermute | solution.py:29
  150.1 4.4 %grads.7 = (bf16[64,8192]{1,0:T(8,128)(2,1)}, bf16[64,8192]{1,0:T(8,128)(2,1)}, bf16[64,8192]{1,0:T(8,128)(2,1)}, bf16[3,64,1024]{2,1,0:T(8,128)(2,1)S(1)}, f32[8,128]{1,0:T(8,128)S(1)}) custom-call(s32[2]{0:T(128)S(1)} %get-tuple-element.148.refs_0_, ...), custom_call_target="tpu_custom_call", output_to_operand_aliasing={{0}: (7, {}), {1}: (8, {}), {2}: (9, {})} | custom-call | flops 4000000000 | bytes 1 | tf_op jit(solution)/shard_map/grads/pallas_call | solution.py:67
  154.5 7.0 %collective-permute-done.21.refs_1_ = bf16[3,64,1024]{2,1,0:T(8,128)(2,1)S(1)} collective-permute-done((bf16[3,64,1024]{2,1,0:T(8,128)(2,1)S(1)}, bf16[3,64,1024]{2,1,0:T(8,128)(2,1)S(1)}, u32[]{:S(2)}, u32[]{:S(2)}) %collective-permute-start.21) | collective-permute-done | bytes 393248 | tf_op jit(solution)/shard_map/ppermute | solution.py:29
  162.9 5.9 %collective-permute-done.20.refs_2_ = bf16[3,64,1024]{2,1,0:T(8,128)(2,1)S(1)} collective-permute-done((bf16[3,64,1024]{2,1,0:T(8,128)(2,1)S(1)}, bf16[3,64,1024]{2,1,0:T(8,128)(2,1)S(1)}, u32[]{:S(2)}, u32[]{:S(2)}) %collective-permute-start.20) | collective-permute-done | bytes 393248 | tf_op jit(solution)/shard_map/ppermute | solution.py:29
  168.8 1.5 place.5
  (88 shorter events, 20.9 us)
Async XLA Ops:
  1.3 6.2 %copy-start.12 = (f32[16,256]{1,0:T(8,128)S(1)}, f32[16,256]{1,0:T(8,128)}, u32[]{:S(2)}) copy-start(f32[16,256]{1,0:T(8,128)} %refs_1_.7) | copy-start | bytes 49156
  1.3 8.7 %copy-start = (bf16[64,8192]{1,0:T(8,128)(2,1)S(1)}, bf16[64,8192]{1,0:T(8,128)(2,1)}, u32[]{:S(2)}) copy-start(bf16[64,8192]{1,0:T(8,128)(2,1)} %refs_1_.9) | copy-start | bytes 3145732
  1.3 8.7 %copy-start.1 = (bf16[64,8192]{1,0:T(8,128)(2,1)S(1)}, bf16[64,8192]{1,0:T(8,128)(2,1)}, u32[]{:S(2)}) copy-start(bf16[64,8192]{1,0:T(8,128)(2,1)} %refs_2_.7) | copy-start | bytes 3145732
  1.3 8.7 %copy-start.2 = (bf16[64,8192]{1,0:T(8,128)(2,1)S(1)}, bf16[64,8192]{1,0:T(8,128)(2,1)}, u32[]{:S(2)}) copy-start(bf16[64,8192]{1,0:T(8,128)(2,1)} %refs_3_.7) | copy-start | bytes 3145732
  4.3 5.7 %copy-start.13 = (f32[8,128]{1,0:T(8,128)S(1)}, f32[8,128]{1,0:T(8,128)}, u32[]{:S(2)}) copy-start(f32[8,128]{1,0:T(8,128)} %get-tuple-element.73.refs_5_) | copy-start | bytes 12292
  4.4 27.7 %collective-permute-start.1 = (bf16[2,4,64,1024]{3,2,1,0:T(8,128)(2,1)}, bf16[2,4,64,1024]{3,2,1,0:T(8,128)(2,1)}, u32[]{:S(2)}, u32[]{:S(2)}) collective-permute-start(bf16[2,4,64,1024]{3,2,1,0:T(8,128)(2,1)} %get-tuple-element.72), channel_id=1, source_target_pairs={{0,1},{1,0},{2,3},{3,2},{4,5},{5,4},{6,7},{7,6},{8,9},{9,8},{10,11... | collective-permute-start | bytes 3145736 | tf_op jit(solution)/shard_map/ppermute | solution.py:29
  7.4 24.7 %collective-permute-start = (f32[16,256]{1,0:T(8,128)S(1)}, f32[16,256]{1,0:T(8,128)S(1)}, u32[]{:S(2)}, u32[]{:S(2)}) collective-permute-start(f32[16,256]{1,0:T(8,128)S(1)} %copy-done.12), channel_id=1, source_target_pairs={{0,2},{1,3},{2,0},{3,1},{4,6},{5,7},{6,4},{7,5},{8,10},{9,11},{10,... | collective-permute-start | bytes 49160 | tf_op jit(solution)/shard_map/ppermute | solution.py:29
  13.1 51.9 %collective-permute-start.2 = (bf16[2,4,64,1024]{3,2,1,0:T(8,128)(2,1)}, bf16[2,4,64,1024]{3,2,1,0:T(8,128)(2,1)}, u32[]{:S(2)}, u32[]{:S(2)}) collective-permute-start(bf16[2,4,64,1024]{3,2,1,0:T(8,128)(2,1)} %get-tuple-element.81), channel_id=1, source_target_pairs={{0,1},{1,0},{2,3},{3,2},{4,5},{5,4},{6,7},{7,6},{8,9},{9,8},{10,11... | collective-permute-start | bytes 3145736 | tf_op jit(solution)/shard_map/ppermute | solution.py:29
  13.9 1.2 collective-permute-start.3
  15.1 3.6 %collective-permute-start.4 = (f32[2,16]{1,0:T(2,128)S(1)}, f32[2,16]{1,0:T(2,128)S(1)}, u32[]{:S(2)}, u32[]{:S(2)}) collective-permute-start(f32[2,16]{1,0:T(2,128)S(1)} %maximum_select_fusion.2), channel_id=1, source_target_pairs={{0,8},{4,12},{8,0},{12,4},{16,24},{20,28},{24,16},{28,20},{1,9},{5... | collective-permute-start | bytes 392 | tf_op jit(solution)/shard_map/ppermute | solution.py:29
  16.7 16.6 %copy-start.4 = (bf16[64,8192]{1,0:T(8,128)(2,1)S(1)}, bf16[64,8192]{1,0:T(8,128)(2,1)}, u32[]{:S(2)}) copy-start(bf16[64,8192]{1,0:T(8,128)(2,1)} %refs_4_.7) | copy-start | bytes 3145732
  18.7 23.2 %collective-permute-start.5 = (f32[4,16]{1,0:T(4,128)S(1)}, f32[4,16]{1,0:T(4,128)S(1)}, u32[]{:S(2)}, u32[]{:S(2)}) collective-permute-start(f32[4,16]{1,0:T(4,128)S(1)} %maximum_select_fusion.1), channel_id=1, source_target_pairs={{0,16},{4,20},{8,24},{12,28},{16,0},{20,4},{24,8},{28,12},{1,17},{... | collective-permute-start | bytes 776 | tf_op jit(solution)/shard_map/ppermute | solution.py:29
  34.2 3.9 %copy-start.10 = (bf16[2,4,64,1024]{3,2,1,0:T(8,128)(2,1)}, bf16[2,4,64,1024]{3,2,1,0:T(8,128)(2,1)S(1)}, u32[]{:S(2)}) copy-start(bf16[2,4,64,1024]{3,2,1,0:T(8,128)(2,1)S(1)} %get-tuple-element.76.refs_0_.refs_1_) | copy-start | bytes 3145732
  39.1 28.9 %collective-permute-start.7 = (bf16[2,8,128,128]{3,2,1,0:T(8,128)(2,1)}, bf16[2,8,128,128]{3,2,1,0:T(8,128)(2,1)}, u32[]{:S(2)}, u32[]{:S(2)}) collective-permute-start(bf16[2,8,128,128]{3,2,1,0:T(8,128)(2,1)} %get-tuple-element.88), channel_id=1, source_target_pairs={{0,2},{1,3},{2,0},{3,1},{4,6},{5,7},{6,4},{7,5},{8,10},{9,11},{10,... | collective-permute-start | bytes 1572872 | tf_op jit(solution)/shard_map/ppermute | solution.py:29
  43.4 21.5 %copy-start.9 = (f32[4,2,128,12]{3,2,1,0:T(8,128)S(1)}, f32[4,2,128,12]{3,2,1,0:T(8,128)}, u32[]{:S(2)}) copy-start(f32[4,2,128,12]{3,2,1,0:T(8,128)} %copy-done.8) | copy-start | bytes 147460
  65.0 3.0 %copy-start.7 = (f32[2,8,128,128]{3,2,1,0:T(8,128)S(1)}, f32[2,8,128,128]{3,2,1,0:T(8,128)}, u32[]{:S(2)}) copy-start(f32[2,8,128,128]{3,2,1,0:T(8,128)} %copy-done.6) | copy-start | bytes 3145732
  69.9 2.0 %collective-permute-start.8 = (bf16[2,8,128,128]{3,2,1,0:T(8,128)(2,1)S(1)}, bf16[2,8,128,128]{3,2,1,0:T(8,128)(2,1)S(1)}, u32[]{:S(2)}, u32[]{:S(2)}) collective-permute-start(bf16[2,8,128,128]{3,2,1,0:T(8,128)(2,1)S(1)} %get-tuple-element.91), channel_id=1, source_target_pairs={{0,4},{4,0},{8,12},{12,8},{16,20},{20,16},{24,28},{28,24},{1,5},{5... | collective-permute-start | bytes 1572872 | tf_op jit(solution)/shard_map/ppermute | solution.py:29
  70.0 26.5 %collective-permute-start.6 = (bf16[2,8,128,128]{3,2,1,0:T(8,128)(2,1)S(1)}, bf16[2,8,128,128]{3,2,1,0:T(8,128)(2,1)S(1)}, u32[]{:S(2)}, u32[]{:S(2)}) collective-permute-start(bf16[2,8,128,128]{3,2,1,0:T(8,128)(2,1)S(1)} %get-tuple-element.86), channel_id=1, source_target_pairs={{0,2},{1,3},{2,0},{3,1},{4,6},{5,7},{6,4},{7,5},{8,10},{9,11},{10,... | collective-permute-start | bytes 1572872 | tf_op jit(solution)/shard_map/ppermute | solution.py:29
  72.9 14.1 %collective-permute-start.10 = (bf16[8,128,128]{2,1,0:T(8,128)(2,1)S(1)}, bf16[8,128,128]{2,1,0:T(8,128)(2,1)S(1)}, u32[]{:S(2)}, u32[]{:S(2)}) collective-permute-start(bf16[8,128,128]{2,1,0:T(8,128)(2,1)S(1)} %get-tuple-element.94), channel_id=1, source_target_pairs={{0,16},{4,20},{8,24},{12,28},{16,0},{20,4},{24,8},{28,12},{1,17},{... | collective-permute-start | bytes 786440 | tf_op jit(solution)/shard_map/ppermute | solution.py:29
  74.6 12.3 %collective-permute-start.11 = (bf16[8,128,128]{2,1,0:T(8,128)(2,1)S(1)}, bf16[8,128,128]{2,1,0:T(8,128)(2,1)S(1)}, u32[]{:S(2)}, u32[]{:S(2)}) collective-permute-start(bf16[8,128,128]{2,1,0:T(8,128)(2,1)S(1)} %get-tuple-element.94), channel_id=1, source_target_pairs={{0,24},{4,28},{8,16},{12,20},{16,8},{20,12},{24,0},{28,4},{1,25},{... | collective-permute-start | bytes 786440 | tf_op jit(solution)/shard_map/ppermute | solution.py:29
  76.1 12.1 %collective-permute-start.9 = (bf16[8,128,128]{2,1,0:T(8,128)(2,1)S(1)}, bf16[8,128,128]{2,1,0:T(8,128)(2,1)S(1)}, u32[]{:S(2)}, u32[]{:S(2)}) collective-permute-start(bf16[8,128,128]{2,1,0:T(8,128)(2,1)S(1)} %get-tuple-element.93), channel_id=1, source_target_pairs={{0,8},{4,12},{8,0},{12,4},{16,24},{20,28},{24,16},{28,20},{1,9},{5... | collective-permute-start | bytes 786440 | tf_op jit(solution)/shard_map/ppermute | solution.py:29
  97.4 6.6 %copy-start.11 = (bf16[2,4,64,1024]{3,2,1,0:T(8,128)(2,1)S(1)}, bf16[2,4,64,1024]{3,2,1,0:T(8,128)(2,1)}, u32[]{:S(2)}) copy-start(bf16[2,4,64,1024]{3,2,1,0:T(8,128)(2,1)} %copy-done.10) | copy-start | bytes 3145732
  97.4 2.0 %collective-permute-start.12 = (bf16[2,8,128,128]{3,2,1,0:T(8,128)(2,1)S(1)}, bf16[2,8,128,128]{3,2,1,0:T(8,128)(2,1)S(1)}, u32[]{:S(2)}, u32[]{:S(2)}) collective-permute-start(bf16[2,8,128,128]{3,2,1,0:T(8,128)(2,1)S(1)} %get-tuple-element.99), channel_id=1, source_target_pairs={{0,4},{4,0},{8,12},{12,8},{16,20},{20,16},{24,28},{28,24},{1,5},{5... | collective-permute-start | bytes 1572872 | tf_op jit(solution)/shard_map/ppermute | solution.py:29
  97.5 26.6 %collective-permute-start.16 = (bf16[2,8,128,128]{3,2,1,0:T(8,128)(2,1)S(1)}, bf16[2,8,128,128]{3,2,1,0:T(8,128)(2,1)S(1)}, u32[]{:S(2)}, u32[]{:S(2)}) collective-permute-start(bf16[2,8,128,128]{3,2,1,0:T(8,128)(2,1)S(1)} %get-tuple-element.104), channel_id=1, source_target_pairs={{0,2},{1,3},{2,0},{3,1},{4,6},{5,7},{6,4},{7,5},{8,10},{9,11},{10,... | collective-permute-start | bytes 1572872 | tf_op jit(solution)/shard_map/ppermute | solution.py:29
  100.4 23.7 %collective-permute-start.14 = (bf16[8,128,128]{2,1,0:T(8,128)(2,1)S(1)}, bf16[8,128,128]{2,1,0:T(8,128)(2,1)S(1)}, u32[]{:S(2)}, u32[]{:S(2)}) collective-permute-start(bf16[8,128,128]{2,1,0:T(8,128)(2,1)S(1)} %get-tuple-element.102), channel_id=1, source_target_pairs={{0,16},{4,20},{8,24},{12,28},{16,0},{20,4},{24,8},{28,12},{1,17},{... | collective-permute-start | bytes 786440 | tf_op jit(solution)/shard_map/ppermute | solution.py:29
  102.1 21.9 %collective-permute-start.15 = (bf16[8,128,128]{2,1,0:T(8,128)(2,1)S(1)}, bf16[8,128,128]{2,1,0:T(8,128)(2,1)S(1)}, u32[]{:S(2)}, u32[]{:S(2)}) collective-permute-start(bf16[8,128,128]{2,1,0:T(8,128)(2,1)S(1)} %get-tuple-element.102), channel_id=1, source_target_pairs={{0,24},{4,28},{8,16},{12,20},{16,8},{20,12},{24,0},{28,4},{1,25},{... | collective-permute-start | bytes 786440 | tf_op jit(solution)/shard_map/ppermute | solution.py:29
  103.5 20.5 %collective-permute-start.13 = (bf16[8,128,128]{2,1,0:T(8,128)(2,1)S(1)}, bf16[8,128,128]{2,1,0:T(8,128)(2,1)S(1)}, u32[]{:S(2)}, u32[]{:S(2)}) collective-permute-start(bf16[8,128,128]{2,1,0:T(8,128)(2,1)S(1)} %get-tuple-element.101), channel_id=1, source_target_pairs={{0,8},{4,12},{8,0},{12,4},{16,24},{20,28},{24,16},{28,20},{1,9},{5... | collective-permute-start | bytes 786440 | tf_op jit(solution)/shard_map/ppermute | solution.py:29
  108.3 23.3 %collective-permute-start.19 = (bf16[3,64,1024]{2,1,0:T(8,128)(2,1)S(1)}, bf16[3,64,1024]{2,1,0:T(8,128)(2,1)S(1)}, u32[]{:S(2)}, u32[]{:S(2)}) collective-permute-start(bf16[3,64,1024]{2,1,0:T(8,128)(2,1)S(1)} %get-tuple-element.115), channel_id=1, source_target_pairs={{0,1},{1,0},{2,3},{3,2},{4,5},{5,4},{6,7},{7,6},{8,9},{9,8},{10,11... | collective-permute-start | bytes 1179656 | tf_op jit(solution)/shard_map/ppermute | solution.py:29
  125.4 24.7 %collective-permute-start.18 = (bf16[2,8,128,128]{3,2,1,0:T(8,128)(2,1)S(1)}, bf16[2,8,128,128]{3,2,1,0:T(8,128)(2,1)S(1)}, u32[]{:S(2)}, u32[]{:S(2)}) collective-permute-start(bf16[2,8,128,128]{3,2,1,0:T(8,128)(2,1)S(1)} %get-tuple-element.114), channel_id=1, source_target_pairs={{0,2},{1,3},{2,0},{3,1},{4,6},{5,7},{6,4},{7,5},{8,10},{9,11},{10,... | collective-permute-start | bytes 1572872 | tf_op jit(solution)/shard_map/ppermute | solution.py:29
  129.9 33.0 %collective-permute-start.17 = (bf16[3,64,1024]{2,1,0:T(8,128)(2,1)S(1)}, bf16[3,64,1024]{2,1,0:T(8,128)(2,1)S(1)}, u32[]{:S(2)}, u32[]{:S(2)}) collective-permute-start(bf16[3,64,1024]{2,1,0:T(8,128)(2,1)S(1)} %get-tuple-element.113), channel_id=1, source_target_pairs={{0,1},{1,0},{2,3},{3,2},{4,5},{5,4},{6,7},{7,6},{8,9},{9,8},{10,11... | collective-permute-start | bytes 1179656 | tf_op jit(solution)/shard_map/ppermute | solution.py:29
  137.3 24.1 %collective-permute-start.21 = (bf16[3,64,1024]{2,1,0:T(8,128)(2,1)S(1)}, bf16[3,64,1024]{2,1,0:T(8,128)(2,1)S(1)}, u32[]{:S(2)}, u32[]{:S(2)}) collective-permute-start(bf16[3,64,1024]{2,1,0:T(8,128)(2,1)S(1)} %get-tuple-element.129), channel_id=1, source_target_pairs={{0,1},{1,0},{2,3},{3,2},{4,5},{5,4},{6,7},{7,6},{8,9},{9,8},{10,11... | collective-permute-start | bytes 1179656 | tf_op jit(solution)/shard_map/ppermute | solution.py:29
  154.5 14.3 %collective-permute-start.20 = (bf16[3,64,1024]{2,1,0:T(8,128)(2,1)S(1)}, bf16[3,64,1024]{2,1,0:T(8,128)(2,1)S(1)}, u32[]{:S(2)}, u32[]{:S(2)}) collective-permute-start(bf16[3,64,1024]{2,1,0:T(8,128)(2,1)S(1)} %get-tuple-element.128), channel_id=1, source_target_pairs={{0,1},{1,0},{2,3},{3,2},{4,5},{5,4},{6,7},{7,6},{8,9},{9,8},{10,11... | collective-permute-start | bytes 1179656 | tf_op jit(solution)/shard_map/ppermute | solution.py:29
  (5 other events, 5.8 us)

commit v5 on v4

--- a/solution.py
+++ b/solution.py
@@ -132,17 +132,19 @@
     return packed
 
 
-def pack_away(order, target, arrays, hw):
+def pack_away(order, wave, m, arrays, hw):
     rows = arrays[0].shape[0]
     width = hw * HEAD_DIM
-    groups = target.shape[0]
+    groups = 2
+    half, heads, w0 = wave.env.n // 2, wave.env.heads, wave.w0
     shape = (groups, 4, rows, width)
 
-    def kernel(at_ref, *refs):
+    def kernel(*refs):
+        device = lax.axis_index("head") ^ m
         ins, out, buffer, sems = refs[:4], refs[4], refs[5], refs[6]
         loads, stores = [], []
         for o in range(groups):
-            columns = pl.ds(pl.multiple_of(at_ref[o] * HEAD_DIM, HEAD_DIM), width)
+            columns = pl.ds(pl.multiple_of(((device ^ (o * half)) * heads + w0) * HEAD_DIM, HEAD_DIM), width)
             for a, ref in enumerate(ins):
                 n = len(loads)
                 loads.append(
@@ -162,7 +164,7 @@
     (packed,) = order.call(
         kernel,
         "pack",
-        [target],
+        [],
         arrays,
         [ANY] * 4,
         [jax.ShapeDtypeStruct(shape, LOW)],
@@ -534,8 +536,10 @@
         e = self.env
         self.received = [None] * len(self.peers)
         for m in sorted(self.peers, reverse=True):
-            first = pack_away if self.w0 == 0 else pack
-            packed = first(e.order, self.columns(e.z ^ m), e.arrays, self.hw)
+            if self.w0 == 0:
+                packed = pack_away(e.order, self, m, e.arrays, self.hw)
+            else:
+                packed = pack(e.order, self.columns(e.z ^ m), e.arrays, self.hw)
             self.received[m - 1] = swap(packed, "head", m)
 
     def keep(self):

time: 171 us -> 169 us (0.988)
    unnamed x30 -> x28, local copies, waits for them, and re-layouts: 3.47 us -> 4.07 us
where the time goes in v5:
time: 169 us
  waiting for transfers between devices  92.7 us (55%)
  Pallas kernels  44.2 us (26%)
  starting transfers between devices  25.1 us (15%)
  local copies, waits for them, and re-layouts  5.15 us (3%)
    ppermute x22, waiting for transfers between devices, swap(): lax.ppermute(x, axis, [(i, i ^ bit) for i in range(lax.axis_size(axis))])  92.7 us
    pallas_call x22, Pallas kernels, call(): pl.pallas_call(body, grid_spec=pltpu.PrefetchScalarGridSpec(num_scalar_pr...  44.2 us
    ppermute x22, starting transfers between devices, swap(): lax.ppermute(x, axis, [(i, i ^ bit) for i in range(lax.axis_size(axis))])  25.1 us
    unnamed x28, local copies, waits for them, and re-layouts  4.07 us
  transfers between devices with their start and end apart: 22, of which 12 were waited for; matrix products, arithmetic and copies ran while one was open for 1% of the time, Pallas kernels for 22%

profile of v5, /device:TPU:0, one launch (start us, length us, event | category | flops | bytes accessed | tf_op | source)
XLA Modules:
  0.0 168.8 jit_solution(10321849086658675942)
XLA Ops:
  0.7 2.2 %pack.4 = (bf16[2,4,64,1024]{3,2,1,0:T(8,128)(2,1)}, f32[8,128]{1,0:T(8,128)}) custom-call(bf16[64,8192]{1,0:T(8,128)(2,1)} %refs_1_.9, bf16[64,8192]{1,0:T(8,128)(2,1)} %refs_2_.7, bf16[64,8192]{1,0:T(8,128)(2,1)} %refs_3_.7, bf16[64,8192]{1,0:T(8,128)(2,1)} %refs_4_.5), custom_call_target="tpu_custom_call" | custom-call | flops 1 | bytes 1 | tf_op jit(solution)/shard_map/pack/pallas_call | solution.py:67
  2.9 3.1 %collective-permute-start.1 = (bf16[2,4,64,1024]{3,2,1,0:T(8,128)(2,1)}, bf16[2,4,64,1024]{3,2,1,0:T(8,128)(2,1)}, u32[]{:S(2)}, u32[]{:S(2)}) collective-permute-start(bf16[2,4,64,1024]{3,2,1,0:T(8,128)(2,1)} %get-tuple-element.72), channel_id=1, source_target_pairs={{0,1},{1,0},{2,3},{3,2},{4,5},{5,4},{6,7},{7,6},{8,9},{9,8},{10,11... | collective-permute-start | bytes 3145736 | tf_op jit(solution)/shard_map/ppermute | solution.py:29
  6.0 2.6 %collective-permute-start = (f32[16,256]{1,0:T(8,128)S(1)}, f32[16,256]{1,0:T(8,128)S(1)}, u32[]{:S(2)}, u32[]{:S(2)}) collective-permute-start(f32[16,256]{1,0:T(8,128)S(1)} %copy-done.12), channel_id=1, source_target_pairs={{0,2},{1,3},{2,0},{3,1},{4,6},{5,7},{6,4},{7,5},{8,10},{9,11},{10,... | collective-permute-start | bytes 49160 | tf_op jit(solution)/shard_map/ppermute | solution.py:29
  10.5 1.8 %pack.5 = (bf16[2,4,64,1024]{3,2,1,0:T(8,128)(2,1)}, f32[8,128]{1,0:T(8,128)S(1)}) custom-call(s32[2]{0:T(128)S(1)} %get-tuple-element.143.refs_0_, bf16[64,8192]{1,0:T(8,128)(2,1)S(1)} %copy-done, bf16[64,8192]{1,0:T(8,128)(2,1)S(1)} %copy-done.1, bf16[64,8192]{1,0:T(8,128)(2,1)S(1)} %copy-done.2, bf16[64,8192]{1,0:T(8,128)(2,1)S(1)} %copy-done.3, ...), custom_call_target="tpu_custom_call" | custom-call | flops 1 | bytes 1 | tf_op jit(solution)/shard_map/pack/pallas_call | solution.py:67
  14.3 1.6 collective-permute-start.4
  16.0 1.9 %collective-permute-done.4 = f32[2,16]{1,0:T(2,128)S(1)} collective-permute-done((f32[2,16]{1,0:T(2,128)S(1)}, f32[2,16]{1,0:T(2,128)S(1)}, u32[]{:S(2)}, u32[]{:S(2)}) %collective-permute-start.4) | collective-permute-done | bytes 160 | tf_op jit(solution)/shard_map/ppermute | solution.py:29
  17.9 1.6 collective-permute-start.5
  19.5 11.1 %collective-permute-done.1.refs_0_.refs_1_.refs_2_ = bf16[2,4,64,1024]{3,2,1,0:T(8,128)(2,1)} collective-permute-done((bf16[2,4,64,1024]{3,2,1,0:T(8,128)(2,1)}, bf16[2,4,64,1024]{3,2,1,0:T(8,128)(2,1)}, u32[]{:S(2)}, u32[]{:S(2)}) %collective-permute-start.1) | collective-permute-done | bytes 1048608 | tf_op jit(solution)/shard_map/ppermute | solution.py:29
  32.8 3.9 %states.2 = (f32[2,8,128,128]{3,2,1,0:T(8,128)S(1)}, bf16[2,8,128,128]{3,2,1,0:T(8,128)(2,1)}, f32[8,128]{1,0:T(8,128)S(1)}) custom-call(bf16[2,4,64,1024]{3,2,1,0:T(8,128)(2,1)S(1)} %get-tuple-element.76.refs_0_.refs_1_, bf16[2,4,64,1024]{3,2,1,0:T(8,128)(2,1)} %collective-permute-done.1.refs_0_.refs_1_.refs_2_, ...), custom_call_target="tpu_custom_call" | custom-call | flops 1 | bytes 1 | tf_op jit(solution)/shard_map/states/pallas_call | solution.py:67
  37.6 2.8 %collective-permute-start.7 = (bf16[2,8,128,128]{3,2,1,0:T(8,128)(2,1)}, bf16[2,8,128,128]{3,2,1,0:T(8,128)(2,1)}, u32[]{:S(2)}, u32[]{:S(2)}) collective-permute-start(bf16[2,8,128,128]{3,2,1,0:T(8,128)(2,1)} %get-tuple-element.88), channel_id=1, source_target_pairs={{0,2},{1,3},{2,0},{3,1},{4,6},{5,7},{6,4},{7,5},{8,10},{9,11},{10,... | collective-permute-start | bytes 1572872 | tf_op jit(solution)/shard_map/ppermute | solution.py:29
  42.8 20.7 %collective-permute-done.2.refs_1_.refs_2_ = bf16[2,4,64,1024]{3,2,1,0:T(8,128)(2,1)} collective-permute-done((bf16[2,4,64,1024]{3,2,1,0:T(8,128)(2,1)}, bf16[2,4,64,1024]{3,2,1,0:T(8,128)(2,1)}, u32[]{:S(2)}, u32[]{:S(2)}) %collective-permute-start.2) | collective-permute-done | bytes 1048608 | tf_op jit(solution)/shard_map/ppermute | solution.py:29
  63.5 3.0 %states.3 = (f32[2,8,128,128]{3,2,1,0:T(8,128)S(1)}, bf16[2,8,128,128]{3,2,1,0:T(8,128)(2,1)S(1)}, f32[8,128]{1,0:T(8,128)S(1)}) custom-call(bf16[2,4,64,1024]{3,2,1,0:T(8,128)(2,1)S(1)} %get-tuple-element.80.refs_0_.refs_1_, bf16[2,4,64,1024]{3,2,1,0:T(8,128)(2,1)} %collective-permute-done.2.refs_1_.refs_2_, f32[4,2,128,12]{3,2,1,0:T(8,128)S(1)} %copy-done.9, ...), custom_call_target="tpu_custom_call" | custom-call | flops 1 | bytes 1 | tf_op jit(solution)/shard_map/states/pallas_call | solution.py:67
  66.5 1.9 %step.6 = (f32[2,8,128,128]{3,2,1,0:T(8,128)S(1)}, bf16[2,8,128,128]{3,2,1,0:T(8,128)(2,1)S(1)}, f32[8,128]{1,0:T(8,128)S(1)}) custom-call(f32[23,16]{1,0:T(8,128)S(1)} %exponential_select_fusion.refs_0_, s32[2]{0:T(128)S(1)} %pad_add_fusion.1.refs_1_, f32[2,8,128,128]{3,2,1,0:T(8,128)S(1)} %copy-done.7, ...), custom_call_target="tpu_custom_call" | custom-call | flops 1 | bytes 1 | tf_op jit(solution)/shard_map/step/pallas_call | solution.py:67
  68.6 1.9 %collective-permute-start.6 = (bf16[2,8,128,128]{3,2,1,0:T(8,128)(2,1)S(1)}, bf16[2,8,128,128]{3,2,1,0:T(8,128)(2,1)S(1)}, u32[]{:S(2)}, u32[]{:S(2)}) collective-permute-start(bf16[2,8,128,128]{3,2,1,0:T(8,128)(2,1)S(1)} %get-tuple-element.86), channel_id=1, source_target_pairs={{0,2},{1,3},{2,0},{3,1},{4,6},{5,7},{6,4},{7,5},{8,10},{9,11},{10,... | collective-permute-start | bytes 1572872 | tf_op jit(solution)/shard_map/ppermute | solution.py:29
  71.5 1.7 %collective-permute-start.10 = (bf16[8,128,128]{2,1,0:T(8,128)(2,1)S(1)}, bf16[8,128,128]{2,1,0:T(8,128)(2,1)S(1)}, u32[]{:S(2)}, u32[]{:S(2)}) collective-permute-start(bf16[8,128,128]{2,1,0:T(8,128)(2,1)S(1)} %get-tuple-element.94), channel_id=1, source_target_pairs={{0,16},{4,20},{8,24},{12,28},{16,0},{20,4},{24,8},{28,12},{1,17},{... | collective-permute-start | bytes 786440 | tf_op jit(solution)/shard_map/ppermute | solution.py:29
  73.2 1.4 collective-permute-start.11
  75.0 10.5 %collective-permute-done.10.refs_3_ = bf16[8,128,128]{2,1,0:T(8,128)(2,1)S(1)} collective-permute-done((bf16[8,128,128]{2,1,0:T(8,128)(2,1)S(1)}, bf16[8,128,128]{2,1,0:T(8,128)(2,1)S(1)}, u32[]{:S(2)}, u32[]{:S(2)}) %collective-permute-start.10) | collective-permute-done | bytes 262176 | tf_op jit(solution)/shard_map/ppermute | solution.py:29
  86.8 2.4 %step.8 = (bf16[2,8,128,128]{3,2,1,0:T(8,128)(2,1)S(1)}, bf16[2,8,128,128]{3,2,1,0:T(8,128)(2,1)S(1)}, f32[8,128]{1,0:T(8,128)S(1)}) custom-call(f32[23,16]{1,0:T(8,128)S(1)} %exponential_select_fusion.refs_0_, s32[2]{0:T(128)S(1)} %pad_add_fusion.1.refs_1_, bf16[8,128,128]{2,1,0:T(8,128)(2,1)S(1)} %collective-permute-done.9.refs_2_, ...), custom_call_target="tpu_custom_call" | custom-call | flops 1 | bytes 1 | tf_op jit(solution)/shard_map/step/pallas_call | solution.py:67
  89.2 5.9 %collective-permute-done.6.refs_3_.refs_6_ = bf16[2,8,128,128]{3,2,1,0:T(8,128)(2,1)S(1)} collective-permute-done((bf16[2,8,128,128]{3,2,1,0:T(8,128)(2,1)S(1)}, bf16[2,8,128,128]{3,2,1,0:T(8,128)(2,1)S(1)}, u32[]{:S(2)}, u32[]{:S(2)}) %collective-permute-start.6) | collective-permute-done | bytes 524320 | tf_op jit(solution)/shard_map/ppermute | solution.py:29
  96.1 1.8 %collective-permute-done.12.refs_3_ = bf16[2,8,128,128]{3,2,1,0:T(8,128)(2,1)S(1)} collective-permute-done((bf16[2,8,128,128]{3,2,1,0:T(8,128)(2,1)S(1)}, bf16[2,8,128,128]{3,2,1,0:T(8,128)(2,1)S(1)}, u32[]{:S(2)}, u32[]{:S(2)}) %collective-permute-start.12) | collective-permute-done | bytes 524320 | tf_op jit(solution)/shard_map/ppermute | solution.py:29
  98.9 1.8 %collective-permute-start.14 = (bf16[8,128,128]{2,1,0:T(8,128)(2,1)S(1)}, bf16[8,128,128]{2,1,0:T(8,128)(2,1)S(1)}, u32[]{:S(2)}, u32[]{:S(2)}) collective-permute-start(bf16[8,128,128]{2,1,0:T(8,128)(2,1)S(1)} %get-tuple-element.102), channel_id=1, source_target_pairs={{0,16},{4,20},{8,24},{12,28},{16,0},{20,4},{24,8},{28,12},{1,17},{... | collective-permute-start | bytes 786440 | tf_op jit(solution)/shard_map/ppermute | solution.py:29
  102.5 4.4 %grads.4 = (bf16[64,8192]{1,0:T(8,128)(2,1)}, bf16[64,8192]{1,0:T(8,128)(2,1)}, bf16[64,8192]{1,0:T(8,128)(2,1)}, bf16[3,64,1024]{2,1,0:T(8,128)(2,1)S(1)}, f32[8,128]{1,0:T(8,128)S(1)}) custom-call(s32[2]{0:T(128)S(1)} %get-tuple-element.141.refs_0_, bf16[2,4,64,1024]{3,2,1,0:T(8,128)(2,1)S(1)} %copy-done.11, ...), custom_call_target="tpu_custom_call" | custom-call | flops 4000000000 | bytes 1 | tf_op jit(solution)/shard_map/grads/pallas_call | solution.py:67
  106.9 1.5 collective-permute-start.19
  109.0 13.6 %collective-permute-done.16.refs_0_.refs_6_ = bf16[2,8,128,128]{3,2,1,0:T(8,128)(2,1)S(1)} collective-permute-done((bf16[2,8,128,128]{3,2,1,0:T(8,128)(2,1)S(1)}, bf16[2,8,128,128]{3,2,1,0:T(8,128)(2,1)S(1)}, u32[]{:S(2)}, u32[]{:S(2)}) %collective-permute-start.16) | collective-permute-done | bytes 524320 | tf_op jit(solution)/shard_map/ppermute | solution.py:29
  124.1 4.4 %grads.5 = (bf16[64,8192]{1,0:T(8,128)(2,1)}, bf16[64,8192]{1,0:T(8,128)(2,1)}, bf16[64,8192]{1,0:T(8,128)(2,1)}, bf16[3,64,1024]{2,1,0:T(8,128)(2,1)S(1)}, f32[8,128]{1,0:T(8,128)S(1)}) custom-call(s32[2]{0:T(128)S(1)} %get-tuple-element.148.refs_0_, ...), custom_call_target="tpu_custom_call", output_to_operand_aliasing={{0}: (7, {}), {1}: (8, {}), {2}: (9, {})} | custom-call | flops 4000000000 | bytes 1 | tf_op jit(solution)/shard_map/grads/pallas_call | solution.py:67
  128.5 1.7 %collective-permute-start.17 = (bf16[3,64,1024]{2,1,0:T(8,128)(2,1)S(1)}, bf16[3,64,1024]{2,1,0:T(8,128)(2,1)S(1)}, u32[]{:S(2)}, u32[]{:S(2)}) collective-permute-start(bf16[3,64,1024]{2,1,0:T(8,128)(2,1)S(1)} %get-tuple-element.113), channel_id=1, source_target_pairs={{0,1},{1,0},{2,3},{3,2},{4,5},{5,4},{6,7},{7,6},{8,9},{9,8},{10,11... | collective-permute-start | bytes 1179656 | tf_op jit(solution)/shard_map/ppermute | solution.py:29
  131.6 4.4 %grads.6 = (bf16[64,8192]{1,0:T(8,128)(2,1)}, bf16[64,8192]{1,0:T(8,128)(2,1)}, bf16[64,8192]{1,0:T(8,128)(2,1)}, bf16[3,64,1024]{2,1,0:T(8,128)(2,1)S(1)}, f32[8,128]{1,0:T(8,128)S(1)}) custom-call(s32[2]{0:T(128)S(1)} %get-tuple-element.141.refs_0_, ...), custom_call_target="tpu_custom_call", output_to_operand_aliasing={{0}: (7, {}), {1}: (8, {}), {2}: (9, {})} | custom-call | flops 4000000000 | bytes 1 | tf_op jit(solution)/shard_map/grads/pallas_call | solution.py:67
  136.3 12.3 %collective-permute-done.18.refs_6_ = bf16[2,8,128,128]{3,2,1,0:T(8,128)(2,1)S(1)} collective-permute-done((bf16[2,8,128,128]{3,2,1,0:T(8,128)(2,1)S(1)}, bf16[2,8,128,128]{3,2,1,0:T(8,128)(2,1)S(1)}, u32[]{:S(2)}, u32[]{:S(2)}) %collective-permute-start.18) | collective-permute-done | bytes 524320 | tf_op jit(solution)/shard_map/ppermute | solution.py:29
  148.6 4.4 %grads.7 = (bf16[64,8192]{1,0:T(8,128)(2,1)}, bf16[64,8192]{1,0:T(8,128)(2,1)}, bf16[64,8192]{1,0:T(8,128)(2,1)}, bf16[3,64,1024]{2,1,0:T(8,128)(2,1)S(1)}, f32[8,128]{1,0:T(8,128)S(1)}) custom-call(s32[2]{0:T(128)S(1)} %get-tuple-element.148.refs_0_, ...), custom_call_target="tpu_custom_call", output_to_operand_aliasing={{0}: (7, {}), {1}: (8, {}), {2}: (9, {})} | custom-call | flops 4000000000 | bytes 1 | tf_op jit(solution)/shard_map/grads/pallas_call | solution.py:67
  153.1 7.0 %collective-permute-done.21.refs_1_ = bf16[3,64,1024]{2,1,0:T(8,128)(2,1)S(1)} collective-permute-done((bf16[3,64,1024]{2,1,0:T(8,128)(2,1)S(1)}, bf16[3,64,1024]{2,1,0:T(8,128)(2,1)S(1)}, u32[]{:S(2)}, u32[]{:S(2)}) %collective-permute-start.21) | collective-permute-done | bytes 393248 | tf_op jit(solution)/shard_map/ppermute | solution.py:29
  161.4 6.0 %collective-permute-done.20.refs_2_ = bf16[3,64,1024]{2,1,0:T(8,128)(2,1)S(1)} collective-permute-done((bf16[3,64,1024]{2,1,0:T(8,128)(2,1)S(1)}, bf16[3,64,1024]{2,1,0:T(8,128)(2,1)S(1)}, u32[]{:S(2)}, u32[]{:S(2)}) %collective-permute-start.20) | collective-permute-done | bytes 393248 | tf_op jit(solution)/shard_map/ppermute | solution.py:29
  167.3 1.5 place.5
  (86 shorter events, 20.9 us)
Async XLA Ops:
  0.6 8.1 %copy-start = (bf16[64,8192]{1,0:T(8,128)(2,1)S(1)}, bf16[64,8192]{1,0:T(8,128)(2,1)}, u32[]{:S(2)}) copy-start(bf16[64,8192]{1,0:T(8,128)(2,1)} %refs_1_.9) | copy-start | bytes 3145732
  0.6 8.0 %copy-start.1 = (bf16[64,8192]{1,0:T(8,128)(2,1)S(1)}, bf16[64,8192]{1,0:T(8,128)(2,1)}, u32[]{:S(2)}) copy-start(bf16[64,8192]{1,0:T(8,128)(2,1)} %refs_2_.7) | copy-start | bytes 3145732
  0.7 8.0 %copy-start.2 = (bf16[64,8192]{1,0:T(8,128)(2,1)S(1)}, bf16[64,8192]{1,0:T(8,128)(2,1)}, u32[]{:S(2)}) copy-start(bf16[64,8192]{1,0:T(8,128)(2,1)} %refs_3_.7) | copy-start | bytes 3145732
  0.7 5.4 %copy-start.12 = (f32[16,256]{1,0:T(8,128)S(1)}, f32[16,256]{1,0:T(8,128)}, u32[]{:S(2)}) copy-start(f32[16,256]{1,0:T(8,128)} %refs_1_.7) | copy-start | bytes 49156
  2.9 27.7 %collective-permute-start.1 = (bf16[2,4,64,1024]{3,2,1,0:T(8,128)(2,1)}, bf16[2,4,64,1024]{3,2,1,0:T(8,128)(2,1)}, u32[]{:S(2)}, u32[]{:S(2)}) collective-permute-start(bf16[2,4,64,1024]{3,2,1,0:T(8,128)(2,1)} %get-tuple-element.72), channel_id=1, source_target_pairs={{0,1},{1,0},{2,3},{3,2},{4,5},{5,4},{6,7},{7,6},{8,9},{9,8},{10,11... | collective-permute-start | bytes 3145736 | tf_op jit(solution)/shard_map/ppermute | solution.py:29
  6.0 24.7 %collective-permute-start = (f32[16,256]{1,0:T(8,128)S(1)}, f32[16,256]{1,0:T(8,128)S(1)}, u32[]{:S(2)}, u32[]{:S(2)}) collective-permute-start(f32[16,256]{1,0:T(8,128)S(1)} %copy-done.12), channel_id=1, source_target_pairs={{0,2},{1,3},{2,0},{3,1},{4,6},{5,7},{6,4},{7,5},{8,10},{9,11},{10,... | collective-permute-start | bytes 49160 | tf_op jit(solution)/shard_map/ppermute | solution.py:29
  12.3 51.2 %collective-permute-start.2 = (bf16[2,4,64,1024]{3,2,1,0:T(8,128)(2,1)}, bf16[2,4,64,1024]{3,2,1,0:T(8,128)(2,1)}, u32[]{:S(2)}, u32[]{:S(2)}) collective-permute-start(bf16[2,4,64,1024]{3,2,1,0:T(8,128)(2,1)} %get-tuple-element.81), channel_id=1, source_target_pairs={{0,1},{1,0},{2,3},{3,2},{4,5},{5,4},{6,7},{7,6},{8,9},{9,8},{10,11... | collective-permute-start | bytes 3145736 | tf_op jit(solution)/shard_map/ppermute | solution.py:29
  13.1 1.2 collective-permute-start.3
  14.3 3.6 %collective-permute-start.4 = (f32[2,16]{1,0:T(2,128)S(1)}, f32[2,16]{1,0:T(2,128)S(1)}, u32[]{:S(2)}, u32[]{:S(2)}) collective-permute-start(f32[2,16]{1,0:T(2,128)S(1)} %maximum_select_fusion.2), channel_id=1, source_target_pairs={{0,8},{4,12},{8,0},{12,4},{16,24},{20,28},{24,16},{28,20},{1,9},{5... | collective-permute-start | bytes 392 | tf_op jit(solution)/shard_map/ppermute | solution.py:29
  16.0 16.0 %copy-start.4 = (bf16[64,8192]{1,0:T(8,128)(2,1)S(1)}, bf16[64,8192]{1,0:T(8,128)(2,1)}, u32[]{:S(2)}) copy-start(bf16[64,8192]{1,0:T(8,128)(2,1)} %refs_4_.5) | copy-start | bytes 3145732
  17.9 22.5 %collective-permute-start.5 = (f32[4,16]{1,0:T(4,128)S(1)}, f32[4,16]{1,0:T(4,128)S(1)}, u32[]{:S(2)}, u32[]{:S(2)}) collective-permute-start(f32[4,16]{1,0:T(4,128)S(1)} %maximum_select_fusion.1), channel_id=1, source_target_pairs={{0,16},{4,20},{8,24},{12,28},{16,0},{20,4},{24,8},{28,12},{1,17},{... | collective-permute-start | bytes 776 | tf_op jit(solution)/shard_map/ppermute | solution.py:29
  32.8 3.9 %copy-start.10 = (bf16[2,4,64,1024]{3,2,1,0:T(8,128)(2,1)}, bf16[2,4,64,1024]{3,2,1,0:T(8,128)(2,1)S(1)}, u32[]{:S(2)}) copy-start(bf16[2,4,64,1024]{3,2,1,0:T(8,128)(2,1)S(1)} %get-tuple-element.76.refs_0_.refs_1_) | copy-start | bytes 3145732
  37.6 28.9 %collective-permute-start.7 = (bf16[2,8,128,128]{3,2,1,0:T(8,128)(2,1)}, bf16[2,8,128,128]{3,2,1,0:T(8,128)(2,1)}, u32[]{:S(2)}, u32[]{:S(2)}) collective-permute-start(bf16[2,8,128,128]{3,2,1,0:T(8,128)(2,1)} %get-tuple-element.88), channel_id=1, source_target_pairs={{0,2},{1,3},{2,0},{3,1},{4,6},{5,7},{6,4},{7,5},{8,10},{9,11},{10,... | collective-permute-start | bytes 1572872 | tf_op jit(solution)/shard_map/ppermute | solution.py:29
  40.8 1.2 copy-start.5
  42.0 21.6 %copy-start.9 = (f32[4,2,128,12]{3,2,1,0:T(8,128)S(1)}, f32[4,2,128,12]{3,2,1,0:T(8,128)}, u32[]{:S(2)}) copy-start(f32[4,2,128,12]{3,2,1,0:T(8,128)} %copy-done.8) | copy-start | bytes 147460
  63.5 3.0 %copy-start.7 = (f32[2,8,128,128]{3,2,1,0:T(8,128)S(1)}, f32[2,8,128,128]{3,2,1,0:T(8,128)}, u32[]{:S(2)}) copy-start(f32[2,8,128,128]{3,2,1,0:T(8,128)} %copy-done.6) | copy-start | bytes 3145732
  68.5 2.0 %collective-permute-start.8 = (bf16[2,8,128,128]{3,2,1,0:T(8,128)(2,1)S(1)}, bf16[2,8,128,128]{3,2,1,0:T(8,128)(2,1)S(1)}, u32[]{:S(2)}, u32[]{:S(2)}) collective-permute-start(bf16[2,8,128,128]{3,2,1,0:T(8,128)(2,1)S(1)} %get-tuple-element.91), channel_id=1, source_target_pairs={{0,4},{4,0},{8,12},{12,8},{16,20},{20,16},{24,28},{28,24},{1,5},{5... | collective-permute-start | bytes 1572872 | tf_op jit(solution)/shard_map/ppermute | solution.py:29
  68.6 26.5 %collective-permute-start.6 = (bf16[2,8,128,128]{3,2,1,0:T(8,128)(2,1)S(1)}, bf16[2,8,128,128]{3,2,1,0:T(8,128)(2,1)S(1)}, u32[]{:S(2)}, u32[]{:S(2)}) collective-permute-start(bf16[2,8,128,128]{3,2,1,0:T(8,128)(2,1)S(1)} %get-tuple-element.86), channel_id=1, source_target_pairs={{0,2},{1,3},{2,0},{3,1},{4,6},{5,7},{6,4},{7,5},{8,10},{9,11},{10,... | collective-permute-start | bytes 1572872 | tf_op jit(solution)/shard_map/ppermute | solution.py:29
  71.5 14.1 %collective-permute-start.10 = (bf16[8,128,128]{2,1,0:T(8,128)(2,1)S(1)}, bf16[8,128,128]{2,1,0:T(8,128)(2,1)S(1)}, u32[]{:S(2)}, u32[]{:S(2)}) collective-permute-start(bf16[8,128,128]{2,1,0:T(8,128)(2,1)S(1)} %get-tuple-element.94), channel_id=1, source_target_pairs={{0,16},{4,20},{8,24},{12,28},{16,0},{20,4},{24,8},{28,12},{1,17},{... | collective-permute-start | bytes 786440 | tf_op jit(solution)/shard_map/ppermute | solution.py:29
  73.2 12.3 %collective-permute-start.11 = (bf16[8,128,128]{2,1,0:T(8,128)(2,1)S(1)}, bf16[8,128,128]{2,1,0:T(8,128)(2,1)S(1)}, u32[]{:S(2)}, u32[]{:S(2)}) collective-permute-start(bf16[8,128,128]{2,1,0:T(8,128)(2,1)S(1)} %get-tuple-element.94), channel_id=1, source_target_pairs={{0,24},{4,28},{8,16},{12,20},{16,8},{20,12},{24,0},{28,4},{1,25},{... | collective-permute-start | bytes 786440 | tf_op jit(solution)/shard_map/ppermute | solution.py:29
  74.7 12.1 %collective-permute-start.9 = (bf16[8,128,128]{2,1,0:T(8,128)(2,1)S(1)}, bf16[8,128,128]{2,1,0:T(8,128)(2,1)S(1)}, u32[]{:S(2)}, u32[]{:S(2)}) collective-permute-start(bf16[8,128,128]{2,1,0:T(8,128)(2,1)S(1)} %get-tuple-element.93), channel_id=1, source_target_pairs={{0,8},{4,12},{8,0},{12,4},{16,24},{20,28},{24,16},{28,20},{1,9},{5... | collective-permute-start | bytes 786440 | tf_op jit(solution)/shard_map/ppermute | solution.py:29
  96.0 6.6 %copy-start.11 = (bf16[2,4,64,1024]{3,2,1,0:T(8,128)(2,1)S(1)}, bf16[2,4,64,1024]{3,2,1,0:T(8,128)(2,1)}, u32[]{:S(2)}) copy-start(bf16[2,4,64,1024]{3,2,1,0:T(8,128)(2,1)} %copy-done.10) | copy-start | bytes 3145732
  96.0 2.0 %collective-permute-start.12 = (bf16[2,8,128,128]{3,2,1,0:T(8,128)(2,1)S(1)}, bf16[2,8,128,128]{3,2,1,0:T(8,128)(2,1)S(1)}, u32[]{:S(2)}, u32[]{:S(2)}) collective-permute-start(bf16[2,8,128,128]{3,2,1,0:T(8,128)(2,1)S(1)} %get-tuple-element.99), channel_id=1, source_target_pairs={{0,4},{4,0},{8,12},{12,8},{16,20},{20,16},{24,28},{28,24},{1,5},{5... | collective-permute-start | bytes 1572872 | tf_op jit(solution)/shard_map/ppermute | solution.py:29
  96.0 26.6 %collective-permute-start.16 = (bf16[2,8,128,128]{3,2,1,0:T(8,128)(2,1)S(1)}, bf16[2,8,128,128]{3,2,1,0:T(8,128)(2,1)S(1)}, u32[]{:S(2)}, u32[]{:S(2)}) collective-permute-start(bf16[2,8,128,128]{3,2,1,0:T(8,128)(2,1)S(1)} %get-tuple-element.104), channel_id=1, source_target_pairs={{0,2},{1,3},{2,0},{3,1},{4,6},{5,7},{6,4},{7,5},{8,10},{9,11},{10,... | collective-permute-start | bytes 1572872 | tf_op jit(solution)/shard_map/ppermute | solution.py:29
  98.9 23.7 %collective-permute-start.14 = (bf16[8,128,128]{2,1,0:T(8,128)(2,1)S(1)}, bf16[8,128,128]{2,1,0:T(8,128)(2,1)S(1)}, u32[]{:S(2)}, u32[]{:S(2)}) collective-permute-start(bf16[8,128,128]{2,1,0:T(8,128)(2,1)S(1)} %get-tuple-element.102), channel_id=1, source_target_pairs={{0,16},{4,20},{8,24},{12,28},{16,0},{20,4},{24,8},{28,12},{1,17},{... | collective-permute-start | bytes 786440 | tf_op jit(solution)/shard_map/ppermute | solution.py:29
  100.7 21.9 %collective-permute-start.15 = (bf16[8,128,128]{2,1,0:T(8,128)(2,1)S(1)}, bf16[8,128,128]{2,1,0:T(8,128)(2,1)S(1)}, u32[]{:S(2)}, u32[]{:S(2)}) collective-permute-start(bf16[8,128,128]{2,1,0:T(8,128)(2,1)S(1)} %get-tuple-element.102), channel_id=1, source_target_pairs={{0,24},{4,28},{8,16},{12,20},{16,8},{20,12},{24,0},{28,4},{1,25},{... | collective-permute-start | bytes 786440 | tf_op jit(solution)/shard_map/ppermute | solution.py:29
  102.1 20.5 %collective-permute-start.13 = (bf16[8,128,128]{2,1,0:T(8,128)(2,1)S(1)}, bf16[8,128,128]{2,1,0:T(8,128)(2,1)S(1)}, u32[]{:S(2)}, u32[]{:S(2)}) collective-permute-start(bf16[8,128,128]{2,1,0:T(8,128)(2,1)S(1)} %get-tuple-element.101), channel_id=1, source_target_pairs={{0,8},{4,12},{8,0},{12,4},{16,24},{20,28},{24,16},{28,20},{1,9},{5... | collective-permute-start | bytes 786440 | tf_op jit(solution)/shard_map/ppermute | solution.py:29
  106.9 23.3 %collective-permute-start.19 = (bf16[3,64,1024]{2,1,0:T(8,128)(2,1)S(1)}, bf16[3,64,1024]{2,1,0:T(8,128)(2,1)S(1)}, u32[]{:S(2)}, u32[]{:S(2)}) collective-permute-start(bf16[3,64,1024]{2,1,0:T(8,128)(2,1)S(1)} %get-tuple-element.115), channel_id=1, source_target_pairs={{0,1},{1,0},{2,3},{3,2},{4,5},{5,4},{6,7},{7,6},{8,9},{9,8},{10,11... | collective-permute-start | bytes 1179656 | tf_op jit(solution)/shard_map/ppermute | solution.py:29
  124.0 24.7 %collective-permute-start.18 = (bf16[2,8,128,128]{3,2,1,0:T(8,128)(2,1)S(1)}, bf16[2,8,128,128]{3,2,1,0:T(8,128)(2,1)S(1)}, u32[]{:S(2)}, u32[]{:S(2)}) collective-permute-start(bf16[2,8,128,128]{3,2,1,0:T(8,128)(2,1)S(1)} %get-tuple-element.114), channel_id=1, source_target_pairs={{0,2},{1,3},{2,0},{3,1},{4,6},{5,7},{6,4},{7,5},{8,10},{9,11},{10,... | collective-permute-start | bytes 1572872 | tf_op jit(solution)/shard_map/ppermute | solution.py:29
  128.5 32.9 %collective-permute-start.17 = (bf16[3,64,1024]{2,1,0:T(8,128)(2,1)S(1)}, bf16[3,64,1024]{2,1,0:T(8,128)(2,1)S(1)}, u32[]{:S(2)}, u32[]{:S(2)}) collective-permute-start(bf16[3,64,1024]{2,1,0:T(8,128)(2,1)S(1)} %get-tuple-element.113), channel_id=1, source_target_pairs={{0,1},{1,0},{2,3},{3,2},{4,5},{5,4},{6,7},{7,6},{8,9},{9,8},{10,11... | collective-permute-start | bytes 1179656 | tf_op jit(solution)/shard_map/ppermute | solution.py:29
  136.0 24.0 %collective-permute-start.21 = (bf16[3,64,1024]{2,1,0:T(8,128)(2,1)S(1)}, bf16[3,64,1024]{2,1,0:T(8,128)(2,1)S(1)}, u32[]{:S(2)}, u32[]{:S(2)}) collective-permute-start(bf16[3,64,1024]{2,1,0:T(8,128)(2,1)S(1)} %get-tuple-element.129), channel_id=1, source_target_pairs={{0,1},{1,0},{2,3},{3,2},{4,5},{5,4},{6,7},{7,6},{8,9},{9,8},{10,11... | collective-permute-start | bytes 1179656 | tf_op jit(solution)/shard_map/ppermute | solution.py:29
  153.1 14.3 %collective-permute-start.20 = (bf16[3,64,1024]{2,1,0:T(8,128)(2,1)S(1)}, bf16[3,64,1024]{2,1,0:T(8,128)(2,1)S(1)}, u32[]{:S(2)}, u32[]{:S(2)}) collective-permute-start(bf16[3,64,1024]{2,1,0:T(8,128)(2,1)S(1)} %get-tuple-element.128), channel_id=1, source_target_pairs={{0,1},{1,0},{2,3},{3,2},{4,5},{5,4},{6,7},{7,6},{8,9},{9,8},{10,11... | collective-permute-start | bytes 1179656 | tf_op jit(solution)/shard_map/ppermute | solution.py:29
  (4 other events, 3.7 us)

commit v6 on v5

--- a/solution.py
+++ b/solution.py
@@ -578,10 +578,10 @@
         else:
             self.total = result[0]
             sends = [result[1]]
-        self.got = []
-        for p in range(1, 1 << level["nb"]):
+        self.got = [None] * ((1 << level["nb"]) - 1)
+        for p in reversed(range(1, 1 << level["nb"])):
             send = sends[p.bit_length() - 1] if level["last"] else sends[0]
-            self.got.append(swap(send, "seq", p << level["base"]))
+            self.got[p - 1] = swap(send, "seq", p << level["base"])
 
     def advance(self):
         e = self.env

time: 169 us -> 169 us (level)
  no operation moved by 1% of the time
where the time goes in v6:
time: 169 us
  waiting for transfers between devices  92.7 us (55%)
  Pallas kernels  44.2 us (26%)
  starting transfers between devices  25.1 us (15%)
  local copies, waits for them, and re-layouts  5.15 us (3%)
    ppermute x22, waiting for transfers between devices, swap(): lax.ppermute(x, axis, [(i, i ^ bit) for i in range(lax.axis_size(axis))])  92.7 us
    pallas_call x22, Pallas kernels, call(): pl.pallas_call(body, grid_spec=pltpu.PrefetchScalarGridSpec(num_scalar_pr...  44.2 us
    ppermute x22, starting transfers between devices, swap(): lax.ppermute(x, axis, [(i, i ^ bit) for i in range(lax.axis_size(axis))])  25.1 us
    unnamed x28, local copies, waits for them, and re-layouts  4.07 us
  transfers between devices with their start and end apart: 22, of which 12 were waited for; matrix products, arithmetic and copies ran while one was open for 1% of the time, Pallas kernels for 22%

profile of v6, /device:TPU:0, one launch (start us, length us, event | category | flops | bytes accessed | tf_op | source)
XLA Modules:
  0.0 168.8 jit_solution(10321849086658675942)
XLA Ops:
  0.7 2.2 %pack.4 = (bf16[2,4,64,1024]{3,2,1,0:T(8,128)(2,1)}, f32[8,128]{1,0:T(8,128)}) custom-call(bf16[64,8192]{1,0:T(8,128)(2,1)} %refs_1_.9, bf16[64,8192]{1,0:T(8,128)(2,1)} %refs_2_.7, bf16[64,8192]{1,0:T(8,128)(2,1)} %refs_3_.7, bf16[64,8192]{1,0:T(8,128)(2,1)} %refs_4_.5), custom_call_target="tpu_custom_call" | custom-call | flops 1 | bytes 1 | tf_op jit(solution)/shard_map/pack/pallas_call | solution.py:67
  2.9 3.1 %collective-permute-start.1 = (bf16[2,4,64,1024]{3,2,1,0:T(8,128)(2,1)}, bf16[2,4,64,1024]{3,2,1,0:T(8,128)(2,1)}, u32[]{:S(2)}, u32[]{:S(2)}) collective-permute-start(bf16[2,4,64,1024]{3,2,1,0:T(8,128)(2,1)} %get-tuple-element.72), channel_id=1, source_target_pairs={{0,1},{1,0},{2,3},{3,2},{4,5},{5,4},{6,7},{7,6},{8,9},{9,8},{10,11... | collective-permute-start | bytes 3145736 | tf_op jit(solution)/shard_map/ppermute | solution.py:29
  6.0 2.6 %collective-permute-start = (f32[16,256]{1,0:T(8,128)S(1)}, f32[16,256]{1,0:T(8,128)S(1)}, u32[]{:S(2)}, u32[]{:S(2)}) collective-permute-start(f32[16,256]{1,0:T(8,128)S(1)} %copy-done.12), channel_id=1, source_target_pairs={{0,2},{1,3},{2,0},{3,1},{4,6},{5,7},{6,4},{7,5},{8,10},{9,11},{10,... | collective-permute-start | bytes 49160 | tf_op jit(solution)/shard_map/ppermute | solution.py:29
  10.5 1.8 %pack.5 = (bf16[2,4,64,1024]{3,2,1,0:T(8,128)(2,1)}, f32[8,128]{1,0:T(8,128)S(1)}) custom-call(s32[2]{0:T(128)S(1)} %get-tuple-element.143.refs_0_, bf16[64,8192]{1,0:T(8,128)(2,1)S(1)} %copy-done, bf16[64,8192]{1,0:T(8,128)(2,1)S(1)} %copy-done.1, bf16[64,8192]{1,0:T(8,128)(2,1)S(1)} %copy-done.2, bf16[64,8192]{1,0:T(8,128)(2,1)S(1)} %copy-done.3, ...), custom_call_target="tpu_custom_call" | custom-call | flops 1 | bytes 1 | tf_op jit(solution)/shard_map/pack/pallas_call | solution.py:67
  14.3 1.6 collective-permute-start.4
  16.0 1.9 %collective-permute-done.4 = f32[2,16]{1,0:T(2,128)S(1)} collective-permute-done((f32[2,16]{1,0:T(2,128)S(1)}, f32[2,16]{1,0:T(2,128)S(1)}, u32[]{:S(2)}, u32[]{:S(2)}) %collective-permute-start.4) | collective-permute-done | bytes 160 | tf_op jit(solution)/shard_map/ppermute | solution.py:29
  17.9 1.6 collective-permute-start.5
  19.5 11.1 %collective-permute-done.1.refs_0_.refs_1_.refs_2_ = bf16[2,4,64,1024]{3,2,1,0:T(8,128)(2,1)} collective-permute-done((bf16[2,4,64,1024]{3,2,1,0:T(8,128)(2,1)}, bf16[2,4,64,1024]{3,2,1,0:T(8,128)(2,1)}, u32[]{:S(2)}, u32[]{:S(2)}) %collective-permute-start.1) | collective-permute-done | bytes 1048608 | tf_op jit(solution)/shard_map/ppermute | solution.py:29
  32.8 3.9 %states.2 = (f32[2,8,128,128]{3,2,1,0:T(8,128)S(1)}, bf16[2,8,128,128]{3,2,1,0:T(8,128)(2,1)}, f32[8,128]{1,0:T(8,128)S(1)}) custom-call(bf16[2,4,64,1024]{3,2,1,0:T(8,128)(2,1)S(1)} %get-tuple-element.76.refs_0_.refs_1_, bf16[2,4,64,1024]{3,2,1,0:T(8,128)(2,1)} %collective-permute-done.1.refs_0_.refs_1_.refs_2_, ...), custom_call_target="tpu_custom_call" | custom-call | flops 1 | bytes 1 | tf_op jit(solution)/shard_map/states/pallas_call | solution.py:67
  37.6 2.8 %collective-permute-start.7 = (bf16[2,8,128,128]{3,2,1,0:T(8,128)(2,1)}, bf16[2,8,128,128]{3,2,1,0:T(8,128)(2,1)}, u32[]{:S(2)}, u32[]{:S(2)}) collective-permute-start(bf16[2,8,128,128]{3,2,1,0:T(8,128)(2,1)} %get-tuple-element.88), channel_id=1, source_target_pairs={{0,2},{1,3},{2,0},{3,1},{4,6},{5,7},{6,4},{7,5},{8,10},{9,11},{10,... | collective-permute-start | bytes 1572872 | tf_op jit(solution)/shard_map/ppermute | solution.py:29
  42.8 20.7 %collective-permute-done.2.refs_1_.refs_2_ = bf16[2,4,64,1024]{3,2,1,0:T(8,128)(2,1)} collective-permute-done((bf16[2,4,64,1024]{3,2,1,0:T(8,128)(2,1)}, bf16[2,4,64,1024]{3,2,1,0:T(8,128)(2,1)}, u32[]{:S(2)}, u32[]{:S(2)}) %collective-permute-start.2) | collective-permute-done | bytes 1048608 | tf_op jit(solution)/shard_map/ppermute | solution.py:29
  63.5 3.0 %states.3 = (f32[2,8,128,128]{3,2,1,0:T(8,128)S(1)}, bf16[2,8,128,128]{3,2,1,0:T(8,128)(2,1)S(1)}, f32[8,128]{1,0:T(8,128)S(1)}) custom-call(bf16[2,4,64,1024]{3,2,1,0:T(8,128)(2,1)S(1)} %get-tuple-element.80.refs_0_.refs_1_, bf16[2,4,64,1024]{3,2,1,0:T(8,128)(2,1)} %collective-permute-done.2.refs_1_.refs_2_, f32[4,2,128,12]{3,2,1,0:T(8,128)S(1)} %copy-done.9, ...), custom_call_target="tpu_custom_call" | custom-call | flops 1 | bytes 1 | tf_op jit(solution)/shard_map/states/pallas_call | solution.py:67
  66.5 1.9 %step.6 = (f32[2,8,128,128]{3,2,1,0:T(8,128)S(1)}, bf16[2,8,128,128]{3,2,1,0:T(8,128)(2,1)S(1)}, f32[8,128]{1,0:T(8,128)S(1)}) custom-call(f32[23,16]{1,0:T(8,128)S(1)} %exponential_select_fusion.refs_0_, s32[2]{0:T(128)S(1)} %pad_add_fusion.1.refs_1_, f32[2,8,128,128]{3,2,1,0:T(8,128)S(1)} %copy-done.7, ...), custom_call_target="tpu_custom_call" | custom-call | flops 1 | bytes 1 | tf_op jit(solution)/shard_map/step/pallas_call | solution.py:67
  68.6 1.9 %collective-permute-start.6 = (bf16[2,8,128,128]{3,2,1,0:T(8,128)(2,1)S(1)}, bf16[2,8,128,128]{3,2,1,0:T(8,128)(2,1)S(1)}, u32[]{:S(2)}, u32[]{:S(2)}) collective-permute-start(bf16[2,8,128,128]{3,2,1,0:T(8,128)(2,1)S(1)} %get-tuple-element.86), channel_id=1, source_target_pairs={{0,2},{1,3},{2,0},{3,1},{4,6},{5,7},{6,4},{7,5},{8,10},{9,11},{10,... | collective-permute-start | bytes 1572872 | tf_op jit(solution)/shard_map/ppermute | solution.py:29
  71.5 1.7 %collective-permute-start.10 = (bf16[8,128,128]{2,1,0:T(8,128)(2,1)S(1)}, bf16[8,128,128]{2,1,0:T(8,128)(2,1)S(1)}, u32[]{:S(2)}, u32[]{:S(2)}) collective-permute-start(bf16[8,128,128]{2,1,0:T(8,128)(2,1)S(1)} %get-tuple-element.94), channel_id=1, source_target_pairs={{0,16},{4,20},{8,24},{12,28},{16,0},{20,4},{24,8},{28,12},{1,17},{... | collective-permute-start | bytes 786440 | tf_op jit(solution)/shard_map/ppermute | solution.py:29
  73.2 1.4 collective-permute-start.11
  75.0 10.5 %collective-permute-done.10.refs_3_ = bf16[8,128,128]{2,1,0:T(8,128)(2,1)S(1)} collective-permute-done((bf16[8,128,128]{2,1,0:T(8,128)(2,1)S(1)}, bf16[8,128,128]{2,1,0:T(8,128)(2,1)S(1)}, u32[]{:S(2)}, u32[]{:S(2)}) %collective-permute-start.10) | collective-permute-done | bytes 262176 | tf_op jit(solution)/shard_map/ppermute | solution.py:29
  86.8 2.4 %step.8 = (bf16[2,8,128,128]{3,2,1,0:T(8,128)(2,1)S(1)}, bf16[2,8,128,128]{3,2,1,0:T(8,128)(2,1)S(1)}, f32[8,128]{1,0:T(8,128)S(1)}) custom-call(f32[23,16]{1,0:T(8,128)S(1)} %exponential_select_fusion.refs_0_, s32[2]{0:T(128)S(1)} %pad_add_fusion.1.refs_1_, bf16[8,128,128]{2,1,0:T(8,128)(2,1)S(1)} %collective-permute-done.9.refs_2_, ...), custom_call_target="tpu_custom_call" | custom-call | flops 1 | bytes 1 | tf_op jit(solution)/shard_map/step/pallas_call | solution.py:67
  89.2 5.9 %collective-permute-done.6.refs_3_.refs_6_ = bf16[2,8,128,128]{3,2,1,0:T(8,128)(2,1)S(1)} collective-permute-done((bf16[2,8,128,128]{3,2,1,0:T(8,128)(2,1)S(1)}, bf16[2,8,128,128]{3,2,1,0:T(8,128)(2,1)S(1)}, u32[]{:S(2)}, u32[]{:S(2)}) %collective-permute-start.6) | collective-permute-done | bytes 524320 | tf_op jit(solution)/shard_map/ppermute | solution.py:29
  96.1 1.8 %collective-permute-done.12.refs_3_ = bf16[2,8,128,128]{3,2,1,0:T(8,128)(2,1)S(1)} collective-permute-done((bf16[2,8,128,128]{3,2,1,0:T(8,128)(2,1)S(1)}, bf16[2,8,128,128]{3,2,1,0:T(8,128)(2,1)S(1)}, u32[]{:S(2)}, u32[]{:S(2)}) %collective-permute-start.12) | collective-permute-done | bytes 524320 | tf_op jit(solution)/shard_map/ppermute | solution.py:29
  98.9 1.8 %collective-permute-start.14 = (bf16[8,128,128]{2,1,0:T(8,128)(2,1)S(1)}, bf16[8,128,128]{2,1,0:T(8,128)(2,1)S(1)}, u32[]{:S(2)}, u32[]{:S(2)}) collective-permute-start(bf16[8,128,128]{2,1,0:T(8,128)(2,1)S(1)} %get-tuple-element.102), channel_id=1, source_target_pairs={{0,16},{4,20},{8,24},{12,28},{16,0},{20,4},{24,8},{28,12},{1,17},{... | collective-permute-start | bytes 786440 | tf_op jit(solution)/shard_map/ppermute | solution.py:29
  102.5 4.4 %grads.4 = (bf16[64,8192]{1,0:T(8,128)(2,1)}, bf16[64,8192]{1,0:T(8,128)(2,1)}, bf16[64,8192]{1,0:T(8,128)(2,1)}, bf16[3,64,1024]{2,1,0:T(8,128)(2,1)S(1)}, f32[8,128]{1,0:T(8,128)S(1)}) custom-call(s32[2]{0:T(128)S(1)} %get-tuple-element.141.refs_0_, bf16[2,4,64,1024]{3,2,1,0:T(8,128)(2,1)S(1)} %copy-done.11, ...), custom_call_target="tpu_custom_call" | custom-call | flops 4000000000 | bytes 1 | tf_op jit(solution)/shard_map/grads/pallas_call | solution.py:67
  106.9 1.5 collective-permute-start.19
  109.0 13.6 %collective-permute-done.16.refs_0_.refs_6_ = bf16[2,8,128,128]{3,2,1,0:T(8,128)(2,1)S(1)} collective-permute-done((bf16[2,8,128,128]{3,2,1,0:T(8,128)(2,1)S(1)}, bf16[2,8,128,128]{3,2,1,0:T(8,128)(2,1)S(1)}, u32[]{:S(2)}, u32[]{:S(2)}) %collective-permute-start.16) | collective-permute-done | bytes 524320 | tf_op jit(solution)/shard_map/ppermute | solution.py:29
  124.1 4.4 %grads.5 = (bf16[64,8192]{1,0:T(8,128)(2,1)}, bf16[64,8192]{1,0:T(8,128)(2,1)}, bf16[64,8192]{1,0:T(8,128)(2,1)}, bf16[3,64,1024]{2,1,0:T(8,128)(2,1)S(1)}, f32[8,128]{1,0:T(8,128)S(1)}) custom-call(s32[2]{0:T(128)S(1)} %get-tuple-element.148.refs_0_, ...), custom_call_target="tpu_custom_call", output_to_operand_aliasing={{0}: (7, {}), {1}: (8, {}), {2}: (9, {})} | custom-call | flops 4000000000 | bytes 1 | tf_op jit(solution)/shard_map/grads/pallas_call | solution.py:67
  128.5 1.7 %collective-permute-start.17 = (bf16[3,64,1024]{2,1,0:T(8,128)(2,1)S(1)}, bf16[3,64,1024]{2,1,0:T(8,128)(2,1)S(1)}, u32[]{:S(2)}, u32[]{:S(2)}) collective-permute-start(bf16[3,64,1024]{2,1,0:T(8,128)(2,1)S(1)} %get-tuple-element.113), channel_id=1, source_target_pairs={{0,1},{1,0},{2,3},{3,2},{4,5},{5,4},{6,7},{7,6},{8,9},{9,8},{10,11... | collective-permute-start | bytes 1179656 | tf_op jit(solution)/shard_map/ppermute | solution.py:29
  131.6 4.4 %grads.6 = (bf16[64,8192]{1,0:T(8,128)(2,1)}, bf16[64,8192]{1,0:T(8,128)(2,1)}, bf16[64,8192]{1,0:T(8,128)(2,1)}, bf16[3,64,1024]{2,1,0:T(8,128)(2,1)S(1)}, f32[8,128]{1,0:T(8,128)S(1)}) custom-call(s32[2]{0:T(128)S(1)} %get-tuple-element.141.refs_0_, ...), custom_call_target="tpu_custom_call", output_to_operand_aliasing={{0}: (7, {}), {1}: (8, {}), {2}: (9, {})} | custom-call | flops 4000000000 | bytes 1 | tf_op jit(solution)/shard_map/grads/pallas_call | solution.py:67
  136.3 12.3 %collective-permute-done.18.refs_6_ = bf16[2,8,128,128]{3,2,1,0:T(8,128)(2,1)S(1)} collective-permute-done((bf16[2,8,128,128]{3,2,1,0:T(8,128)(2,1)S(1)}, bf16[2,8,128,128]{3,2,1,0:T(8,128)(2,1)S(1)}, u32[]{:S(2)}, u32[]{:S(2)}) %collective-permute-start.18) | collective-permute-done | bytes 524320 | tf_op jit(solution)/shard_map/ppermute | solution.py:29
  148.6 4.4 %grads.7 = (bf16[64,8192]{1,0:T(8,128)(2,1)}, bf16[64,8192]{1,0:T(8,128)(2,1)}, bf16[64,8192]{1,0:T(8,128)(2,1)}, bf16[3,64,1024]{2,1,0:T(8,128)(2,1)S(1)}, f32[8,128]{1,0:T(8,128)S(1)}) custom-call(s32[2]{0:T(128)S(1)} %get-tuple-element.148.refs_0_, ...), custom_call_target="tpu_custom_call", output_to_operand_aliasing={{0}: (7, {}), {1}: (8, {}), {2}: (9, {})} | custom-call | flops 4000000000 | bytes 1 | tf_op jit(solution)/shard_map/grads/pallas_call | solution.py:67
  153.1 7.0 %collective-permute-done.21.refs_1_ = bf16[3,64,1024]{2,1,0:T(8,128)(2,1)S(1)} collective-permute-done((bf16[3,64,1024]{2,1,0:T(8,128)(2,1)S(1)}, bf16[3,64,1024]{2,1,0:T(8,128)(2,1)S(1)}, u32[]{:S(2)}, u32[]{:S(2)}) %collective-permute-start.21) | collective-permute-done | bytes 393248 | tf_op jit(solution)/shard_map/ppermute | solution.py:29
  161.4 6.0 %collective-permute-done.20.refs_2_ = bf16[3,64,1024]{2,1,0:T(8,128)(2,1)S(1)} collective-permute-done((bf16[3,64,1024]{2,1,0:T(8,128)(2,1)S(1)}, bf16[3,64,1024]{2,1,0:T(8,128)(2,1)S(1)}, u32[]{:S(2)}, u32[]{:S(2)}) %collective-permute-start.20) | collective-permute-done | bytes 393248 | tf_op jit(solution)/shard_map/ppermute | solution.py:29
  167.3 1.5 place.5
  (86 shorter events, 20.9 us)
Async XLA Ops:
  0.6 8.1 %copy-start = (bf16[64,8192]{1,0:T(8,128)(2,1)S(1)}, bf16[64,8192]{1,0:T(8,128)(2,1)}, u32[]{:S(2)}) copy-start(bf16[64,8192]{1,0:T(8,128)(2,1)} %refs_1_.9) | copy-start | bytes 3145732
  0.6 8.0 %copy-start.1 = (bf16[64,8192]{1,0:T(8,128)(2,1)S(1)}, bf16[64,8192]{1,0:T(8,128)(2,1)}, u32[]{:S(2)}) copy-start(bf16[64,8192]{1,0:T(8,128)(2,1)} %refs_2_.7) | copy-start | bytes 3145732
  0.7 8.0 %copy-start.2 = (bf16[64,8192]{1,0:T(8,128)(2,1)S(1)}, bf16[64,8192]{1,0:T(8,128)(2,1)}, u32[]{:S(2)}) copy-start(bf16[64,8192]{1,0:T(8,128)(2,1)} %refs_3_.7) | copy-start | bytes 3145732
  0.7 5.4 %copy-start.12 = (f32[16,256]{1,0:T(8,128)S(1)}, f32[16,256]{1,0:T(8,128)}, u32[]{:S(2)}) copy-start(f32[16,256]{1,0:T(8,128)} %refs_1_.7) | copy-start | bytes 49156
  2.9 27.7 %collective-permute-start.1 = (bf16[2,4,64,1024]{3,2,1,0:T(8,128)(2,1)}, bf16[2,4,64,1024]{3,2,1,0:T(8,128)(2,1)}, u32[]{:S(2)}, u32[]{:S(2)}) collective-permute-start(bf16[2,4,64,1024]{3,2,1,0:T(8,128)(2,1)} %get-tuple-element.72), channel_id=1, source_target_pairs={{0,1},{1,0},{2,3},{3,2},{4,5},{5,4},{6,7},{7,6},{8,9},{9,8},{10,11... | collective-permute-start | bytes 3145736 | tf_op jit(solution)/shard_map/ppermute | solution.py:29
  6.0 24.7 %collective-permute-start = (f32[16,256]{1,0:T(8,128)S(1)}, f32[16,256]{1,0:T(8,128)S(1)}, u32[]{:S(2)}, u32[]{:S(2)}) collective-permute-start(f32[16,256]{1,0:T(8,128)S(1)} %copy-done.12), channel_id=1, source_target_pairs={{0,2},{1,3},{2,0},{3,1},{4,6},{5,7},{6,4},{7,5},{8,10},{9,11},{10,... | collective-permute-start | bytes 49160 | tf_op jit(solution)/shard_map/ppermute | solution.py:29
  12.3 51.2 %collective-permute-start.2 = (bf16[2,4,64,1024]{3,2,1,0:T(8,128)(2,1)}, bf16[2,4,64,1024]{3,2,1,0:T(8,128)(2,1)}, u32[]{:S(2)}, u32[]{:S(2)}) collective-permute-start(bf16[2,4,64,1024]{3,2,1,0:T(8,128)(2,1)} %get-tuple-element.81), channel_id=1, source_target_pairs={{0,1},{1,0},{2,3},{3,2},{4,5},{5,4},{6,7},{7,6},{8,9},{9,8},{10,11... | collective-permute-start | bytes 3145736 | tf_op jit(solution)/shard_map/ppermute | solution.py:29
  13.1 1.2 collective-permute-start.3
  14.3 3.6 %collective-permute-start.4 = (f32[2,16]{1,0:T(2,128)S(1)}, f32[2,16]{1,0:T(2,128)S(1)}, u32[]{:S(2)}, u32[]{:S(2)}) collective-permute-start(f32[2,16]{1,0:T(2,128)S(1)} %maximum_select_fusion.2), channel_id=1, source_target_pairs={{0,8},{4,12},{8,0},{12,4},{16,24},{20,28},{24,16},{28,20},{1,9},{5... | collective-permute-start | bytes 392 | tf_op jit(solution)/shard_map/ppermute | solution.py:29
  16.0 16.0 %copy-start.4 = (bf16[64,8192]{1,0:T(8,128)(2,1)S(1)}, bf16[64,8192]{1,0:T(8,128)(2,1)}, u32[]{:S(2)}) copy-start(bf16[64,8192]{1,0:T(8,128)(2,1)} %refs_4_.5) | copy-start | bytes 3145732
  17.9 22.5 %collective-permute-start.5 = (f32[4,16]{1,0:T(4,128)S(1)}, f32[4,16]{1,0:T(4,128)S(1)}, u32[]{:S(2)}, u32[]{:S(2)}) collective-permute-start(f32[4,16]{1,0:T(4,128)S(1)} %maximum_select_fusion.1), channel_id=1, source_target_pairs={{0,16},{4,20},{8,24},{12,28},{16,0},{20,4},{24,8},{28,12},{1,17},{... | collective-permute-start | bytes 776 | tf_op jit(solution)/shard_map/ppermute | solution.py:29
  32.8 3.9 %copy-start.10 = (bf16[2,4,64,1024]{3,2,1,0:T(8,128)(2,1)}, bf16[2,4,64,1024]{3,2,1,0:T(8,128)(2,1)S(1)}, u32[]{:S(2)}) copy-start(bf16[2,4,64,1024]{3,2,1,0:T(8,128)(2,1)S(1)} %get-tuple-element.76.refs_0_.refs_1_) | copy-start | bytes 3145732
  37.6 28.9 %collective-permute-start.7 = (bf16[2,8,128,128]{3,2,1,0:T(8,128)(2,1)}, bf16[2,8,128,128]{3,2,1,0:T(8,128)(2,1)}, u32[]{:S(2)}, u32[]{:S(2)}) collective-permute-start(bf16[2,8,128,128]{3,2,1,0:T(8,128)(2,1)} %get-tuple-element.88), channel_id=1, source_target_pairs={{0,2},{1,3},{2,0},{3,1},{4,6},{5,7},{6,4},{7,5},{8,10},{9,11},{10,... | collective-permute-start | bytes 1572872 | tf_op jit(solution)/shard_map/ppermute | solution.py:29
  40.8 1.2 copy-start.5
  42.0 21.6 %copy-start.9 = (f32[4,2,128,12]{3,2,1,0:T(8,128)S(1)}, f32[4,2,128,12]{3,2,1,0:T(8,128)}, u32[]{:S(2)}) copy-start(f32[4,2,128,12]{3,2,1,0:T(8,128)} %copy-done.8) | copy-start | bytes 147460
  63.5 3.0 %copy-start.7 = (f32[2,8,128,128]{3,2,1,0:T(8,128)S(1)}, f32[2,8,128,128]{3,2,1,0:T(8,128)}, u32[]{:S(2)}) copy-start(f32[2,8,128,128]{3,2,1,0:T(8,128)} %copy-done.6) | copy-start | bytes 3145732
  68.5 2.0 %collective-permute-start.8 = (bf16[2,8,128,128]{3,2,1,0:T(8,128)(2,1)S(1)}, bf16[2,8,128,128]{3,2,1,0:T(8,128)(2,1)S(1)}, u32[]{:S(2)}, u32[]{:S(2)}) collective-permute-start(bf16[2,8,128,128]{3,2,1,0:T(8,128)(2,1)S(1)} %get-tuple-element.91), channel_id=1, source_target_pairs={{0,4},{4,0},{8,12},{12,8},{16,20},{20,16},{24,28},{28,24},{1,5},{5... | collective-permute-start | bytes 1572872 | tf_op jit(solution)/shard_map/ppermute | solution.py:29
  68.6 26.5 %collective-permute-start.6 = (bf16[2,8,128,128]{3,2,1,0:T(8,128)(2,1)S(1)}, bf16[2,8,128,128]{3,2,1,0:T(8,128)(2,1)S(1)}, u32[]{:S(2)}, u32[]{:S(2)}) collective-permute-start(bf16[2,8,128,128]{3,2,1,0:T(8,128)(2,1)S(1)} %get-tuple-element.86), channel_id=1, source_target_pairs={{0,2},{1,3},{2,0},{3,1},{4,6},{5,7},{6,4},{7,5},{8,10},{9,11},{10,... | collective-permute-start | bytes 1572872 | tf_op jit(solution)/shard_map/ppermute | solution.py:29
  71.5 14.1 %collective-permute-start.10 = (bf16[8,128,128]{2,1,0:T(8,128)(2,1)S(1)}, bf16[8,128,128]{2,1,0:T(8,128)(2,1)S(1)}, u32[]{:S(2)}, u32[]{:S(2)}) collective-permute-start(bf16[8,128,128]{2,1,0:T(8,128)(2,1)S(1)} %get-tuple-element.94), channel_id=1, source_target_pairs={{0,16},{4,20},{8,24},{12,28},{16,0},{20,4},{24,8},{28,12},{1,17},{... | collective-permute-start | bytes 786440 | tf_op jit(solution)/shard_map/ppermute | solution.py:29
  73.2 12.3 %collective-permute-start.11 = (bf16[8,128,128]{2,1,0:T(8,128)(2,1)S(1)}, bf16[8,128,128]{2,1,0:T(8,128)(2,1)S(1)}, u32[]{:S(2)}, u32[]{:S(2)}) collective-permute-start(bf16[8,128,128]{2,1,0:T(8,128)(2,1)S(1)} %get-tuple-element.94), channel_id=1, source_target_pairs={{0,24},{4,28},{8,16},{12,20},{16,8},{20,12},{24,0},{28,4},{1,25},{... | collective-permute-start | bytes 786440 | tf_op jit(solution)/shard_map/ppermute | solution.py:29
  74.7 12.1 %collective-permute-start.9 = (bf16[8,128,128]{2,1,0:T(8,128)(2,1)S(1)}, bf16[8,128,128]{2,1,0:T(8,128)(2,1)S(1)}, u32[]{:S(2)}, u32[]{:S(2)}) collective-permute-start(bf16[8,128,128]{2,1,0:T(8,128)(2,1)S(1)} %get-tuple-element.93), channel_id=1, source_target_pairs={{0,8},{4,12},{8,0},{12,4},{16,24},{20,28},{24,16},{28,20},{1,9},{5... | collective-permute-start | bytes 786440 | tf_op jit(solution)/shard_map/ppermute | solution.py:29
  96.0 6.6 %copy-start.11 = (bf16[2,4,64,1024]{3,2,1,0:T(8,128)(2,1)S(1)}, bf16[2,4,64,1024]{3,2,1,0:T(8,128)(2,1)}, u32[]{:S(2)}) copy-start(bf16[2,4,64,1024]{3,2,1,0:T(8,128)(2,1)} %copy-done.10) | copy-start | bytes 3145732
  96.0 2.0 %collective-permute-start.12 = (bf16[2,8,128,128]{3,2,1,0:T(8,128)(2,1)S(1)}, bf16[2,8,128,128]{3,2,1,0:T(8,128)(2,1)S(1)}, u32[]{:S(2)}, u32[]{:S(2)}) collective-permute-start(bf16[2,8,128,128]{3,2,1,0:T(8,128)(2,1)S(1)} %get-tuple-element.99), channel_id=1, source_target_pairs={{0,4},{4,0},{8,12},{12,8},{16,20},{20,16},{24,28},{28,24},{1,5},{5... | collective-permute-start | bytes 1572872 | tf_op jit(solution)/shard_map/ppermute | solution.py:29
  96.0 26.6 %collective-permute-start.16 = (bf16[2,8,128,128]{3,2,1,0:T(8,128)(2,1)S(1)}, bf16[2,8,128,128]{3,2,1,0:T(8,128)(2,1)S(1)}, u32[]{:S(2)}, u32[]{:S(2)}) collective-permute-start(bf16[2,8,128,128]{3,2,1,0:T(8,128)(2,1)S(1)} %get-tuple-element.104), channel_id=1, source_target_pairs={{0,2},{1,3},{2,0},{3,1},{4,6},{5,7},{6,4},{7,5},{8,10},{9,11},{10,... | collective-permute-start | bytes 1572872 | tf_op jit(solution)/shard_map/ppermute | solution.py:29
  98.9 23.7 %collective-permute-start.14 = (bf16[8,128,128]{2,1,0:T(8,128)(2,1)S(1)}, bf16[8,128,128]{2,1,0:T(8,128)(2,1)S(1)}, u32[]{:S(2)}, u32[]{:S(2)}) collective-permute-start(bf16[8,128,128]{2,1,0:T(8,128)(2,1)S(1)} %get-tuple-element.102), channel_id=1, source_target_pairs={{0,16},{4,20},{8,24},{12,28},{16,0},{20,4},{24,8},{28,12},{1,17},{... | collective-permute-start | bytes 786440 | tf_op jit(solution)/shard_map/ppermute | solution.py:29
  100.7 21.9 %collective-permute-start.15 = (bf16[8,128,128]{2,1,0:T(8,128)(2,1)S(1)}, bf16[8,128,128]{2,1,0:T(8,128)(2,1)S(1)}, u32[]{:S(2)}, u32[]{:S(2)}) collective-permute-start(bf16[8,128,128]{2,1,0:T(8,128)(2,1)S(1)} %get-tuple-element.102), channel_id=1, source_target_pairs={{0,24},{4,28},{8,16},{12,20},{16,8},{20,12},{24,0},{28,4},{1,25},{... | collective-permute-start | bytes 786440 | tf_op jit(solution)/shard_map/ppermute | solution.py:29
  102.1 20.5 %collective-permute-start.13 = (bf16[8,128,128]{2,1,0:T(8,128)(2,1)S(1)}, bf16[8,128,128]{2,1,0:T(8,128)(2,1)S(1)}, u32[]{:S(2)}, u32[]{:S(2)}) collective-permute-start(bf16[8,128,128]{2,1,0:T(8,128)(2,1)S(1)} %get-tuple-element.101), channel_id=1, source_target_pairs={{0,8},{4,12},{8,0},{12,4},{16,24},{20,28},{24,16},{28,20},{1,9},{5... | collective-permute-start | bytes 786440 | tf_op jit(solution)/shard_map/ppermute | solution.py:29
  106.9 23.3 %collective-permute-start.19 = (bf16[3,64,1024]{2,1,0:T(8,128)(2,1)S(1)}, bf16[3,64,1024]{2,1,0:T(8,128)(2,1)S(1)}, u32[]{:S(2)}, u32[]{:S(2)}) collective-permute-start(bf16[3,64,1024]{2,1,0:T(8,128)(2,1)S(1)} %get-tuple-element.115), channel_id=1, source_target_pairs={{0,1},{1,0},{2,3},{3,2},{4,5},{5,4},{6,7},{7,6},{8,9},{9,8},{10,11... | collective-permute-start | bytes 1179656 | tf_op jit(solution)/shard_map/ppermute | solution.py:29
  124.0 24.7 %collective-permute-start.18 = (bf16[2,8,128,128]{3,2,1,0:T(8,128)(2,1)S(1)}, bf16[2,8,128,128]{3,2,1,0:T(8,128)(2,1)S(1)}, u32[]{:S(2)}, u32[]{:S(2)}) collective-permute-start(bf16[2,8,128,128]{3,2,1,0:T(8,128)(2,1)S(1)} %get-tuple-element.114), channel_id=1, source_target_pairs={{0,2},{1,3},{2,0},{3,1},{4,6},{5,7},{6,4},{7,5},{8,10},{9,11},{10,... | collective-permute-start | bytes 1572872 | tf_op jit(solution)/shard_map/ppermute | solution.py:29
  128.5 32.9 %collective-permute-start.17 = (bf16[3,64,1024]{2,1,0:T(8,128)(2,1)S(1)}, bf16[3,64,1024]{2,1,0:T(8,128)(2,1)S(1)}, u32[]{:S(2)}, u32[]{:S(2)}) collective-permute-start(bf16[3,64,1024]{2,1,0:T(8,128)(2,1)S(1)} %get-tuple-element.113), channel_id=1, source_target_pairs={{0,1},{1,0},{2,3},{3,2},{4,5},{5,4},{6,7},{7,6},{8,9},{9,8},{10,11... | collective-permute-start | bytes 1179656 | tf_op jit(solution)/shard_map/ppermute | solution.py:29
  136.0 24.0 %collective-permute-start.21 = (bf16[3,64,1024]{2,1,0:T(8,128)(2,1)S(1)}, bf16[3,64,1024]{2,1,0:T(8,128)(2,1)S(1)}, u32[]{:S(2)}, u32[]{:S(2)}) collective-permute-start(bf16[3,64,1024]{2,1,0:T(8,128)(2,1)S(1)} %get-tuple-element.129), channel_id=1, source_target_pairs={{0,1},{1,0},{2,3},{3,2},{4,5},{5,4},{6,7},{7,6},{8,9},{9,8},{10,11... | collective-permute-start | bytes 1179656 | tf_op jit(solution)/shard_map/ppermute | solution.py:29
  153.1 14.3 %collective-permute-start.20 = (bf16[3,64,1024]{2,1,0:T(8,128)(2,1)S(1)}, bf16[3,64,1024]{2,1,0:T(8,128)(2,1)S(1)}, u32[]{:S(2)}, u32[]{:S(2)}) collective-permute-start(bf16[3,64,1024]{2,1,0:T(8,128)(2,1)S(1)} %get-tuple-element.128), channel_id=1, source_target_pairs={{0,1},{1,0},{2,3},{3,2},{4,5},{5,4},{6,7},{7,6},{8,9},{9,8},{10,11... | collective-permute-start | bytes 1179656 | tf_op jit(solution)/shard_map/ppermute | solution.py:29
  (4 other events, 3.7 us)
